TPU v7x, 128 devices: a whole 4x4x4 slice. The times are simulated.
128 devices in a mesh: inp: 8 (over z, core), out: 8 (over y_lo, x), dep: 2 (over y_hi).
Axes of the slice: x: 4, y: 4 (y_hi: 2, y_lo: 2; y = y_hi * 2 + y_lo), z: 4, core: 2. Of those that a mesh axis runs over, the one named last changes fastest.
Arguments:
- tokens_in: bfloat16 [1024, 8192], P(('out', 'dep'), 'inp'), may hold values from -6 to 6
- grad_out: bfloat16 [1024, 8192], P(('out', 'dep'), 'inp'), may hold values from -0.59765625 to 0.59765625
- w_gate: bfloat16 [8192, 14336], P('inp', ('out', 'dep')), may hold values from -0.0625 to 0.0625
- w_up: bfloat16 [8192, 14336], P('inp', ('out', 'dep')), may hold values from -0.0625 to 0.0625
- w_down: bfloat16 [14336, 8192], P(('out', 'dep'), 'inp'), may hold values from -0.046875 to 0.046875
Outputs:
- grad_tokens: bfloat16 [1024, 8192], P(('out', 'dep'), 'inp')
- grad_w_gate: bfloat16 [8192, 14336], P('inp', ('out', 'dep'))
- grad_w_up: bfloat16 [8192, 14336], P('inp', ('out', 'dep'))
- grad_w_down: bfloat16 [14336, 8192], P(('out', 'dep'), 'inp')
All inputs are finite; a program needn't handle non-finite values.
Results may differ from a plain program's by a relative error of at most 0.034.
Values may be sent and summed in bfloat16 or wider, within the bound.
No kernel may reach another device: no remote copies, remote signals or barrier semaphores. Data moves between devices by JAX's collectives and lax.ppermute only.
A program may use at most 128 MiB of HBM per device.

v0:
```python
import jax
import jax.numpy as jnp
from jax import lax
from jax.sharding import PartitionSpec as P


def activate(sums):
    gate = sums[0]
    up = sums[1]
    grad_hidden = sums[2]
    sig = jax.nn.sigmoid(gate)
    silu = gate * sig
    hidden = silu * up
    grad_gate = grad_hidden * up * sig * (1.0 + gate * (1.0 - sig))
    grad_up = grad_hidden * silu
    return jnp.stack([hidden, grad_gate, grad_up]).astype(jnp.bfloat16)


def hidden_terms(x_rows, dy_rows, paired, down_cols):
    both = jnp.einsum("td,kdf->ktf", x_rows, paired, preferred_element_type=jnp.float32)
    back = jnp.einsum("te,fe->tf", dy_rows, down_cols, preferred_element_type=jnp.float32)
    partials = jnp.concatenate([both, back[None]], axis=0)
    sums = lax.psum(partials.astype(jnp.bfloat16), "inp").astype(jnp.float32)
    trio = activate(sums)
    return trio


def local_grads(x_rows, dy_rows, paired, trio):
    weight_terms = jnp.einsum("td,ktf->kdf", x_rows, trio[1:3], preferred_element_type=jnp.float32)
    down_terms = jnp.einsum("tf,te->fe", trio[0], dy_rows, preferred_element_type=jnp.float32)
    input_terms = jnp.einsum("ktf,kdf->td", trio[1:3], paired, preferred_element_type=jnp.float32)
    return (weight_terms, down_terms, input_terms)


def local(tokens_in, grad_out, w_gate, w_up, w_down):
    paired = jnp.stack([w_gate, w_up])
    x_rows, dy_rows = (
        lax.all_gather(tokens_in, ("out", "dep"), axis=0, tiled=True),
        lax.all_gather(grad_out, ("out", "dep"), axis=0, tiled=True),
    )
    trio = hidden_terms(x_rows, dy_rows, paired, w_down)
    weight_sums, down_sums, input_terms = local_grads(x_rows, dy_rows, paired, trio)
    input_sums = lax.psum_scatter(input_terms, ("out", "dep"), scatter_dimension=0, tiled=True)
    grad_tokens = input_sums.astype(jnp.bfloat16)
    grad_w_gate = weight_sums[0].astype(jnp.bfloat16)
    grad_w_up = weight_sums[1].astype(jnp.bfloat16)
    grad_w_down = down_sums.astype(jnp.bfloat16)
    return (grad_tokens, grad_w_gate, grad_w_up, grad_w_down)


def solution(mesh):
    return jax.shard_map(
        local,
        mesh=mesh,
        in_specs=(
            P(("out", "dep"), "inp"),
            P(("out", "dep"), "inp"),
            P("inp", ("out", "dep")),
            P("inp", ("out", "dep")),
            P(("out", "dep"), "inp"),
        ),
        out_specs=(
            P(("out", "dep"), "inp"),
            P("inp", ("out", "dep")),
            P("inp", ("out", "dep")),
            P(("out", "dep"), "inp"),
        ),
        check_vma=False,
    )
```

profile of v0, /device:TPU:1, one launch (start us, length us, event | category | flops | bytes accessed | tf_op | source)
XLA Modules:
  0.0 381.2 jit_solution(14848182482577318259)
XLA Ops:
  7.2 0.7 all-gather.5.cloned.1.call-update
  8.0 0.7 all-gather.3.cloned.1.call-update
  8.7 3.8 copy.9
  12.5 3.8 copy.10
  16.3 65.1 %all-gather.5.cloned.1.call-done = bf16[1024,1024]{1,0:T(8,128)(2,1)} async-done(((bf16[64,1024]{1,0:T(8,128)(2,1)}), bf16[1024,1024]{1,0:T(8,128)(2,1)}) %all-gather.5.cloned.1.call-update) | async-done | bytes 2097168 | tf_op jit(solution)/shard_map/all_gather | solution.py:39
  81.4 4.9 %convert_bitcast_fusion.2 = bf16[1,1024,896]{1,2,0:T(8,128)(2,1)} fusion(bf16[1024,1024]{1,0:T(8,128)(2,1)} %all-gather.5.cloned.1.call-done, bf16[896,1024]{1,0:T(8,128)(2,1)S(1)} %copy-done), kind=kOutput, calls=%fused_computation.18 | convolution fusion | flops 1879965696 | bytes 5767168 | tf_op jit(solution)/shard_map/te,fe->tf/dot_general | solution.py:21
  86.3 75.7 %all-gather.3.cloned.1.call-done = bf16[1024,1024]{1,0:T(8,128)(2,1)} async-done(((bf16[64,1024]{1,0:T(8,128)(2,1)}), bf16[1024,1024]{1,0:T(8,128)(2,1)}) %all-gather.3.cloned.1.call-update) | async-done | bytes 2097168 | tf_op jit(solution)/shard_map/all_gather | solution.py:38
  162.0 6.8 %convert_bitcast_fusion.1 = bf16[2,1024,896]{1,2,0:T(8,128)(2,1)S(1)} fusion(bf16[1,1024,896]{1,2,0:T(8,128)(2,1)} %bitcast.29, bf16[1,1024,896]{1,2,0:T(8,128)(2,1)} %bitcast.27, bf16[1024,1024]{1,0:T(8,128)(2,1)} %all-gather.3.cloned.1.call-done), kind=kOutput, calls=%fused_computation.9 | convolution fusion | flops 3761766400 | bytes 9437184 | tf_op jit(solution)/shard_map/td,kdf->ktf/dot_general | solution.py:20
  168.9 2.9 pad_maximum_fusion
  171.8 0.2 reduce-scatter.2.cloned.1.call-start
  172.0 88.6 %all-reduce.2.cloned.1.call-done = bf16[3,1024,896]{1,2,0:T(8,128)(2,1)} async-done(((bf16[3,1024,896]{1,2,0:T(8,128)(2,1)}), bf16[3,1024,896]{1,2,0:T(8,128)(2,1)}) %all-reduce.2.cloned.1.call-update) | async-done | bytes 5505040 | tf_op jit(solution)/shard_map/psum | solution.py:23
  260.6 3.9 %convert_element_type.19 = f32[3,1024,896]{1,2,0:T(8,128)S(1)} convert(bf16[3,1024,896]{1,2,0:T(8,128)(2,1)} %all-reduce.2.cloned.1.call-done) | non-fusion elementwise | flops 2752512 | bytes 16515072 | tf_op jit(solution)/shard_map/convert_element_type | solution.py:23
  264.5 2.3 multiply_convert_fusion.2
  266.8 2.6 copy-done.1
  269.5 1.2 copy-done.2
  270.7 0.6 copy-done.3
  271.3 5.5 %fusion.2 = f32[1024,1024]{1,0:T(8,128)} fusion(bf16[1,1024,896]{1,2,0:T(8,128)(2,1)S(1)} %bitcast.30, bf16[1,1024,896]{1,2,0:T(8,128)(2,1)S(1)} %bitcast.28, bf16[1,1024,896]{1,2,0:T(8,128)(2,1)S(1)} %get-tuple-element.9, bf16[1,1024,896]{1,2,0:T(8,128)(2,1)S(1)} %get-tuple-element.8), kind=kOutput, calls=%fused_computation.11 | convolution fusion | flops 3761766400 | bytes 11534336 | tf_op jit(solution)/shard_map/ktf,kdf->td/dot_general | solution.py:31
  276.8 6.7 %convert_bitcast_fusion = bf16[2,1024,896]{1,2,0:T(8,128)(2,1)S(1)} fusion(bf16[1,1024,896]{1,2,0:T(8,128)(2,1)} %copy-done.3, bf16[1,1024,896]{1,2,0:T(8,128)(2,1)} %copy-done.2, bf16[1024,1024]{1,0:T(8,128)(2,1)} %all-gather.3.cloned.1.call-done), kind=kOutput, calls=%fused_computation.3 | convolution fusion | flops 3761766400 | bytes 9437184 | tf_op jit(solution)/shard_map/td,ktf->kdf/dot_general | solution.py:29
  283.5 2.2 slice_bitcast_fusion
  285.8 3.9 %copy.15 = bf16[1024,896]{1,0:T(8,128)(2,1)} copy(bf16[1024,896]{0,1:T(8,128)(2,1)} %get-tuple-element.10) | data formatting | bytes 3670016
  289.6 3.8 copy.14
  293.4 7.1 %fusion.8 = bf16[896,1024]{1,0:T(8,128)(2,1)} fusion(bf16[1024,1024]{1,0:T(8,128)(2,1)} %all-gather.5.cloned.1.call-done, f32[3,1024,896]{1,2,0:T(8,128)} %copy-done.1), kind=kOutput, calls=%fused_computation.19 | convolution fusion | flops 1885470720 | bytes 11272192 | tf_op jit(solution)/shard_map/tf,te->fe/dot_general | solution.py:30
  300.6 72.5 %reduce-scatter.2.cloned.1.call-done = f32[64,1024]{1,0:T(8,128)} async-done(((f32[1024,1024]{1,0:T(8,128)}), f32[64,1024]{1,0:T(8,128)}) %reduce-scatter.2.cloned.1.call-update) | async-done | bytes 262160 | tf_op jit(solution)/shard_map/reduce_scatter | solution.py:43
  373.1 1.6 convert_element_type.20
  (16 shorter events, 0.2 us)
Async XLA Ops:
  7.2 74.2 %copy-start = (bf16[896,1024]{1,0:T(8,128)(2,1)S(1)}, bf16[896,1024]{1,0:T(8,128)(2,1)}, u32[]{:S(2)}) copy-start(bf16[896,1024]{1,0:T(8,128)(2,1)} %param.9) | copy-start | bytes 5505028
  7.2 74.2 %all-gather.5.cloned.1.call-start = ((), (), s32[]{:S(2)}) async-start(), calls=%async_computation.2 | async-start | bytes 2228224 | tf_op jit(solution)/shard_map/all_gather | solution.py:39
  7.9 154.1 %all-gather.3.cloned.1.call-start = ((), (), s32[]{:S(2)}) async-start(), calls=%async_computation.1 | async-start | bytes 2228224 | tf_op jit(solution)/shard_map/all_gather | solution.py:38
  8.7 251.9 %all-reduce.2.cloned.1.call-start = ((), (), s32[]{:S(2)}) async-start(), calls=%async_computation.3 | async-start | bytes 11010048 | tf_op jit(solution)/shard_map/psum | solution.py:23
  162.0 6.8 %copy-start.6 = (bf16[1,1024,896]{1,2,0:T(8,128)(2,1)S(1)}, bf16[1,1024,896]{1,2,0:T(8,128)(2,1)}, u32[]{:S(2)}) copy-start(bf16[1,1024,896]{1,2,0:T(8,128)(2,1)} %convert_bitcast_fusion.2) | copy-start | bytes 5505028
  171.8 201.3 %reduce-scatter.2.cloned.1.call-start = ((), (), s32[]{:S(2)}) async-start(), calls=%async_computation.4 | async-start | bytes 4456448 | tf_op jit(solution)/shard_map/reduce_scatter | solution.py:43
  264.5 5.0 %copy-start.1 = (f32[3,1024,896]{1,2,0:T(8,128)}, f32[3,1024,896]{1,2,0:T(8,128)S(1)}, u32[]{:S(2)}) copy-start(f32[3,1024,896]{1,2,0:T(8,128)S(1)} %convert_element_type.19) | copy-start | bytes 33030148
  264.5 6.8 %copy-start.4 = (bf16[1024,896]{0,1:T(8,128)(2,1)S(1)}, bf16[1024,896]{0,1:T(8,128)(2,1)}, u32[]{:S(2)}) copy-start(bf16[1024,896]{0,1:T(8,128)(2,1)} %copy.9) | copy-start | bytes 5505028
  264.5 6.8 %copy-start.5 = (bf16[1024,896]{0,1:T(8,128)(2,1)S(1)}, bf16[1024,896]{0,1:T(8,128)(2,1)}, u32[]{:S(2)}) copy-start(bf16[1024,896]{0,1:T(8,128)(2,1)} %copy.10) | copy-start | bytes 5505028
  269.4 1.2 copy-start.2
  269.5 1.8 copy-start.3
Sparse Core Ops, SparseCore 0:
  9.7 71.6 all-gather.4
  83.0 78.9 all-gather.2
  171.9 88.6 all-reduce.1
  277.0 96.0 reduce-scatter.1
where the time goes:
time: 387 us; the launch traced here: 381 us
  waiting for transfers between devices  303 us (78%)
  matrix products  31.1 us (8%)
  local copies, waits for them, and re-layouts  21.9 us (6%)
  between operations  13.8 us (4%)
  other arithmetic  10.7 us (3%)
    psum x1, waiting for transfers between devices, hidden_terms(): sums = lax.psum(partials.astype(jnp.bfloat16), 'inp').astype(jnp.float32)  88.6 us
    all_gather x1, waiting for transfers between devices, local(): lax.all_gather(tokens_in, ('out', 'dep'), axis=0, tiled=True)  75.7 us
    reduce_scatter x1, waiting for transfers between devices, local(): lax.psum_scatter(input_terms, ('out', 'dep'), scatter_dimension=0, tiled=...  72.5 us
    all_gather x1, waiting for transfers between devices, local(): lax.all_gather(grad_out, ('out', 'dep'), axis=0, tiled=True)  65.1 us
    unnamed x18, local copies, waits for them, and re-layouts  19.7 us
  transfers between devices with their start and end apart: 4, of which 4 were waited for; matrix products, arithmetic and copies ran while one was open for 9% of the time, Pallas kernels for 0%

commit v1 on v0

v1 whole, which is shorter than its diff:
```python
import functools

import jax
import jax.numpy as jnp
from jax import lax
from jax.experimental import pallas as pl
from jax.experimental.pallas import tpu as pltpu
from jax.sharding import PartitionSpec as P

XY = ("out", "dep")
BF = jnp.bfloat16
F32 = jnp.float32
MB = 1024 * 1024
PIECE = 32
OFFSETS = (0, 1, 3, 2)


def xy_index(x, y):
    return ((y % 2) * 4 + x) * 2 + y // 2


def from_xy(value, dx, dy):
    pairs = [
        (xy_index((x + dx) % 4, (y + dy) % 4), xy_index(x, y)) for x in range(4) for y in range(4)
    ]
    return lax.ppermute(value, XY, pairs)


def from_z(value, dz, dc=0):
    pairs = [
        (((z + dz) % 4) * 2 + (c + dc) % 2, z * 2 + c) for z in range(4) for c in range(2)
    ]
    return lax.ppermute(value, "inp", pairs)


def params(mb):
    return pltpu.CompilerParams(vmem_limit_bytes=mb * MB)


def vmem(n):
    return [pl.BlockSpec(memory_space=pltpu.VMEM)] * n


def place_of(i, per, z, c):
    slot = i // per
    away = lax.rem(slot // 2 - z + 4, 4)
    away = jnp.where(away == 3, 2, jnp.where(away == 2, 3, away))
    other = jnp.where(slot % 2 == c, 0, 1)
    return (other * 4 + away) * per + i % per


def forward_kernel(counts, where, *refs):
    n = len(counts)
    pieces, (wg, wu, wd) = refs[:n], refs[n:n + 3]
    xs, dys, keep, send = refs[n + 3:]
    total = sum(counts)
    per = total // 8
    z, c = where[0], where[1]
    i = 0
    for ref, count in zip(pieces, counts):
        for j in range(count):
            row = pl.multiple_of(place_of(i, per, z, c) * PIECE, PIECE)
            xs[pl.ds(row, PIECE), :] = ref[j, 0]
            dys[pl.ds(row, PIECE), :] = ref[j, 1]
            i += 1
    t = per * PIECE
    rows = 256
    for half, out in ((1, send), (0, keep)):
        half_rows = 4 * t
        step = min(rows, half_rows)
        for r in range(half_rows // step):
            at = half * half_rows + r * step
            a = xs[pl.ds(at, step), :]
            b = dys[pl.ds(at, step), :]
            gate = jnp.dot(a, wg[...], preferred_element_type=F32).astype(BF)
            up = jnp.dot(a, wu[...], preferred_element_type=F32).astype(BF)
            back = lax.dot_general(b, wd[...], (((1,), (1,)), ((), ())), preferred_element_type=F32).astype(BF)
            blocks = step // t
            for k in range(blocks):
                for m, v in enumerate((gate, up, back)):
                    out[r * blocks + k, m] = v[k * t:(k + 1) * t]


def forward(where, pieces, wg, wu, wd):
    counts = tuple(p.shape[0] for p in pieces)
    per = sum(counts) // 8
    t = per * PIECE
    f = wg.shape[1]
    d = wg.shape[0]
    block = jax.ShapeDtypeStruct((4, 3, t, f), BF)
    rows = jax.ShapeDtypeStruct((8 * t, d), BF)
    return pl.pallas_call(
        functools.partial(forward_kernel, counts),
        out_shape=(rows, rows, block, block),
        in_specs=[pl.BlockSpec(memory_space=pltpu.SMEM)] + vmem(len(pieces) + 3),
        out_specs=vmem(4),
        compiler_params=params(48),
        cost_estimate=pl.CostEstimate(flops=6 * 8 * t * d * f, bytes_accessed=6 * d * f + 16 * t * d * 4, transcendentals=0),
        name="forward",
    )(where, *pieces, wg, wu, wd)


def add_cores_kernel(keep, got, b0, b1, b2, h0, h1):
    t = b0.shape[1]

    def add(k):
        return keep[k].astype(F32) + got[k].astype(F32)

    b0[...] = add(0)
    b1[...] = add(1).astype(BF)
    b2[...] = add(2).astype(BF)
    far = add(3).astype(BF)
    h0[...] = far[:, : t // 2]
    h1[...] = far[:, t // 2:]


def add_cores(keep, got):
    _, _, t, f = keep.shape
    whole = jax.ShapeDtypeStruct((3, t, f), BF)
    half = jax.ShapeDtypeStruct((3, t // 2, f), BF)
    return pl.pallas_call(
        add_cores_kernel,
        out_shape=(jax.ShapeDtypeStruct((3, t, f), F32), whole, whole, half, half),
        in_specs=vmem(2),
        out_specs=vmem(5),
        compiler_params=params(32),
        name="add_cores",
    )(keep, got)


def add_far_kernel(b1, b2, r0, r1, o1, o2):
    t = b1.shape[1]
    o1[:, : t // 2] = (b1[:, : t // 2].astype(F32) + r0[...].astype(F32)).astype(BF)
    o1[:, t // 2:] = b1[:, t // 2:]
    o2[:, : t // 2] = b2[:, : t // 2]
    o2[:, t // 2:] = (b2[:, t // 2:].astype(F32) + r1[...].astype(F32)).astype(BF)


def add_far(b1, b2, r0, r1):
    whole = jax.ShapeDtypeStruct(b1.shape, BF)
    return pl.pallas_call(
        add_far_kernel,
        out_shape=(whole, whole),
        in_specs=vmem(4),
        out_specs=vmem(2),
        compiler_params=params(32),
        name="add_far",
    )(b1, b2, r0, r1)


def activate_kernel(b0, q1, q2, out):
    sums = [b0[m] + q1[m].astype(F32) + q2[m].astype(F32) for m in range(3)]
    gate, up, back = sums
    sig = 1.0 / (1.0 + jnp.exp(-gate))
    silu = gate * sig
    out[0] = (silu * up).astype(BF)
    out[1] = (back * up * sig * (1.0 + gate * (1.0 - sig))).astype(BF)
    out[2] = (back * silu).astype(BF)


def activate(b0, q1, q2):
    return pl.pallas_call(
        activate_kernel,
        out_shape=jax.ShapeDtypeStruct(b0.shape, BF),
        in_specs=vmem(3),
        out_specs=vmem(1)[0],
        compiler_params=params(32),
        name="activate",
    )(b0, q1, q2)


def backward_kernel(counts, targets, where, mine, theirs, wg, wu, hidden, both, sums, gg, gu, res):
    per = sum(counts) // 8
    _, _, t, f = mine.shape
    for half, ref in ((0, mine), (1, theirs)):
        for k in range(4):
            at = (half * 4 + k) * t
            hidden[at:at + t, :] = ref[k, 0]
            both[at:at + t, :f] = ref[k, 1]
            both[at:at + t, f:] = ref[k, 2]
    rows = 256
    dims = (((1,), (1,)), ((), ()))
    for r in range(8 * t // rows):
        part = slice(r * rows, (r + 1) * rows)
        value = lax.dot_general(both[part, :f], wg[...], dims, preferred_element_type=F32)
        value = value + lax.dot_general(both[part, f:], wu[...], dims, preferred_element_type=F32)
        res[part, :] = value.astype(BF)
    z, c = where[0], where[1]
    x, y = where[2], where[3]
    for i, (dx, dy, lo) in enumerate(targets):
        xx = lax.rem(x + dx, 4)
        yy = lax.rem(y + dy, 4)
        device = (lax.rem(yy, 2) * 4 + xx) * 2 + yy // 2
        row = pl.multiple_of(place_of(i, per, z, c) * PIECE, PIECE)
        sums[device, lo:lo + PIECE, :] = res[pl.ds(row, PIECE), :]


def backward(where, mine, theirs, wg, wu, counts, targets):
    _, _, t, f = mine.shape
    d = wg.shape[0]
    return pl.pallas_call(
        functools.partial(backward_kernel, counts, targets),
        out_shape=(
            jax.ShapeDtypeStruct((8 * t, f), BF),
            jax.ShapeDtypeStruct((8 * t, 2 * f), BF),
            jax.ShapeDtypeStruct((16, 2 * PIECE, d), BF),
        ),
        in_specs=[pl.BlockSpec(memory_space=pltpu.SMEM)] + vmem(4),
        out_specs=vmem(3),
        scratch_shapes=[pltpu.VMEM((8, 128), BF), pltpu.VMEM((8, 128), BF), pltpu.VMEM((8 * t, d), BF)],
        compiler_params=params(48),
        cost_estimate=pl.CostEstimate(flops=4 * 8 * t * d * f, bytes_accessed=4 * d * f + 8 * t * (6 * f + 2 * d), transcendentals=0),
        name="backward",
    )(where, mine, theirs, wg, wu)


def weights_kernel(xs, dys, hidden, both, o_gate, o_up, o_down, turned):
    f = o_gate.shape[1]
    dims = (((0,), (0,)), ((), ()))

    @pl.when(pl.program_id(0) == 0)
    def _():
        turned[...] = hidden[...].T

    value = lax.dot_general(xs[...], both[...], dims, preferred_element_type=F32).astype(BF)
    o_gate[...] = value[:, :f]
    o_up[...] = value[:, f:]
    o_down[...] = jnp.dot(turned[...], dys[...], preferred_element_type=F32).astype(BF)


def weights(xs, dys, hidden, both):
    tokens, d = xs.shape
    f = hidden.shape[1]
    n = 4
    w = d // n
    return pl.pallas_call(
        weights_kernel,
        grid=(n,),
        out_shape=(
            jax.ShapeDtypeStruct((d, f), BF),
            jax.ShapeDtypeStruct((d, f), BF),
            jax.ShapeDtypeStruct((f, d), BF),
        ),
        in_specs=[
            pl.BlockSpec((tokens, w), lambda i: (0, i)),
            pl.BlockSpec((tokens, w), lambda i: (0, i)),
            pl.BlockSpec((tokens, f), lambda i: (0, 0)),
            pl.BlockSpec((tokens, 2 * f), lambda i: (0, 0)),
        ],
        out_specs=[
            pl.BlockSpec((w, f), lambda i: (i, 0)),
            pl.BlockSpec((w, f), lambda i: (i, 0)),
            pl.BlockSpec((f, w), lambda i: (0, i)),
        ],
        scratch_shapes=[pltpu.VMEM((f, tokens), BF)],
        compiler_params=params(48),
        cost_estimate=pl.CostEstimate(flops=6 * tokens * d * f, bytes_accessed=6 * d * f + tokens * (4 * d + 6 * f), transcendentals=0),
        name="weights",
    )(xs, dys, hidden, both)


def gather_plane(first, second):
    def along(value, swap, a, b=0):
        return from_xy(value, *((b, a) if swap else (a, b)))

    lines = []
    for value, swap in ((first, False), (second, True)):
        lines.append([value] + [along(value, swap, o) for o in OFFSETS[1:]])
    lines = [jnp.stack(line) for line in lines]
    near = []
    for line, swap in zip(lines, (False, True)):
        near.append((along(line, not swap, 1), along(line, not swap, -1)))
    far = []
    for (ahead, behind), swap in zip(near, (False, True)):
        far.append((along(ahead[:2], not swap, 1), along(behind[2:], not swap, -1)))
    pieces, targets = [], []

    def put(array, which, step, parts):
        pieces.append(array)
        for j in parts:
            one, two = OFFSETS[j], step % 4
            targets.append((one, two, 0) if which == 0 else (two, one, PIECE))

    for which in range(2):
        put(lines[which], which, 0, range(4))
    for which in range(2):
        put(near[which][0], which, 1, range(4))
        put(near[which][1], which, -1, range(4))
    for which in range(2):
        put(far[which][0], which, 2, (0, 1))
        put(far[which][1], which, 2, (2, 3))
    return pieces, tuple(targets)


def local(tokens_in, grad_out, w_gate, w_up, w_down):
    inp, out, dep = (lax.axis_index(a) for a in ("inp", "out", "dep"))
    where = jnp.stack([inp // 2, inp % 2, out % 4, dep * 2 + out // 4]).astype(jnp.int32)
    own = jnp.stack([tokens_in, grad_out])
    pieces, targets = gather_plane(own[:, :PIECE], own[:, PIECE:])
    counts = tuple(p.shape[0] for p in pieces)

    xs, dys, keep, send = forward(where, pieces, w_gate, w_up, w_down)
    b0, b1, b2, h0, h1 = add_cores(keep, from_z(send, 0, 1))
    t = b0.shape[1]
    b1, b2 = add_far(b1, b2, from_z(h0, -1), from_z(h1, 1))
    trio = activate(b0, from_z(b1, -1), from_z(b2, 1))
    ahead, behind = from_z(trio, 1), from_z(trio, -1)
    far = jnp.concatenate([from_z(behind[:, : t // 2], -1), from_z(ahead[:, t // 2:], 1)], axis=1)
    mine = jnp.stack([trio, ahead, behind, far])
    theirs = from_z(mine, 0, 1)
    hidden, both, sums = backward(where, mine, theirs, w_gate, w_up, counts, targets)
    parts = lax.all_to_all(sums, XY, 0, 0)
    grad_w_gate, grad_w_up, grad_w_down = weights(xs, dys, hidden, both)
    grad_tokens = jnp.sum(parts.astype(F32), axis=0).astype(BF)
    return grad_tokens, grad_w_gate, grad_w_up, grad_w_down


def solution(mesh):
    return jax.shard_map(
        local,
        mesh=mesh,
        in_specs=(P(XY, "inp"), P(XY, "inp"), P("inp", XY), P("inp", XY), P(XY, "inp")),
        out_specs=(P(XY, "inp"), P("inp", XY), P("inp", XY), P(XY, "inp")),
        check_vma=False,
    )
```

time: 387 us -> 179 us (0.46)
  waiting for transfers between devices: 303 us -> 82.6 us
  starting transfers between devices: 0.34 us -> 46.1 us
  Pallas kernels: 0 us -> 31.9 us
  matrix products: 31.1 us -> 0 us
  between operations: 13.8 us -> 0.79 us
  local copies, waits for them, and re-layouts: 21.9 us -> 11 us
  other arithmetic: 10.7 us -> 4.35 us
    all_gather x2 -> x0, waiting for transfers between devices: 141 us -> none  [the longest x1 75.7 us: local(): lax.all_gather(tokens_in, ('out', 'dep'), axis=0, tiled=True)]
    psum x1 -> x0, waiting for transfers between devices: 88.6 us -> none  [hidden_terms(): sums = lax.psum(partials.astype(jnp.bfloat16), 'inp').astype(jnp.float32)]
    reduce_scatter x1 -> x0, waiting for transfers between devices: 72.5 us -> none  [local(): lax.psum_scatter(input_terms, ('out', 'dep'), scatter_dimension=0, tiled=...]
    ppermute x0 -> x24, waiting for transfers between devices: none -> 64.8 us  [the longest x10 51.3 us: from_z(): return lax.ppermute(value, 'inp', pairs)]
    ppermute x0 -> x24, starting transfers between devices: none -> 41.2 us  [the longest x14 21.5 us: from_xy(): return lax.ppermute(value, XY, pairs)]
    pallas_call x0 -> x6, Pallas kernels: none -> 31.9 us  [the longest x1 10.8 us: forward(): pl.pallas_call(functools.partial(forward_kernel, counts), out_shape=(rows...]
    dot_general x5 -> x0, matrix products: 31.1 us -> none  [the longest x1 7.14 us: local_grads(): jnp.einsum('tf,te->fe', trio[0], dy_rows, preferred_element_type=jnp.floa...]
    all_to_all x0 -> x1, waiting for transfers between devices: none -> 17.8 us  [local(): parts = lax.all_to_all(sums, XY, 0, 0)]
  transfers between devices with their start and end apart: 4 -> 25, of which waited for: 4 -> 11; matrix products, arithmetic and copies ran while one was open for 9% -> 2% of each run, Pallas kernels for 0% -> 6%
where the time goes in v1:
time: 179 us; the launch traced here: 177 us
  waiting for transfers between devices  82.6 us (46%)
  starting transfers between devices  46.1 us (26%)
  Pallas kernels  31.9 us (18%)
  local copies, waits for them, and re-layouts  11 us (6%)
  other arithmetic  4.35 us (2%)
    ppermute x10, waiting for transfers between devices, from_z(): return lax.ppermute(value, 'inp', pairs)  51.3 us
    ppermute x14, starting transfers between devices, from_xy(): return lax.ppermute(value, XY, pairs)  21.5 us
    ppermute x10, starting transfers between devices, from_z(): return lax.ppermute(value, 'inp', pairs)  19.6 us
    all_to_all x1, waiting for transfers between devices, local(): parts = lax.all_to_all(sums, XY, 0, 0)  17.8 us
    ppermute x14, waiting for transfers between devices, from_xy(): return lax.ppermute(value, XY, pairs)  13.5 us
    pallas_call x1, Pallas kernels, forward(): pl.pallas_call(functools.partial(forward_kernel, counts), out_shape=(rows...  10.8 us
    pallas_call x1, Pallas kernels, weights(): pl.pallas_call(weights_kernel, grid=(n,), out_shape=(jax.ShapeDtypeStruct...  10.4 us
    pallas_call x1, Pallas kernels, backward(): pl.pallas_call(functools.partial(backward_kernel, counts, targets), out_s...  9.55 us
  transfers between devices with their start and end apart: 25, of which 11 were waited for; matrix products, arithmetic and copies ran while one was open for 2% of the time, Pallas kernels for 6%

profile of v1, /device:TPU:1, one launch (start us, length us, event | category | flops | bytes accessed | tf_op | source)
XLA Modules:
  0.0 176.7 jit_solution(7445335158255634073)
XLA Ops:
  1.6 3.7 %collective-permute-start.2 = (bf16[2,32,1024]{2,1,0:T(8,128)(2,1)S(1)}, bf16[2,32,1024]{2,1,0:T(8,128)(2,1)S(1)}, u32[]{:S(2)}, u32[]{:S(2)}) collective-permute-start(bf16[2,32,1024]{2,1,0:T(8,128)(2,1)S(1)} %get-tuple-element.39), channel_id=1, source_target_pairs={{4,0},{12,8},{5,1},{13,9},{6,2},{14,10},{7,3},{15,11},{0,4},{8,12}... | collective-permute-start | bytes 393224 | tf_op jit(solution)/shard_map/ppermute | solution.py:26
  5.6 2.4 %collective-permute-start = (bf16[2,32,1024]{2,1,0:T(8,128)(2,1)S(1)}, bf16[2,32,1024]{2,1,0:T(8,128)(2,1)S(1)}, u32[]{:S(2)}, u32[]{:S(2)}) collective-permute-start(bf16[2,32,1024]{2,1,0:T(8,128)(2,1)S(1)} %get-tuple-element.39), channel_id=1, source_target_pairs={{2,0},{10,8},{3,1},{11,9},{4,2},{12,10},{5,3},{13,11},{6,4},{14,12... | collective-permute-start | bytes 393224 | tf_op jit(solution)/shard_map/ppermute | solution.py:26
  17.4 2.7 %collective-permute-start.8 = (bf16[4,2,32,1024]{3,2,1,0:T(8,128)(2,1)S(1)}, bf16[4,2,32,1024]{3,2,1,0:T(8,128)(2,1)S(1)}, u32[]{:S(2)}, u32[]{:S(2)}) collective-permute-start(bf16[4,2,32,1024]{3,2,1,0:T(8,128)(2,1)S(1)} %pad_maximum_fusion.2.refs_1_), channel_id=1, source_target_pairs={{2,0},{10,8},{3,1},{11,9},{4,2},{12,10},{5,3},{13,11},{6,4},{14,12... | collective-permute-start | bytes 1572872 | tf_op jit(solution)/shard_map/ppermute | solution.py:26
  20.0 7.9 %collective-permute-done.7.refs_3_ = bf16[4,2,32,1024]{3,2,1,0:T(8,128)(2,1)S(1)} collective-permute-done((bf16[4,2,32,1024]{3,2,1,0:T(8,128)(2,1)S(1)}, bf16[4,2,32,1024]{3,2,1,0:T(8,128)(2,1)S(1)}, u32[]{:S(2)}, u32[]{:S(2)}) %collective-permute-start.7) | collective-permute-done | bytes 524320 | tf_op jit(solution)/shard_map/ppermute | solution.py:26
  29.4 2.7 %collective-permute-start.10 = (bf16[2,2,32,1024]{3,2,1,0:T(8,128)(2,1)}, bf16[2,2,32,1024]{3,2,1,0:T(8,128)(2,1)}, u32[]{:S(2)}, u32[]{:S(2)}) collective-permute-start(bf16[2,2,32,1024]{3,2,1,0:T(8,128)(2,1)} %slice.34), channel_id=1, source_target_pairs={{8,0},{1,8},{9,1},{0,9},{10,2},{3,10},{11,3},{2,11},{12,4},{5,12},... | collective-permute-start | bytes 786440 | tf_op jit(solution)/shard_map/ppermute | solution.py:26
  33.5 2.7 %collective-permute-start.12 = (bf16[2,2,32,1024]{3,2,1,0:T(8,128)(2,1)}, bf16[2,2,32,1024]{3,2,1,0:T(8,128)(2,1)}, u32[]{:S(2)}, u32[]{:S(2)}) collective-permute-start(bf16[2,2,32,1024]{3,2,1,0:T(8,128)(2,1)} %slice.36), channel_id=1, source_target_pairs={{2,0},{10,8},{3,1},{11,9},{4,2},{12,10},{5,3},{13,11},{6,4},{14,12... | collective-permute-start | bytes 786440 | tf_op jit(solution)/shard_map/ppermute | solution.py:26
  36.2 3.3 %collective-permute-done.13.refs_9_ = bf16[2,2,32,1024]{3,2,1,0:T(8,128)(2,1)} collective-permute-done((bf16[2,2,32,1024]{3,2,1,0:T(8,128)(2,1)}, bf16[2,2,32,1024]{3,2,1,0:T(8,128)(2,1)}, u32[]{:S(2)}, u32[]{:S(2)}) %collective-permute-start.13) | collective-permute-done | bytes 262176 | tf_op jit(solution)/shard_map/ppermute | solution.py:26
  41.3 10.8 %forward.1 = (bf16[1024,1024]{1,0:T(8,128)(2,1)}, bf16[1024,1024]{1,0:T(8,128)(2,1)}, bf16[4,3,128,896]{3,2,1,0:T(8,128)(2,1)}, bf16[4,3,128,896]{3,2,1,0:T(8,128)(2,1)}) custom-call(s32[4]{0:T(128)S(1)} %pad_add_fusion.where, bf16[4,2,32,1024]{3,2,1,0:T(8,128)(2,1)S(1)} %pad_maximum_fusion.1.refs_0_, ...), custom_call_target="tpu_custom_call" | custom-call | flops 5637144576 | bytes 13893632 | tf_op jit(solution)/shard_map/forward/pallas_call | solution.py:92
  52.1 3.7 %collective-permute-start.14 = (bf16[4,3,128,896]{3,2,1,0:T(8,128)(2,1)}, bf16[4,3,128,896]{3,2,1,0:T(8,128)(2,1)S(1)}, u32[]{:S(2)}, u32[]{:S(2)}) collective-permute-start(bf16[4,3,128,896]{3,2,1,0:T(8,128)(2,1)} %get-tuple-element.22), channel_id=1, source_target_pairs={{16,0},{0,16},{48,32},{32,48},{80,64},{64,80},{112,96},{96,112},{1... | collective-permute-start | bytes 8257544 | tf_op jit(solution)/shard_map/ppermute | solution.py:33
  55.8 4.9 %collective-permute-done.14.got = bf16[4,3,128,896]{3,2,1,0:T(8,128)(2,1)S(1)} collective-permute-done((bf16[4,3,128,896]{3,2,1,0:T(8,128)(2,1)}, bf16[4,3,128,896]{3,2,1,0:T(8,128)(2,1)S(1)}, u32[]{:S(2)}, u32[]{:S(2)}) %collective-permute-start.14) | collective-permute-done | bytes 2752544 | tf_op jit(solution)/shard_map/ppermute | solution.py:33
  67.0 8.1 %collective-permute-done.15.r0 = bf16[3,64,896]{2,1,0:T(8,128)(2,1)S(1)} collective-permute-done((bf16[3,64,896]{2,1,0:T(8,128)(2,1)S(1)}, bf16[3,64,896]{2,1,0:T(8,128)(2,1)S(1)}, u32[]{:S(2)}, u32[]{:S(2)}) %collective-permute-start.15) | collective-permute-done | bytes 344096 | tf_op jit(solution)/shard_map/ppermute | solution.py:33
  75.7 2.3 %collective-permute-start.18 = (bf16[3,128,896]{2,1,0:T(8,128)(2,1)S(1)}, bf16[3,128,896]{2,1,0:T(8,128)(2,1)S(1)}, u32[]{:S(2)}, u32[]{:S(2)}) collective-permute-start(bf16[3,128,896]{2,1,0:T(8,128)(2,1)S(1)} %get-tuple-element.29), channel_id=1, source_target_pairs={{32,0},{48,16},{64,32},{80,48},{96,64},{112,80},{0,96},{16,112},{3... | collective-permute-start | bytes 2064392 | tf_op jit(solution)/shard_map/ppermute | solution.py:33
  78.0 14.6 %collective-permute-done.17.q1 = bf16[3,128,896]{2,1,0:T(8,128)(2,1)S(1)} collective-permute-done((bf16[3,128,896]{2,1,0:T(8,128)(2,1)S(1)}, bf16[3,128,896]{2,1,0:T(8,128)(2,1)S(1)}, u32[]{:S(2)}, u32[]{:S(2)}) %collective-permute-start.17) | collective-permute-done | bytes 688160 | tf_op jit(solution)/shard_map/ppermute | solution.py:33
  93.2 2.7 %collective-permute-start.19 = (bf16[3,128,896]{2,1,0:T(8,128)(2,1)S(1)}, bf16[3,128,896]{2,1,0:T(8,128)(2,1)S(1)}, u32[]{:S(2)}, u32[]{:S(2)}) collective-permute-start(bf16[3,128,896]{2,1,0:T(8,128)(2,1)S(1)} %activate.1), channel_id=1, source_target_pairs={{32,0},{48,16},{64,32},{80,48},{96,64},{112,80},{0,96},{16,112},{3... | collective-permute-start | bytes 2064392 | tf_op jit(solution)/shard_map/ppermute | solution.py:33
  95.8 13.7 %collective-permute-done.20 = bf16[3,128,896]{2,1,0:T(8,128)(2,1)S(1)} collective-permute-done((bf16[3,128,896]{2,1,0:T(8,128)(2,1)S(1)}, bf16[3,128,896]{2,1,0:T(8,128)(2,1)S(1)}, u32[]{:S(2)}, u32[]{:S(2)}) %collective-permute-start.20) | collective-permute-done | bytes 688160 | tf_op jit(solution)/shard_map/ppermute | solution.py:33
  109.7 2.7 %collective-permute-start.22 = (bf16[3,64,896]{2,1,0:T(8,128)(2,1)S(1)}, bf16[3,64,896]{2,1,0:T(8,128)(2,1)S(1)}, u32[]{:S(2)}, u32[]{:S(2)}) collective-permute-start(bf16[3,64,896]{2,1,0:T(8,128)(2,1)S(1)} %slice.39), channel_id=1, source_target_pairs={{32,0},{48,16},{64,32},{80,48},{96,64},{112,80},{0,96},{16,112},{3... | collective-permute-start | bytes 1032200 | tf_op jit(solution)/shard_map/ppermute | solution.py:33
  112.4 5.3 %collective-permute-done.21 = bf16[3,64,896]{2,1,0:T(8,128)(2,1)S(1)} collective-permute-done((bf16[3,64,896]{2,1,0:T(8,128)(2,1)S(1)}, bf16[3,64,896]{2,1,0:T(8,128)(2,1)S(1)}, u32[]{:S(2)}, u32[]{:S(2)}) %collective-permute-start.21) | collective-permute-done | bytes 344096 | tf_op jit(solution)/shard_map/ppermute | solution.py:33
  118.2 3.7 %collective-permute-start.23 = (bf16[4,3,128,896]{3,2,1,0:T(8,128)(2,1)S(1)}, bf16[4,3,128,896]{3,2,1,0:T(8,128)(2,1)S(1)}, u32[]{:S(2)}, u32[]{:S(2)}) collective-permute-start(bf16[4,3,128,896]{3,2,1,0:T(8,128)(2,1)S(1)} %pad_maximum_fusion.mine), channel_id=1, source_target_pairs={{16,0},{0,16},{48,32},{32,48},{80,64},{64,80},{112,96},{96,112},{1... | collective-permute-start | bytes 8257544 | tf_op jit(solution)/shard_map/ppermute | solution.py:33
  121.9 4.7 %collective-permute-done.23.theirs = bf16[4,3,128,896]{3,2,1,0:T(8,128)(2,1)S(1)} collective-permute-done((bf16[4,3,128,896]{3,2,1,0:T(8,128)(2,1)S(1)}, bf16[4,3,128,896]{3,2,1,0:T(8,128)(2,1)S(1)}, u32[]{:S(2)}, u32[]{:S(2)}) %collective-permute-start.23) | collective-permute-done | bytes 2752544 | tf_op jit(solution)/shard_map/ppermute | solution.py:33
  128.3 9.5 %backward.1 = (bf16[1024,896]{1,0:T(8,128)(2,1)S(1)}, bf16[1024,1792]{1,0:T(8,128)(2,1)}, bf16[16,64,1024]{2,1,0:T(8,128)(2,1)}) custom-call(s32[4]{0:T(128)S(1)} %pad_add_fusion.where, bf16[4,3,128,896]{3,2,1,0:T(8,128)(2,1)} %copy-done.6, bf16[4,3,128,896]{3,2,1,0:T(8,128)(2,1)} %copy-done.7, bf16[1024,896]{1,0:T(8,128)(2,1)S(1)} %copy-done.2, ...), custom_call_target="tpu_custom_call" | custom-call | flops 3758096384 | bytes 11272192 | tf_op jit(solution)/shard_map/backward/pallas_call | solution.py:201
  137.8 4.9 %all-to-all-start = ((bf16[16,64,1024]{2,1,0:T(8,128)(2,1)}), bf16[16,64,1024]{2,1,0:T(8,128)(2,1)}, u32[]{:S(2)}, u32[]{:S(2)}) async-start(bf16[16,64,1024]{2,1,0:T(8,128)(2,1)} %get-tuple-element.30), calls=%async_computation | async-start | bytes 4194304 | tf_op jit(solution)/shard_map/all_to_all | solution.py:312
  145.9 10.4 %weights.1 = (bf16[1024,896]{1,0:T(8,128)(2,1)}, bf16[1024,896]{1,0:T(8,128)(2,1)}, bf16[896,1024]{1,0:T(8,128)(2,1)}) custom-call(bf16[1024,1024]{1,0:T(8,128)(2,1)S(1)} %copy-done.4, bf16[1024,1024]{1,0:T(8,128)(2,1)S(1)} %copy-done.5, bf16[1024,896]{1,0:T(8,128)(2,1)S(1)} %get-tuple-element.33.hidden, bf16[1024,1792]{1,0:T(8,128)(2,1)} %get-tuple-element.34.both), custom_call_target="tpu_custom_call" | custom-call | flops 5637144576 | bytes 15204352 | tf_op jit(solution)/shard_map/weights/pallas_call | solution.py:236
  156.3 17.8 %all-to-all-done = bf16[16,64,1024]{2,1,0:T(8,128)(2,1)} async-done(((bf16[16,64,1024]{2,1,0:T(8,128)(2,1)}), bf16[16,64,1024]{2,1,0:T(8,128)(2,1)}, u32[]{:S(2)}, u32[]{:S(2)}) %all-to-all-start) | async-done | bytes 2097184 | tf_op jit(solution)/shard_map/all_to_all | solution.py:312
  174.0 2.7 %reduce_sum.12 = bf16[64,1024]{1,0:T(8,128)(2,1)} reduce(bf16[16,64,1024]{2,1,0:T(8,128)(2,1)} %all-to-all-done, bf16[]{:T(256)} %constant.56.clone.1), dimensions={0}, to_apply=%region_0.1 | reduce | flops 983040 | bytes 2228226 | tf_op jit(solution)/shard_map/reduce_sum | solution.py:314
  (61 shorter events, 28.3 us)
Async XLA Ops:
  1.6 9.1 %collective-permute-start.2 = (bf16[2,32,1024]{2,1,0:T(8,128)(2,1)S(1)}, bf16[2,32,1024]{2,1,0:T(8,128)(2,1)S(1)}, u32[]{:S(2)}, u32[]{:S(2)}) collective-permute-start(bf16[2,32,1024]{2,1,0:T(8,128)(2,1)S(1)} %get-tuple-element.39), channel_id=1, source_target_pairs={{4,0},{12,8},{5,1},{13,9},{6,2},{14,10},{7,3},{15,11},{0,4},{8,12}... | collective-permute-start | bytes 393224 | tf_op jit(solution)/shard_map/ppermute | solution.py:26
  5.2 7.1 %collective-permute-start.1 = (bf16[2,32,1024]{2,1,0:T(8,128)(2,1)S(1)}, bf16[2,32,1024]{2,1,0:T(8,128)(2,1)S(1)}, u32[]{:S(2)}, u32[]{:S(2)}) collective-permute-start(bf16[2,32,1024]{2,1,0:T(8,128)(2,1)S(1)} %get-tuple-element.39), channel_id=1, source_target_pairs={{6,0},{14,8},{7,1},{15,9},{0,2},{8,10},{1,3},{9,11},{2,4},{10,12},... | collective-permute-start | bytes 393224 | tf_op jit(solution)/shard_map/ppermute | solution.py:26
  5.6 6.8 %collective-permute-start = (bf16[2,32,1024]{2,1,0:T(8,128)(2,1)S(1)}, bf16[2,32,1024]{2,1,0:T(8,128)(2,1)S(1)}, u32[]{:S(2)}, u32[]{:S(2)}) collective-permute-start(bf16[2,32,1024]{2,1,0:T(8,128)(2,1)S(1)} %get-tuple-element.39), channel_id=1, source_target_pairs={{2,0},{10,8},{3,1},{11,9},{4,2},{12,10},{5,3},{13,11},{6,4},{14,12... | collective-permute-start | bytes 393224 | tf_op jit(solution)/shard_map/ppermute | solution.py:26
  7.9 7.2 %collective-permute-start.4 = (bf16[2,32,1024]{2,1,0:T(8,128)(2,1)S(1)}, bf16[2,32,1024]{2,1,0:T(8,128)(2,1)S(1)}, u32[]{:S(2)}, u32[]{:S(2)}) collective-permute-start(bf16[2,32,1024]{2,1,0:T(8,128)(2,1)S(1)} %get-tuple-element.38), channel_id=1, source_target_pairs={{9,0},{0,8},{8,1},{1,9},{11,2},{2,10},{10,3},{3,11},{13,4},{4,12},... | collective-permute-start | bytes 393224 | tf_op jit(solution)/shard_map/ppermute | solution.py:26
  10.7 6.5 %collective-permute-start.5 = (bf16[2,32,1024]{2,1,0:T(8,128)(2,1)S(1)}, bf16[2,32,1024]{2,1,0:T(8,128)(2,1)S(1)}, u32[]{:S(2)}, u32[]{:S(2)}) collective-permute-start(bf16[2,32,1024]{2,1,0:T(8,128)(2,1)S(1)} %get-tuple-element.38), channel_id=1, source_target_pairs={{1,0},{9,8},{0,1},{8,9},{3,2},{11,10},{2,3},{10,11},{5,4},{13,12},... | collective-permute-start | bytes 393224 | tf_op jit(solution)/shard_map/ppermute | solution.py:26
  12.4 15.5 %collective-permute-start.7 = (bf16[4,2,32,1024]{3,2,1,0:T(8,128)(2,1)S(1)}, bf16[4,2,32,1024]{3,2,1,0:T(8,128)(2,1)S(1)}, u32[]{:S(2)}, u32[]{:S(2)}) collective-permute-start(bf16[4,2,32,1024]{3,2,1,0:T(8,128)(2,1)S(1)} %pad_maximum_fusion.1.refs_0_), channel_id=1, source_target_pairs={{9,0},{0,8},{8,1},{1,9},{11,2},{2,10},{10,3},{3,11},{13,4},{4,12},... | collective-permute-start | bytes 1572872 | tf_op jit(solution)/shard_map/ppermute | solution.py:26
  13.3 15.3 %collective-permute-start.6 = (bf16[4,2,32,1024]{3,2,1,0:T(8,128)(2,1)S(1)}, bf16[4,2,32,1024]{3,2,1,0:T(8,128)(2,1)S(1)}, u32[]{:S(2)}, u32[]{:S(2)}) collective-permute-start(bf16[4,2,32,1024]{3,2,1,0:T(8,128)(2,1)S(1)} %pad_maximum_fusion.1.refs_0_), channel_id=1, source_target_pairs={{8,0},{1,8},{9,1},{0,9},{10,2},{3,10},{11,3},{2,11},{12,4},{5,12},... | collective-permute-start | bytes 1572872 | tf_op jit(solution)/shard_map/ppermute | solution.py:26
  17.3 14.8 %collective-permute-start.9 = (bf16[4,2,32,1024]{3,2,1,0:T(8,128)(2,1)S(1)}, bf16[4,2,32,1024]{3,2,1,0:T(8,128)(2,1)S(1)}, u32[]{:S(2)}, u32[]{:S(2)}) collective-permute-start(bf16[4,2,32,1024]{3,2,1,0:T(8,128)(2,1)S(1)} %pad_maximum_fusion.2.refs_1_), channel_id=1, source_target_pairs={{6,0},{14,8},{7,1},{15,9},{0,2},{8,10},{1,3},{9,11},{2,4},{10,12},... | collective-permute-start | bytes 1572872 | tf_op jit(solution)/shard_map/ppermute | solution.py:26
  17.4 15.4 %collective-permute-start.8 = (bf16[4,2,32,1024]{3,2,1,0:T(8,128)(2,1)S(1)}, bf16[4,2,32,1024]{3,2,1,0:T(8,128)(2,1)S(1)}, u32[]{:S(2)}, u32[]{:S(2)}) collective-permute-start(bf16[4,2,32,1024]{3,2,1,0:T(8,128)(2,1)S(1)} %pad_maximum_fusion.2.refs_1_), channel_id=1, source_target_pairs={{2,0},{10,8},{3,1},{11,9},{4,2},{12,10},{5,3},{13,11},{6,4},{14,12... | collective-permute-start | bytes 1572872 | tf_op jit(solution)/shard_map/ppermute | solution.py:26
  28.6 7.6 %collective-permute-start.11 = (bf16[2,2,32,1024]{3,2,1,0:T(8,128)(2,1)}, bf16[2,2,32,1024]{3,2,1,0:T(8,128)(2,1)S(1)}, u32[]{:S(2)}, u32[]{:S(2)}) collective-permute-start(bf16[2,2,32,1024]{3,2,1,0:T(8,128)(2,1)} %slice.35), channel_id=1, source_target_pairs={{9,0},{0,8},{8,1},{1,9},{11,2},{2,10},{10,3},{3,11},{13,4},{4,12},... | collective-permute-start | bytes 786440 | tf_op jit(solution)/shard_map/ppermute | solution.py:26
  29.4 6.9 %collective-permute-start.10 = (bf16[2,2,32,1024]{3,2,1,0:T(8,128)(2,1)}, bf16[2,2,32,1024]{3,2,1,0:T(8,128)(2,1)}, u32[]{:S(2)}, u32[]{:S(2)}) collective-permute-start(bf16[2,2,32,1024]{3,2,1,0:T(8,128)(2,1)} %slice.34), channel_id=1, source_target_pairs={{8,0},{1,8},{9,1},{0,9},{10,2},{3,10},{11,3},{2,11},{12,4},{5,12},... | collective-permute-start | bytes 786440 | tf_op jit(solution)/shard_map/ppermute | solution.py:26
  32.8 6.7 %collective-permute-start.13 = (bf16[2,2,32,1024]{3,2,1,0:T(8,128)(2,1)}, bf16[2,2,32,1024]{3,2,1,0:T(8,128)(2,1)}, u32[]{:S(2)}, u32[]{:S(2)}) collective-permute-start(bf16[2,2,32,1024]{3,2,1,0:T(8,128)(2,1)} %slice.37), channel_id=1, source_target_pairs={{6,0},{14,8},{7,1},{15,9},{0,2},{8,10},{1,3},{9,11},{2,4},{10,12},... | collective-permute-start | bytes 786440 | tf_op jit(solution)/shard_map/ppermute | solution.py:26
  33.5 6.3 %collective-permute-start.12 = (bf16[2,2,32,1024]{3,2,1,0:T(8,128)(2,1)}, bf16[2,2,32,1024]{3,2,1,0:T(8,128)(2,1)}, u32[]{:S(2)}, u32[]{:S(2)}) collective-permute-start(bf16[2,2,32,1024]{3,2,1,0:T(8,128)(2,1)} %slice.36), channel_id=1, source_target_pairs={{2,0},{10,8},{3,1},{11,9},{4,2},{12,10},{5,3},{13,11},{6,4},{14,12... | collective-permute-start | bytes 786440 | tf_op jit(solution)/shard_map/ppermute | solution.py:26
  52.1 8.7 %collective-permute-start.14 = (bf16[4,3,128,896]{3,2,1,0:T(8,128)(2,1)}, bf16[4,3,128,896]{3,2,1,0:T(8,128)(2,1)S(1)}, u32[]{:S(2)}, u32[]{:S(2)}) collective-permute-start(bf16[4,3,128,896]{3,2,1,0:T(8,128)(2,1)} %get-tuple-element.22), channel_id=1, source_target_pairs={{16,0},{0,16},{48,32},{32,48},{80,64},{64,80},{112,96},{96,112},{1... | collective-permute-start | bytes 8257544 | tf_op jit(solution)/shard_map/ppermute | solution.py:33
  63.1 12.0 %collective-permute-start.15 = (bf16[3,64,896]{2,1,0:T(8,128)(2,1)S(1)}, bf16[3,64,896]{2,1,0:T(8,128)(2,1)S(1)}, u32[]{:S(2)}, u32[]{:S(2)}) collective-permute-start(bf16[3,64,896]{2,1,0:T(8,128)(2,1)S(1)} %get-tuple-element.26), channel_id=1, source_target_pairs={{96,0},{112,16},{0,32},{16,48},{32,64},{48,80},{64,96},{80,112},{9... | collective-permute-start | bytes 1032200 | tf_op jit(solution)/shard_map/ppermute | solution.py:33
  64.9 10.3 %collective-permute-start.16 = (bf16[3,64,896]{2,1,0:T(8,128)(2,1)S(1)}, bf16[3,64,896]{2,1,0:T(8,128)(2,1)S(1)}, u32[]{:S(2)}, u32[]{:S(2)}) collective-permute-start(bf16[3,64,896]{2,1,0:T(8,128)(2,1)S(1)} %get-tuple-element.27), channel_id=1, source_target_pairs={{32,0},{48,16},{64,32},{80,48},{96,64},{112,80},{0,96},{16,112},{3... | collective-permute-start | bytes 1032200 | tf_op jit(solution)/shard_map/ppermute | solution.py:33
  75.3 17.3 %collective-permute-start.17 = (bf16[3,128,896]{2,1,0:T(8,128)(2,1)S(1)}, bf16[3,128,896]{2,1,0:T(8,128)(2,1)S(1)}, u32[]{:S(2)}, u32[]{:S(2)}) collective-permute-start(bf16[3,128,896]{2,1,0:T(8,128)(2,1)S(1)} %get-tuple-element.28), channel_id=1, source_target_pairs={{96,0},{112,16},{0,32},{16,48},{32,64},{48,80},{64,96},{80,112},{9... | collective-permute-start | bytes 2064392 | tf_op jit(solution)/shard_map/ppermute | solution.py:33
  75.7 16.9 %collective-permute-start.18 = (bf16[3,128,896]{2,1,0:T(8,128)(2,1)S(1)}, bf16[3,128,896]{2,1,0:T(8,128)(2,1)S(1)}, u32[]{:S(2)}, u32[]{:S(2)}) collective-permute-start(bf16[3,128,896]{2,1,0:T(8,128)(2,1)S(1)} %get-tuple-element.29), channel_id=1, source_target_pairs={{32,0},{48,16},{64,32},{80,48},{96,64},{112,80},{0,96},{16,112},{3... | collective-permute-start | bytes 2064392 | tf_op jit(solution)/shard_map/ppermute | solution.py:33
  93.1 16.4 %collective-permute-start.20 = (bf16[3,128,896]{2,1,0:T(8,128)(2,1)S(1)}, bf16[3,128,896]{2,1,0:T(8,128)(2,1)S(1)}, u32[]{:S(2)}, u32[]{:S(2)}) collective-permute-start(bf16[3,128,896]{2,1,0:T(8,128)(2,1)S(1)} %activate.1), channel_id=1, source_target_pairs={{96,0},{112,16},{0,32},{16,48},{32,64},{48,80},{64,96},{80,112},{9... | collective-permute-start | bytes 2064392 | tf_op jit(solution)/shard_map/ppermute | solution.py:33
  93.2 16.5 %collective-permute-start.19 = (bf16[3,128,896]{2,1,0:T(8,128)(2,1)S(1)}, bf16[3,128,896]{2,1,0:T(8,128)(2,1)S(1)}, u32[]{:S(2)}, u32[]{:S(2)}) collective-permute-start(bf16[3,128,896]{2,1,0:T(8,128)(2,1)S(1)} %activate.1), channel_id=1, source_target_pairs={{32,0},{48,16},{64,32},{80,48},{96,64},{112,80},{0,96},{16,112},{3... | collective-permute-start | bytes 2064392 | tf_op jit(solution)/shard_map/ppermute | solution.py:33
  109.5 8.1 %collective-permute-start.21 = (bf16[3,64,896]{2,1,0:T(8,128)(2,1)S(1)}, bf16[3,64,896]{2,1,0:T(8,128)(2,1)S(1)}, u32[]{:S(2)}, u32[]{:S(2)}) collective-permute-start(bf16[3,64,896]{2,1,0:T(8,128)(2,1)S(1)} %slice.38), channel_id=1, source_target_pairs={{96,0},{112,16},{0,32},{16,48},{32,64},{48,80},{64,96},{80,112},{9... | collective-permute-start | bytes 1032200 | tf_op jit(solution)/shard_map/ppermute | solution.py:33
  109.7 8.0 %collective-permute-start.22 = (bf16[3,64,896]{2,1,0:T(8,128)(2,1)S(1)}, bf16[3,64,896]{2,1,0:T(8,128)(2,1)S(1)}, u32[]{:S(2)}, u32[]{:S(2)}) collective-permute-start(bf16[3,64,896]{2,1,0:T(8,128)(2,1)S(1)} %slice.39), channel_id=1, source_target_pairs={{32,0},{48,16},{64,32},{80,48},{96,64},{112,80},{0,96},{16,112},{3... | collective-permute-start | bytes 1032200 | tf_op jit(solution)/shard_map/ppermute | solution.py:33
  118.2 8.4 %collective-permute-start.23 = (bf16[4,3,128,896]{3,2,1,0:T(8,128)(2,1)S(1)}, bf16[4,3,128,896]{3,2,1,0:T(8,128)(2,1)S(1)}, u32[]{:S(2)}, u32[]{:S(2)}) collective-permute-start(bf16[4,3,128,896]{3,2,1,0:T(8,128)(2,1)S(1)} %pad_maximum_fusion.mine), channel_id=1, source_target_pairs={{16,0},{0,16},{48,32},{32,48},{80,64},{64,80},{112,96},{96,112},{1... | collective-permute-start | bytes 8257544 | tf_op jit(solution)/shard_map/ppermute | solution.py:33
  137.8 36.2 %all-to-all-start = ((bf16[16,64,1024]{2,1,0:T(8,128)(2,1)}), bf16[16,64,1024]{2,1,0:T(8,128)(2,1)}, u32[]{:S(2)}, u32[]{:S(2)}) async-start(bf16[16,64,1024]{2,1,0:T(8,128)(2,1)} %get-tuple-element.30), calls=%async_computation | async-start | bytes 4194304 | tf_op jit(solution)/shard_map/all_to_all | solution.py:312
  (9 other events, 43.5 us)

commit v2 on v0

v2 whole, which is shorter than its diff:
```python
import functools

import jax
import jax.numpy as jnp
from jax import lax
from jax.experimental import pallas as pl
from jax.experimental.pallas import tpu as pltpu
from jax.sharding import PartitionSpec as P

XY = ("out", "dep")
ALL = ("inp", "out", "dep")
BF = jnp.bfloat16
F32 = jnp.float32
MB = 1024 * 1024
PIECE = 32
OFFSETS = (0, 1, 3, 2)
ROWS = (((0,), (0,)), ((), ()))
LANES = (((1,), (1,)), ((), ()))


def index(x, y, z, c):
    return (z * 2 + c) * 16 + ((y % 2) * 4 + x) * 2 + y // 2


def from_where(value, shift):
    pairs = []
    for x in range(4):
        for y in range(4):
            for z in range(4):
                for c in range(2):
                    a, b, d, e = shift(x, y, z, c)
                    pairs.append((index(a % 4, b % 4, d % 4, e % 2), index(x, y, z, c)))
    return lax.ppermute(value, ALL, pairs)


def from_line(value, step):
    return from_where(value, lambda x, y, z, c: (x + (step if c == 0 else 0), y + (step if c == 1 else 0), z, c))


def from_side(value, step):
    return from_where(value, lambda x, y, z, c: (x + (step if c == 1 else 0), y + (step if c == 0 else 0), z, c))


def from_z(value, step):
    return from_where(value, lambda x, y, z, c: (x, y, z + step, c))


def from_core(value):
    return from_where(value, lambda x, y, z, c: (x, y, z, c + 1))


def params(mb=48):
    return pltpu.CompilerParams(vmem_limit_bytes=mb * MB)


def vmem(n):
    return [pl.BlockSpec(memory_space=pltpu.VMEM)] * n


def shape(*dims, dtype=BF):
    return jax.ShapeDtypeStruct(dims, dtype)


def hbm(arrays):
    return [pltpu.with_memory_space_constraint(a, pltpu.HBM) for a in arrays]


SMEM = pl.BlockSpec(memory_space=pltpu.SMEM)


def place_of(i, per, z):
    if z is None:
        return i * PIECE
    away = lax.rem(i // per - z + 4, 4)
    away = jnp.where(away == 3, 2, jnp.where(away == 2, 3, away))
    return pl.multiple_of((away * per + i % per) * PIECE, PIECE)


def forward_kernel(counts, ring, where, *refs):
    n = len(counts)
    pieces, mine, other = refs[:n], refs[n:n + 3], refs[n + 3:n + 6]
    rows_mine, rows_other, *outs, rows, wide, down, sems = refs[n + 6:]
    held = wide.at[0], wide.at[1], wide.at[2], wide.at[3], down.at[0], down.at[1]
    per = sum(counts) // 4
    t = per * PIECE
    moves = []
    for ref, count in zip(pieces, counts):
        for j in range(count):
            row = place_of(len(moves), per, where[0] if ring else None)
            moves.append((ref.at[j], rows.at[:, :, pl.ds(row, PIECE), :]))
    total = len(moves)
    moves += list(zip((mine[0], other[0], mine[1], other[1], mine[2], other[2]), held))
    copies = [pltpu.make_async_copy(a, b, sems.at[k]) for k, (a, b) in enumerate(moves)]
    for copy in copies:
        copy.start()
    for copy in copies[:total]:
        copy.wait()
    copies = copies[total:]
    results = [pltpu.make_async_copy(rows.at[k], out, sems.at[k]) for k, out in enumerate((rows_mine, rows_other))]
    for copy in results:
        copy.start()
    for m in range(3):
        src = 0 if m < 2 else 1
        dims = (((1,), (0,)), ((), ())) if m < 2 else LANES
        copies[2 * m].wait()
        copies[2 * m + 1].wait()
        v = lax.dot_general(rows[0, src], held[2 * m][...], dims, preferred_element_type=F32)
        v = v + lax.dot_general(rows[1, src], held[2 * m + 1][...], dims, preferred_element_type=F32)
        v = v.astype(BF)
        for block in range(4):
            part = v[block * t:(block + 1) * t]
            if not ring:
                outs[0][block, m] = part
            elif block < 3:
                outs[block][m] = part
            else:
                outs[3][m] = part[: t // 2]
                outs[4][m] = part[t // 2:]
    for copy in results:
        copy.wait()


def forward(where, pieces, mine, other, ring):
    counts = tuple(p.shape[0] for p in pieces)
    t = sum(counts) // 4 * PIECE
    d, f = mine[0].shape
    rows = pltpu.HBM((2, 4 * t, d), BF)
    whole, half = shape(3, t, f), shape(3, t // 2, f)
    outs = (whole, whole, whole, half, half) if ring else (shape(4, 3, t, f),)
    far = [pl.BlockSpec(memory_space=pltpu.HBM)]
    return pl.pallas_call(
        functools.partial(forward_kernel, counts, ring),
        out_shape=(rows, rows, *outs),
        in_specs=[SMEM] + far * (len(pieces) + 6),
        out_specs=far * 2 + vmem(len(outs)),
        scratch_shapes=[
            pltpu.VMEM((2, 2, 4 * t, d), BF),
            pltpu.VMEM((4, d, f), BF),
            pltpu.VMEM((2, f, d), BF),
            pltpu.SemaphoreType.DMA((sum(counts) + 6,)),
        ],
        compiler_params=params(18 + 16 * t // 256),
        cost_estimate=pl.CostEstimate(flops=12 * 4 * t * d * f, bytes_accessed=12 * d * f + 64 * t * d, transcendentals=0),
        name="forward",
    )(where, *hbm(pieces), *hbm(mine), *hbm(other))


def add_far_kernel(b1, b2, r0, r1, o1, o2):
    t = b1.shape[1]
    o1[:, : t // 2] = (b1[:, : t // 2].astype(F32) + r0[...].astype(F32)).astype(BF)
    o1[:, t // 2:] = b1[:, t // 2:]
    o2[:, : t // 2] = b2[:, : t // 2]
    o2[:, t // 2:] = (b2[:, t // 2:].astype(F32) + r1[...].astype(F32)).astype(BF)


def add_far(b1, b2, r0, r1):
    return pl.pallas_call(
        add_far_kernel,
        out_shape=(shape(*b1.shape), shape(*b1.shape)),
        in_specs=vmem(4),
        out_specs=vmem(2),
        compiler_params=params(8),
        name="add_far",
    )(b1, b2, r0, r1)


def activate_kernel(n, *refs):
    parts, outs = refs[:n], refs[n:]

    def total(m):
        if n == 1:
            return sum(parts[0][k, m].astype(F32) for k in range(4))
        return sum(p[m].astype(F32) for p in parts)

    gate, up, back = (total(m) for m in range(3))
    sig = 1.0 / (1.0 + jnp.exp(-gate))
    silu = gate * sig
    values = (silu * up, back * up * sig * (1.0 + gate * (1.0 - sig)), back * silu)
    for m, v in enumerate(values):
        v = v.astype(BF)
        if n == 1:
            for k in range(4):
                outs[0][k, m] = v
        else:
            outs[0][m] = v


def activate(*parts):
    return pl.pallas_call(
        functools.partial(activate_kernel, len(parts)),
        out_shape=shape(*parts[0].shape),
        in_specs=vmem(len(parts)),
        out_specs=vmem(1)[0],
        compiler_params=params(8),
        name="activate",
    )(*parts)


def assemble_kernel(n, *refs):
    out = refs[n]
    if n == 1:
        t = refs[0].shape[2]
        for k in range(4):
            for m in range(3):
                out[m, k * t:(k + 1) * t] = refs[0][k, m]
        return
    t = refs[0].shape[1]
    for k in range(3):
        out[:, k * t:(k + 1) * t] = refs[k][...]
    out[:, 3 * t:3 * t + t // 2] = refs[3][...]
    out[:, 3 * t + t // 2:] = refs[4][...]


def assemble(*parts):
    *_, t, f = parts[0].shape
    return pl.pallas_call(
        functools.partial(assemble_kernel, len(parts)),
        out_shape=shape(3, 4 * t, f),
        in_specs=vmem(len(parts)),
        out_specs=vmem(1)[0],
        compiler_params=params(12),
        name="assemble",
    )(*parts)


def backward_kernel(counts, ring, where, trio, *refs):
    mine, other = refs[:2], refs[2:4]
    outs, (res, held, sems) = refs[4:-3], refs[-3:]
    copies = [pltpu.make_async_copy(w, held.at[k], sems.at[k]) for k, w in enumerate((*mine, *other))]
    for copy in copies:
        copy.start()
    per = sum(counts) // 4
    for b in range(2):
        copies[2 * b].wait()
        v = lax.dot_general(trio[1], held[2 * b], LANES, preferred_element_type=F32)
        copies[2 * b + 1].wait()
        v = v + lax.dot_general(trio[2], held[2 * b + 1], LANES, preferred_element_type=F32)
        res[b] = v.astype(BF)
    i = 0
    for ref, count in zip(outs, counts):
        for j in range(count):
            row = place_of(i, per, where[0] if ring else None)
            for b in range(2):
                ref[j, b] = res[b, pl.ds(row, PIECE), :]
            i += 1


def backward(where, trio, mine, other, counts, ring):
    _, tokens, f = trio.shape
    d = mine[0].shape[0]
    return pl.pallas_call(
        functools.partial(backward_kernel, counts, ring),
        out_shape=tuple(shape(n, 2, PIECE, d) for n in counts),
        in_specs=[SMEM] + vmem(1) + [pl.BlockSpec(memory_space=pltpu.HBM)] * 4,
        out_specs=tuple(vmem(len(counts))),
        scratch_shapes=[pltpu.VMEM((2, tokens, d), BF), pltpu.VMEM((4, d, f), BF), pltpu.SemaphoreType.DMA((4,))],
        compiler_params=params(12 + 14 * tokens // 512),
        cost_estimate=pl.CostEstimate(flops=8 * tokens * d * f, bytes_accessed=8 * d * f + tokens * (6 * f + 4 * d), transcendentals=0),
        name="backward",
    )(where, trio, *mine[:2], *other[:2])


def weights_kernel(n, *refs):
    rows, trios = refs[:n], refs[n:2 * n]
    o_gate, o_up, x, both = refs[2 * n:]
    f = o_gate.shape[1]

    @pl.when(pl.program_id(0) == 0)
    def _():
        at = 0
        for ref in trios:
            k = ref.shape[1]
            both[at:at + k, :f] = ref[0]
            both[at:at + k, f:] = ref[1]
            at += k

    at = 0
    for ref in rows:
        k = ref.shape[1]
        x[at:at + k, :] = ref[0]
        at += k
    value = lax.dot_general(x[...], both[...], ROWS, preferred_element_type=F32).astype(BF)
    o_gate[...] = value[:, :f]
    o_up[...] = value[:, f:]


def weights(rows, trios):
    n = len(rows)
    d, f = rows[0].shape[2], trios[0].shape[2]
    tokens = sum(t.shape[1] for t in trios)
    w = 512
    return pl.pallas_call(
        functools.partial(weights_kernel, n),
        grid=(d // w,),
        out_shape=(shape(d, f), shape(d, f)),
        in_specs=[pl.BlockSpec((1, r.shape[1], w), lambda i: (0, 0, i)) for r in rows]
        + [pl.BlockSpec((pl.Element(2, (0, 0)), pl.Element(t.shape[1]), pl.Element(f)), lambda i: (1, 0, 0)) for t in trios],
        out_specs=[pl.BlockSpec((w, f), lambda i: (i, 0))] * 2,
        scratch_shapes=[pltpu.VMEM((tokens, w), BF), pltpu.VMEM((tokens, 2 * f), BF)],
        compiler_params=params(32),
        cost_estimate=pl.CostEstimate(flops=4 * tokens * d * f, bytes_accessed=4 * d * f + tokens * (2 * d + 4 * f), transcendentals=0),
        name="weights",
    )(*rows, *trios)


def down_kernel(n, *refs):
    rows, trios = refs[:n], refs[n:2 * n]
    o_down, y, turned = refs[2 * n:]

    @pl.when(pl.program_id(0) == 0)
    def _():
        at = 0
        for ref in trios:
            k = ref.shape[1]
            turned[:, at:at + k] = ref[0].T
            at += k

    at = 0
    for ref in rows:
        k = ref.shape[1]
        y[at:at + k, :] = ref[0]
        at += k
    o_down[...] = jnp.dot(turned[...], y[...], preferred_element_type=F32).astype(BF)


def down_weights(rows, trios):
    n = len(rows)
    d, f = rows[0].shape[2], trios[0].shape[2]
    tokens = sum(t.shape[1] for t in trios)
    w = 512
    return pl.pallas_call(
        functools.partial(down_kernel, n),
        grid=(d // w,),
        out_shape=shape(f, d),
        in_specs=[pl.BlockSpec((1, r.shape[1], w), lambda i: (1, 0, i)) for r in rows]
        + [pl.BlockSpec((1, t.shape[1], f), lambda i: (0, 0, 0)) for t in trios],
        out_specs=pl.BlockSpec((f, w), lambda i: (0, i)),
        scratch_shapes=[pltpu.VMEM((tokens, w), BF), pltpu.VMEM((f, tokens), BF)],
        compiler_params=params(32),
        cost_estimate=pl.CostEstimate(flops=2 * tokens * d * f, bytes_accessed=2 * d * f + tokens * (2 * d + 2 * f), transcendentals=0),
        name="down_weights",
    )(*rows, *trios)


def plus(a, *rest):
    total = a.astype(F32)
    for b in rest:
        total = total + b.astype(F32)
    return total


def after(value, *others):
    return lax.optimization_barrier((value, others))[0]


def to_all_z(value):
    return lax.all_to_all(value, "inp", 0, 0, axis_index_groups=[[0, 2, 4, 6], [1, 3, 5, 7]])


def local(tokens_in, grad_out, w_gate, w_up, w_down):
    inp = lax.axis_index("inp")
    core = inp % 2
    where = jnp.stack([inp // 2]).astype(jnp.int32)
    mine = (w_gate, w_up, w_down)

    own = jnp.stack([tokens_in, grad_out])
    kept = lax.dynamic_slice_in_dim(own, core * PIECE, PIECE, axis=1)
    given = lax.dynamic_slice_in_dim(own, (1 - core) * PIECE, PIECE, axis=1)
    piece = jnp.stack([kept, from_core(given)])
    line = jnp.stack([piece] + [from_line(piece, o) for o in OFFSETS[1:]])
    other = tuple(from_core(w) for w in after(mine, line))
    ahead, behind = from_side(line, 1), from_side(line, -1)
    far = from_side(ahead[:2], 1), from_side(behind[2:], -1)

    near_pieces = (line, ahead, behind)
    near_mine, near_other, b0, b1, b2, h0, h1 = forward(where, near_pieces, mine, other, True)
    r0, r1 = from_z(h0, -1), from_z(h1, 1)
    far_mine, far_other, parts = forward(where, far, mine, other, False)
    r0, r1 = after((r0, r1), parts)
    sums_far = to_all_z(parts)
    b1, b2 = add_far(b1, b2, r0, r1)
    q1, q2 = from_z(b1, -1), from_z(b2, 1)
    near_got, far_got = from_core(near_other), from_core(far_other)
    trio_far = activate(sums_far)
    q1, q2 = after((q1, q2), trio_far)
    trio = activate(b0, q1, q2)
    t = trio.shape[1]
    up, down = from_z(trio, 1), from_z(trio, -1)
    trio_far = assemble(to_all_z(trio_far))
    trio_far_got = from_core(trio_far)
    up, down = after((up, down), trio_far)
    far0, far1 = backward(where, trio_far, mine, other, (2, 2), False)
    up, down = after((up, down), (far0, far1))
    far0, far1 = from_side(far0, -1), from_side(far1, 1)
    trio = assemble(trio, up, down, from_z(down[:, : t // 2], -1), from_z(up[:, t // 2:], 1))
    trio_got = from_core(trio)
    line, ahead, behind = backward(where, trio, mine, other, (4, 4, 4), True)

    ahead = jnp.concatenate([plus(ahead[:2], far0).astype(BF), ahead[2:]])
    behind = jnp.concatenate([behind[:2], plus(behind[2:], far1).astype(BF)])
    ahead, behind = from_side(ahead, -1), from_side(behind, 1)

    rows = near_mine, far_mine, near_got, far_got
    trios = trio, trio_far, trio_got, trio_far_got
    gate_up = weights(rows, trios)
    ahead, behind = after((ahead, behind), gate_up)

    line = plus(line, ahead, behind)
    sent = [from_line(line[j].astype(BF), -OFFSETS[j]) for j in range(1, 4)]
    grad_w_down = down_weights(rows, trios)
    sent = after(sent, grad_w_down)
    sums = plus(line[0], *sent).astype(BF)
    got = from_core(sums[1])
    first = core == 0
    grad_tokens = jnp.concatenate([jnp.where(first, sums[0], got), jnp.where(first, got, sums[0])])
    return (grad_tokens, *gate_up, grad_w_down)


def solution(mesh):
    return jax.shard_map(
        local,
        mesh=mesh,
        in_specs=(P(XY, "inp"), P(XY, "inp"), P("inp", XY), P("inp", XY), P(XY, "inp")),
        out_specs=(P(XY, "inp"), P("inp", XY), P("inp", XY), P(XY, "inp")),
        check_vma=False,
    )
```

time: 387 us -> 144 us (0.37); the launches traced: 381 us -> 144 us
  waiting for transfers between devices: 303 us -> 43.5 us
  starting transfers between devices: 0.34 us -> 51.7 us
  Pallas kernels: 0 us -> 38.6 us
  matrix products: 31.1 us -> 0 us
  local copies, waits for them, and re-layouts: 21.9 us -> 6.58 us
  between operations: 13.8 us -> 1 us
  other arithmetic: 10.7 us -> 2.53 us
    all_gather x2 -> x0, waiting for transfers between devices: 141 us -> none  [the longest x1 75.7 us: local(): lax.all_gather(tokens_in, ('out', 'dep'), axis=0, tiled=True)]
    psum x1 -> x0, waiting for transfers between devices: 88.6 us -> none  [hidden_terms(): sums = lax.psum(partials.astype(jnp.bfloat16), 'inp').astype(jnp.float32)]
    reduce_scatter x1 -> x0, waiting for transfers between devices: 72.5 us -> none  [local(): lax.psum_scatter(input_terms, ('out', 'dep'), scatter_dimension=0, tiled=...]
    ppermute x0 -> x31, starting transfers between devices: none -> 44.6 us  [from_where(): return lax.ppermute(value, ALL, pairs)]
    pallas_call x0 -> x11, Pallas kernels: none -> 38.6 us  [the longest x2 16.1 us: forward(): pl.pallas_call(functools.partial(forward_kernel, counts, ring), out_shape...]
    ppermute x0 -> x31, waiting for transfers between devices: none -> 35.2 us  [from_where(): return lax.ppermute(value, ALL, pairs)]
    dot_general x5 -> x0, matrix products: 31.1 us -> none  [the longest x1 7.14 us: local_grads(): jnp.einsum('tf,te->fe', trio[0], dy_rows, preferred_element_type=jnp.floa...]
    unnamed x18 -> x26, local copies, waits for them, and re-layouts: 19.7 us -> 3.66 us
  transfers between devices with their start and end apart: 4 -> 33, of which waited for: 4 -> 15; matrix products, arithmetic and copies ran while one was open for 9% -> 1% of each run, Pallas kernels for 0% -> 26%
where the time goes in v2:
time: 144 us
  starting transfers between devices  51.7 us (36%)
  waiting for transfers between devices  43.5 us (30%)
  Pallas kernels  38.6 us (27%)
  local copies, waits for them, and re-layouts  6.58 us (5%)
  other arithmetic  2.53 us (2%)
    ppermute x31, starting transfers between devices, from_where(): return lax.ppermute(value, ALL, pairs)  44.6 us
    ppermute x31, waiting for transfers between devices, from_where(): return lax.ppermute(value, ALL, pairs)  35.2 us
    pallas_call x2, Pallas kernels, forward(): pl.pallas_call(functools.partial(forward_kernel, counts, ring), out_shape...  16.1 us
    all_to_all x2, waiting for transfers between devices, to_all_z(): lax.all_to_all(value, 'inp', 0, 0, axis_index_groups=[[0, 2, 4, 6], [1, 3...  8.31 us
    pallas_call x2, Pallas kernels, backward(): pl.pallas_call(functools.partial(backward_kernel, counts, ring), out_shap...  8.14 us
    all_to_all x2, starting transfers between devices, to_all_z(): lax.all_to_all(value, 'inp', 0, 0, axis_index_groups=[[0, 2, 4, 6], [1, 3...  7.16 us
    pallas_call x1, Pallas kernels, weights(): pl.pallas_call(functools.partial(weights_kernel, n), grid=(d // w,), out_...  5.65 us
    pallas_call x1, Pallas kernels, down_weights(): pl.pallas_call(functools.partial(down_kernel, n), grid=(d // w,), out_sha...  3.93 us
  transfers between devices with their start and end apart: 33, of which 15 were waited for; matrix products, arithmetic and copies ran while one was open for 1% of the time, Pallas kernels for 26%

profile of v2, /device:TPU:1, one launch (start us, length us, event | category | flops | bytes accessed | tf_op | source)
XLA Modules:
  0.0 143.9 jit_solution(1951604226649221431)
XLA Ops:
  4.3 3.1 %collective-permute-start.3 = (bf16[2,2,32,1024]{3,2,1,0:T(8,128)(2,1)S(1)}, bf16[2,2,32,1024]{3,2,1,0:T(8,128)(2,1)S(1)}, u32[]{:S(2)}, u32[]{:S(2)}) collective-permute-start(bf16[2,2,32,1024]{3,2,1,0:T(8,128)(2,1)S(1)} %get-tuple-element.80), channel_id=1, source_target_pairs={{4,0},{17,16},{36,32},{49,48},{68,64},{81,80},{100,96},{113,112},{... | collective-permute-start | bytes 786440 | tf_op jit(solution)/shard_map/ppermute | solution.py:33
  7.8 2.3 %collective-permute-start.1 = (bf16[2,2,32,1024]{3,2,1,0:T(8,128)(2,1)S(1)}, bf16[2,2,32,1024]{3,2,1,0:T(8,128)(2,1)S(1)}, u32[]{:S(2)}, u32[]{:S(2)}) collective-permute-start(bf16[2,2,32,1024]{3,2,1,0:T(8,128)(2,1)S(1)} %get-tuple-element.80), channel_id=1, source_target_pairs={{2,0},{24,16},{34,32},{56,48},{66,64},{88,80},{98,96},{120,112},{1... | collective-permute-start | bytes 786440 | tf_op jit(solution)/shard_map/ppermute | solution.py:33
  11.4 2.8 %collective-permute-done.2 = bf16[2,2,32,1024]{3,2,1,0:T(8,128)(2,1)S(1)} collective-permute-done((bf16[2,2,32,1024]{3,2,1,0:T(8,128)(2,1)S(1)}, bf16[2,2,32,1024]{3,2,1,0:T(8,128)(2,1)S(1)}, u32[]{:S(2)}, u32[]{:S(2)}) %collective-permute-start.2) | collective-permute-done | bytes 262176 | tf_op jit(solution)/shard_map/ppermute | solution.py:33
  16.3 2.8 %collective-permute-start.4 = (bf16[4,2,2,32,1024]{4,3,2,1,0:T(8,128)(2,1)S(1)}, bf16[4,2,2,32,1024]{4,3,2,1,0:T(8,128)(2,1)S(1)}, u32[]{:S(2)}, u32[]{:S(2)}) collective-permute-start(bf16[4,2,2,32,1024]{4,3,2,1,0:T(8,128)(2,1)S(1)} %pad_maximum_fusion.refs_0_), channel_id=1, source_target_pairs={{8,0},{18,16},{40,32},{50,48},{72,64},{82,80},{104,96},{114,112},{... | collective-permute-start | bytes 3145736 | tf_op jit(solution)/shard_map/ppermute | solution.py:33
  19.1 11.7 %collective-permute-done.4.refs_1_ = bf16[4,2,2,32,1024]{4,3,2,1,0:T(8,128)(2,1)S(1)} collective-permute-done((bf16[4,2,2,32,1024]{4,3,2,1,0:T(8,128)(2,1)S(1)}, bf16[4,2,2,32,1024]{4,3,2,1,0:T(8,128)(2,1)S(1)}, u32[]{:S(2)}, u32[]{:S(2)}) %collective-permute-start.4) | collective-permute-done | bytes 1048608 | tf_op jit(solution)/shard_map/ppermute | solution.py:33
  31.8 3.4 %collective-permute-start.11 = (bf16[2,2,2,32,1024]{4,3,2,1,0:T(8,128)(2,1)}, bf16[2,2,2,32,1024]{4,3,2,1,0:T(8,128)(2,1)}, u32[]{:S(2)}, u32[]{:S(2)}) collective-permute-start(bf16[2,2,2,32,1024]{4,3,2,1,0:T(8,128)(2,1)} %slice.60), channel_id=1, source_target_pairs={{8,0},{18,16},{40,32},{50,48},{72,64},{82,80},{104,96},{114,112},{... | collective-permute-start | bytes 1572872 | tf_op jit(solution)/shard_map/ppermute | solution.py:33
  36.4 9.0 %forward.2 = (bf16[2,384,1024]{2,1,0:T(8,128)(2,1)}, bf16[2,384,1024]{2,1,0:T(8,128)(2,1)}, bf16[3,96,896]{2,1,0:T(8,128)(2,1)S(1)}, bf16[3,96,896]{2,1,0:T(8,12...) custom-call(s32[1]{0:T(128)} %bitcast.where, ...), custom_call_target="tpu_custom_call" | custom-call | flops 4227858432 | bytes 17301504 | tf_op jit(solution)/shard_map/forward/pallas_call | solution.py:131
  47.2 2.2 %collective-permute-start.10 = (bf16[3,48,896]{2,1,0:T(8,128)(2,1)S(1)}, bf16[3,48,896]{2,1,0:T(8,128)(2,1)S(1)}, u32[]{:S(2)}, u32[]{:S(2)}) collective-permute-start(bf16[3,48,896]{2,1,0:T(8,128)(2,1)S(1)} %get-tuple-element.46), channel_id=1, source_target_pairs={{32,0},{48,16},{64,32},{80,48},{96,64},{112,80},{0,96},{16,112},{4... | collective-permute-start | bytes 774152 | tf_op jit(solution)/shard_map/ppermute | solution.py:33
  49.4 7.1 %forward.3 = (bf16[2,128,1024]{2,1,0:T(8,128)(2,1)}, bf16[2,128,1024]{2,1,0:T(8,128)(2,1)}, bf16[4,3,32,896]{3,2,1,0:T(8,128)(2,1)}) custom-call(s32[1]{0:T(128)} %bitcast.where, bf16[2,2,2,32,1024]{4,3,2,1,0:T(8,128)(2,1)} %collective-permute-done.11.refs_0_, bf16[2,2,2,32,1024]{4,3,2,1,0:T(8,128)(2,1)} %collective-permute-done.12.refs_1_, ...), custom_call_target="tpu_custom_call" | custom-call | flops 1409286144 | bytes 13107200 | tf_op jit(solution)/shard_map/forward/pallas_call | solution.py:131
  56.5 3.5 %all-to-all-start = ((bf16[4,3,32,896]{3,2,1,0:T(8,128)(2,1)}), bf16[4,3,32,896]{3,2,1,0:T(8,128)(2,1)S(1)}, u32[]{:S(2)}, u32[]{:S(2)}) async-start(bf16[4,3,32,896]{3,2,1,0:T(8,128)(2,1)} %get-tuple-element.47), calls=%async_computation | async-start | bytes 1376256 | tf_op jit(solution)/shard_map/all_to_all | solution.py:357
  63.8 5.7 %all-to-all-done.refs_0_ = bf16[4,3,32,896]{3,2,1,0:T(8,128)(2,1)S(1)} async-done(((bf16[4,3,32,896]{3,2,1,0:T(8,128)(2,1)}), bf16[4,3,32,896]{3,2,1,0:T(8,128)(2,1)S(1)}, u32[]{:S(2)}, u32[]{:S(2)}) %all-to-all-start) | async-done | bytes 688160 | tf_op jit(solution)/shard_map/all_to_all | solution.py:357
  70.5 3.7 %all-to-all-start.1 = ((bf16[4,3,32,896]{3,2,1,0:T(8,128)(2,1)}), bf16[4,3,32,896]{3,2,1,0:T(8,128)(2,1)S(1)}, u32[]{:S(2)}, u32[]{:S(2)}) async-start(bf16[4,3,32,896]{3,2,1,0:T(8,128)(2,1)} %activate.2), calls=%async_computation.1 | async-start | bytes 1376256 | tf_op jit(solution)/shard_map/all_to_all | solution.py:357
  74.2 6.4 %collective-permute-done.13.refs_1_ = bf16[3,96,896]{2,1,0:T(8,128)(2,1)S(1)} collective-permute-done((bf16[3,96,896]{2,1,0:T(8,128)(2,1)}, bf16[3,96,896]{2,1,0:T(8,128)(2,1)S(1)}, u32[]{:S(2)}, u32[]{:S(2)}) %collective-permute-start.13) | collective-permute-done | bytes 516128 | tf_op jit(solution)/shard_map/ppermute | solution.py:33
  85.3 2.6 %all-to-all-done.1.refs_0_ = bf16[4,3,32,896]{3,2,1,0:T(8,128)(2,1)S(1)} async-done(((bf16[4,3,32,896]{3,2,1,0:T(8,128)(2,1)}), bf16[4,3,32,896]{3,2,1,0:T(8,128)(2,1)S(1)}, u32[]{:S(2)}, u32[]{:S(2)}) %all-to-all-start.1) | async-done | bytes 688160 | tf_op jit(solution)/shard_map/all_to_all | solution.py:357
  89.5 3.6 %backward.2 = (bf16[2,2,32,1024]{3,2,1,0:T(8,128)(2,1)S(1)}, bf16[2,2,32,1024]{3,2,1,0:T(8,128)(2,1)S(1)}) custom-call(s32[1]{0:T(128)} %bitcast.where, bf16[3,128,896]{2,1,0:T(8,128)(2,1)S(1)} %assemble.2.trio.refs_5_, bf16[1024,896]{1,0:T(8,128)(2,1)S(1)} %copy-done.1, bf16[1024,896]{1,0:T(8,128)(2,1)S(1)} %copy-done.2, ...), custom_call_target="tpu_custom_call" | custom-call | flops 939524096 | bytes 8552448 | tf_op jit(solution)/shard_map/backward/pallas_call | solution.py:251
  93.1 4.1 %collective-permute-done.15.refs_1_ = bf16[3,96,896]{2,1,0:T(8,128)(2,1)S(1)} collective-permute-done((bf16[3,96,896]{2,1,0:T(8,128)(2,1)S(1)}, bf16[3,96,896]{2,1,0:T(8,128)(2,1)S(1)}, u32[]{:S(2)}, u32[]{:S(2)}) %collective-permute-start.15) | collective-permute-done | bytes 516128 | tf_op jit(solution)/shard_map/ppermute | solution.py:33
  102.1 3.6 %collective-permute-done.17.refs_3_ = bf16[3,48,896]{2,1,0:T(8,128)(2,1)S(1)} collective-permute-done((bf16[3,48,896]{2,1,0:T(8,128)(2,1)S(1)}, bf16[3,48,896]{2,1,0:T(8,128)(2,1)S(1)}, u32[]{:S(2)}, u32[]{:S(2)}) %collective-permute-start.17) | collective-permute-done | bytes 258080 | tf_op jit(solution)/shard_map/ppermute | solution.py:33
  107.7 4.1 %collective-permute-start.25 = (bf16[3,384,896]{2,1,0:T(8,128)(2,1)S(1)}, bf16[3,384,896]{2,1,0:T(8,128)(2,1)S(1)}, u32[]{:S(2)}, u32[]{:S(2)}) collective-permute-start(bf16[3,384,896]{2,1,0:T(8,128)(2,1)S(1)} %assemble.3.trio.refs_4_), channel_id=1, source_target_pairs={{16,0},{0,16},{48,32},{32,48},{80,64},{64,80},{112,96},{96,112},{2... | collective-permute-start | bytes 6193160 | tf_op jit(solution)/shard_map/ppermute | solution.py:33
  112.2 2.7 %collective-permute-start.21 = (bf16[2,2,32,1024]{3,2,1,0:T(8,128)(2,1)S(1)}, bf16[2,2,32,1024]{3,2,1,0:T(8,128)(2,1)S(1)}, u32[]{:S(2)}, u32[]{:S(2)}) collective-permute-start(bf16[2,2,32,1024]{3,2,1,0:T(8,128)(2,1)S(1)} %get-tuple-element.57), channel_id=1, source_target_pairs={{8,0},{18,16},{40,32},{50,48},{72,64},{82,80},{104,96},{114,112},{... | collective-permute-start | bytes 786440 | tf_op jit(solution)/shard_map/ppermute | solution.py:33
  114.9 4.5 %backward.3 = (bf16[4,2,32,1024]{3,2,1,0:T(8,128)(2,1)S(1)}, bf16[4,2,32,1024]{3,2,1,0:T(8,128)(2,1)S(1)}, bf16[4,2,32,1024]{3,2,1,0:T(8,128)(2,1)S(1)}) custom-call(s32[1]{0:T(128)} %bitcast.where, bf16[3,384,896]{2,1,0:T(8,128)(2,1)S(1)} %assemble.3.trio.refs_4_, bf16[1024,896]{1,0:T(8,128)(2,1)S(1)} %copy-done.1, bf16[1024,896]{1,0:T(8,128)(2,1)S(1)} %copy-done.3, ...), custom_call_target="tpu_custom_call" | custom-call | flops 2818572288 | bytes 10977280 | tf_op jit(solution)/shard_map/backward/pallas_call | solution.py:251
  120.6 2.9 %collective-permute-start.22 = (bf16[4,2,32,1024]{3,2,1,0:T(8,128)(2,1)S(1)}, bf16[4,2,32,1024]{3,2,1,0:T(8,128)(2,1)S(1)}, u32[]{:S(2)}, u32[]{:S(2)}) collective-permute-start(bf16[4,2,32,1024]{3,2,1,0:T(8,128)(2,1)S(1)} %pad_maximum_fusion.2), channel_id=1, source_target_pairs={{8,0},{18,16},{40,32},{50,48},{72,64},{82,80},{104,96},{114,112},{... | collective-permute-start | bytes 1572872 | tf_op jit(solution)/shard_map/ppermute | solution.py:33
  123.6 5.7 %weights.1 = (bf16[1024,896]{1,0:T(8,128)(2,1)}, bf16[1024,896]{1,0:T(8,128)(2,1)}) custom-call(bf16[2,384,1024]{2,1,0:T(8,128)(2,1)S(1)} %copy-done.4, bf16[2,128,1024]{2,1,0:T(8,128)(2,1)S(1)} %copy-done.5, bf16[2,384,1024]{2,1,0:T(8,128)(2,1)S(1)} %collective-permute-done.23.refs_2_, bf16[2,128,1024]{2,1,0:T(8,128)(2,1)S(1)} %collective-permute-done.24.refs_3_, ...), custom_call_target="tpu_custom_call" | custom-call | flops 3758096384 | bytes 9437184 | tf_op jit(solution)/shard_map/weights/pallas_call | solution.py:292
  134.1 3.9 %down_weights.1 = bf16[896,1024]{1,0:T(8,128)(2,1)} custom-call(bf16[2,384,1024]{2,1,0:T(8,128)(2,1)S(1)} %copy-done.4, bf16[2,128,1024]{2,1,0:T(8,128)(2,1)S(1)} %copy-done.5, bf16[2,384,1024]{2,1,0:T(8,128)(2,1)S(1)} %collective-permute-done.23.refs_2_, bf16[2,128,1024]{2,1,0:T(8,128)(2,1)S(1)} %collective-permute-done.24.refs_3_, ...), custom_call_target="tpu_custom_call" | custom-call | flops 1879048192 | bytes 5767168 | tf_op jit(solution)/shard_map/down_weights/pallas_call | solution.py:331
  138.5 3.8 %collective-permute-start.30 = (bf16[32,1024]{1,0:T(8,128)(2,1)S(1)}, bf16[32,1024]{1,0:T(8,128)(2,1)S(1)}, u32[]{:S(2)}, u32[]{:S(2)}) collective-permute-start(bf16[32,1024]{1,0:T(8,128)(2,1)S(1)} %slice_bitcast_fusion.4), channel_id=1, source_target_pairs={{16,0},{0,16},{48,32},{32,48},{80,64},{64,80},{112,96},{96,112},{2... | collective-permute-start | bytes 196616 | tf_op jit(solution)/shard_map/ppermute | solution.py:33
  (98 shorter events, 37.7 us)
Async XLA Ops:
  4.3 7.1 %collective-permute-start.3 = (bf16[2,2,32,1024]{3,2,1,0:T(8,128)(2,1)S(1)}, bf16[2,2,32,1024]{3,2,1,0:T(8,128)(2,1)S(1)}, u32[]{:S(2)}, u32[]{:S(2)}) collective-permute-start(bf16[2,2,32,1024]{3,2,1,0:T(8,128)(2,1)S(1)} %get-tuple-element.80), channel_id=1, source_target_pairs={{4,0},{17,16},{36,32},{49,48},{68,64},{81,80},{100,96},{113,112},{... | collective-permute-start | bytes 786440 | tf_op jit(solution)/shard_map/ppermute | solution.py:33
  14.8 21.6 %collective-permute-start.6 = (bf16[1024,896]{1,0:T(8,128)(2,1)S(1)}, bf16[1024,896]{1,0:T(8,128)(2,1)}, u32[]{:S(2)}, u32[]{:S(2)}) collective-permute-start(bf16[1024,896]{1,0:T(8,128)(2,1)S(1)} %copy-done), channel_id=1, source_target_pairs={{16,0},{0,16},{48,32},{32,48},{80,64},{64,80},{112,96},{96,112},{2... | collective-permute-start | bytes 5505032 | tf_op jit(solution)/shard_map/ppermute | solution.py:33
  15.8 20.6 %collective-permute-start.7 = (bf16[1024,896]{1,0:T(8,128)(2,1)}, bf16[1024,896]{1,0:T(8,128)(2,1)}, u32[]{:S(2)}, u32[]{:S(2)}) collective-permute-start(bf16[1024,896]{1,0:T(8,128)(2,1)} %refs_1_.3), channel_id=1, source_target_pairs={{16,0},{0,16},{48,32},{32,48},{80,64},{64,80},{112,96},{96,112},{2... | collective-permute-start | bytes 5505032 | tf_op jit(solution)/shard_map/ppermute | solution.py:33
  15.9 20.5 %collective-permute-start.8 = (bf16[896,1024]{1,0:T(8,128)(2,1)}, bf16[896,1024]{1,0:T(8,128)(2,1)}, u32[]{:S(2)}, u32[]{:S(2)}) collective-permute-start(bf16[896,1024]{1,0:T(8,128)(2,1)} %refs_4_.3), channel_id=1, source_target_pairs={{16,0},{0,16},{48,32},{32,48},{80,64},{64,80},{112,96},{96,112},{2... | collective-permute-start | bytes 5505032 | tf_op jit(solution)/shard_map/ppermute | solution.py:33
  16.3 14.5 %collective-permute-start.4 = (bf16[4,2,2,32,1024]{4,3,2,1,0:T(8,128)(2,1)S(1)}, bf16[4,2,2,32,1024]{4,3,2,1,0:T(8,128)(2,1)S(1)}, u32[]{:S(2)}, u32[]{:S(2)}) collective-permute-start(bf16[4,2,2,32,1024]{4,3,2,1,0:T(8,128)(2,1)S(1)} %pad_maximum_fusion.refs_0_), channel_id=1, source_target_pairs={{8,0},{18,16},{40,32},{50,48},{72,64},{82,80},{104,96},{114,112},{... | collective-permute-start | bytes 3145736 | tf_op jit(solution)/shard_map/ppermute | solution.py:33
  19.1 16.1 %collective-permute-start.5 = (bf16[4,2,2,32,1024]{4,3,2,1,0:T(8,128)(2,1)S(1)}, bf16[4,2,2,32,1024]{4,3,2,1,0:T(8,128)(2,1)S(1)}, u32[]{:S(2)}, u32[]{:S(2)}) collective-permute-start(bf16[4,2,2,32,1024]{4,3,2,1,0:T(8,128)(2,1)S(1)} %pad_maximum_fusion.refs_0_), channel_id=1, source_target_pairs={{9,0},{22,16},{41,32},{54,48},{73,64},{86,80},{105,96},{118,112},{... | collective-permute-start | bytes 3145736 | tf_op jit(solution)/shard_map/ppermute | solution.py:33
  31.8 17.6 %collective-permute-start.11 = (bf16[2,2,2,32,1024]{4,3,2,1,0:T(8,128)(2,1)}, bf16[2,2,2,32,1024]{4,3,2,1,0:T(8,128)(2,1)}, u32[]{:S(2)}, u32[]{:S(2)}) collective-permute-start(bf16[2,2,2,32,1024]{4,3,2,1,0:T(8,128)(2,1)} %slice.60), channel_id=1, source_target_pairs={{8,0},{18,16},{40,32},{50,48},{72,64},{82,80},{104,96},{114,112},{... | collective-permute-start | bytes 1572872 | tf_op jit(solution)/shard_map/ppermute | solution.py:33
  36.4 13.0 %collective-permute-start.12 = (bf16[2,2,2,32,1024]{4,3,2,1,0:T(8,128)(2,1)}, bf16[2,2,2,32,1024]{4,3,2,1,0:T(8,128)(2,1)}, u32[]{:S(2)}, u32[]{:S(2)}) collective-permute-start(bf16[2,2,2,32,1024]{4,3,2,1,0:T(8,128)(2,1)} %slice.61), channel_id=1, source_target_pairs={{9,0},{22,16},{41,32},{54,48},{73,64},{86,80},{105,96},{118,112},{... | collective-permute-start | bytes 1572872 | tf_op jit(solution)/shard_map/ppermute | solution.py:33
  45.5 14.5 %collective-permute-start.9 = (bf16[3,48,896]{2,1,0:T(8,128)(2,1)S(1)}, bf16[3,48,896]{2,1,0:T(8,128)(2,1)S(1)}, u32[]{:S(2)}, u32[]{:S(2)}) collective-permute-start(bf16[3,48,896]{2,1,0:T(8,128)(2,1)S(1)} %get-tuple-element.45), channel_id=1, source_target_pairs={{96,0},{112,16},{0,32},{16,48},{32,64},{48,80},{64,96},{80,112},{1... | collective-permute-start | bytes 774152 | tf_op jit(solution)/shard_map/ppermute | solution.py:33
  47.2 12.8 %collective-permute-start.10 = (bf16[3,48,896]{2,1,0:T(8,128)(2,1)S(1)}, bf16[3,48,896]{2,1,0:T(8,128)(2,1)S(1)}, u32[]{:S(2)}, u32[]{:S(2)}) collective-permute-start(bf16[3,48,896]{2,1,0:T(8,128)(2,1)S(1)} %get-tuple-element.46), channel_id=1, source_target_pairs={{32,0},{48,16},{64,32},{80,48},{96,64},{112,80},{0,96},{16,112},{4... | collective-permute-start | bytes 774152 | tf_op jit(solution)/shard_map/ppermute | solution.py:33
  56.5 13.0 %all-to-all-start = ((bf16[4,3,32,896]{3,2,1,0:T(8,128)(2,1)}), bf16[4,3,32,896]{3,2,1,0:T(8,128)(2,1)S(1)}, u32[]{:S(2)}, u32[]{:S(2)}) async-start(bf16[4,3,32,896]{3,2,1,0:T(8,128)(2,1)} %get-tuple-element.47), calls=%async_computation | async-start | bytes 1376256 | tf_op jit(solution)/shard_map/all_to_all | solution.py:357
  61.1 19.5 %collective-permute-start.13 = (bf16[3,96,896]{2,1,0:T(8,128)(2,1)}, bf16[3,96,896]{2,1,0:T(8,128)(2,1)S(1)}, u32[]{:S(2)}, u32[]{:S(2)}) collective-permute-start(bf16[3,96,896]{2,1,0:T(8,128)(2,1)} %get-tuple-element.50), channel_id=1, source_target_pairs={{96,0},{112,16},{0,32},{16,48},{32,64},{48,80},{64,96},{80,112},{1... | collective-permute-start | bytes 1548296 | tf_op jit(solution)/shard_map/ppermute | solution.py:33
  62.5 18.9 %collective-permute-start.14 = (bf16[3,96,896]{2,1,0:T(8,128)(2,1)}, bf16[3,96,896]{2,1,0:T(8,128)(2,1)}, u32[]{:S(2)}, u32[]{:S(2)}) collective-permute-start(bf16[3,96,896]{2,1,0:T(8,128)(2,1)} %get-tuple-element.51), channel_id=1, source_target_pairs={{32,0},{48,16},{64,32},{80,48},{96,64},{112,80},{0,96},{16,112},{4... | collective-permute-start | bytes 1548296 | tf_op jit(solution)/shard_map/ppermute | solution.py:33
  70.5 17.4 %all-to-all-start.1 = ((bf16[4,3,32,896]{3,2,1,0:T(8,128)(2,1)}), bf16[4,3,32,896]{3,2,1,0:T(8,128)(2,1)S(1)}, u32[]{:S(2)}, u32[]{:S(2)}) async-start(bf16[4,3,32,896]{3,2,1,0:T(8,128)(2,1)} %activate.2), calls=%async_computation.1 | async-start | bytes 1376256 | tf_op jit(solution)/shard_map/all_to_all | solution.py:357
  83.8 13.4 %collective-permute-start.15 = (bf16[3,96,896]{2,1,0:T(8,128)(2,1)S(1)}, bf16[3,96,896]{2,1,0:T(8,128)(2,1)S(1)}, u32[]{:S(2)}, u32[]{:S(2)}) collective-permute-start(bf16[3,96,896]{2,1,0:T(8,128)(2,1)S(1)} %activate.3.refs_0_), channel_id=1, source_target_pairs={{32,0},{48,16},{64,32},{80,48},{96,64},{112,80},{0,96},{16,112},{4... | collective-permute-start | bytes 1548296 | tf_op jit(solution)/shard_map/ppermute | solution.py:33
  84.5 13.7 %collective-permute-start.16 = (bf16[3,96,896]{2,1,0:T(8,128)(2,1)S(1)}, bf16[3,96,896]{2,1,0:T(8,128)(2,1)}, u32[]{:S(2)}, u32[]{:S(2)}) collective-permute-start(bf16[3,96,896]{2,1,0:T(8,128)(2,1)S(1)} %activate.3.refs_0_), channel_id=1, source_target_pairs={{96,0},{112,16},{0,32},{16,48},{32,64},{48,80},{64,96},{80,112},{1... | collective-permute-start | bytes 1548296 | tf_op jit(solution)/shard_map/ppermute | solution.py:33
  107.7 15.9 %collective-permute-start.25 = (bf16[3,384,896]{2,1,0:T(8,128)(2,1)S(1)}, bf16[3,384,896]{2,1,0:T(8,128)(2,1)S(1)}, u32[]{:S(2)}, u32[]{:S(2)}) collective-permute-start(bf16[3,384,896]{2,1,0:T(8,128)(2,1)S(1)} %assemble.3.trio.refs_4_), channel_id=1, source_target_pairs={{16,0},{0,16},{48,32},{32,48},{80,64},{64,80},{112,96},{96,112},{2... | collective-permute-start | bytes 6193160 | tf_op jit(solution)/shard_map/ppermute | solution.py:33
  111.7 11.9 %collective-permute-start.23 = (bf16[2,384,1024]{2,1,0:T(8,128)(2,1)S(1)}, bf16[2,384,1024]{2,1,0:T(8,128)(2,1)S(1)}, u32[]{:S(2)}, u32[]{:S(2)}) collective-permute-start(bf16[2,384,1024]{2,1,0:T(8,128)(2,1)S(1)} %copy-done.11), channel_id=1, source_target_pairs={{16,0},{0,16},{48,32},{32,48},{80,64},{64,80},{112,96},{96,112},{2... | collective-permute-start | bytes 4718600 | tf_op jit(solution)/shard_map/ppermute | solution.py:33
  111.8 8.8 %collective-permute-start.24 = (bf16[2,128,1024]{2,1,0:T(8,128)(2,1)S(1)}, bf16[2,128,1024]{2,1,0:T(8,128)(2,1)S(1)}, u32[]{:S(2)}, u32[]{:S(2)}) collective-permute-start(bf16[2,128,1024]{2,1,0:T(8,128)(2,1)S(1)} %copy-done.12), channel_id=1, source_target_pairs={{16,0},{0,16},{48,32},{32,48},{80,64},{64,80},{112,96},{96,112},{2... | collective-permute-start | bytes 1572872 | tf_op jit(solution)/shard_map/ppermute | solution.py:33
  112.2 7.2 %collective-permute-start.19 = (bf16[2,2,32,1024]{3,2,1,0:T(8,128)(2,1)S(1)}, bf16[2,2,32,1024]{3,2,1,0:T(8,128)(2,1)S(1)}, u32[]{:S(2)}, u32[]{:S(2)}) collective-permute-start(bf16[2,2,32,1024]{3,2,1,0:T(8,128)(2,1)S(1)} %get-tuple-element.56), channel_id=1, source_target_pairs={{9,0},{22,16},{41,32},{54,48},{73,64},{86,80},{105,96},{118,112},{... | collective-permute-start | bytes 786440 | tf_op jit(solution)/shard_map/ppermute | solution.py:33
  112.2 8.2 %collective-permute-start.21 = (bf16[2,2,32,1024]{3,2,1,0:T(8,128)(2,1)S(1)}, bf16[2,2,32,1024]{3,2,1,0:T(8,128)(2,1)S(1)}, u32[]{:S(2)}, u32[]{:S(2)}) collective-permute-start(bf16[2,2,32,1024]{3,2,1,0:T(8,128)(2,1)S(1)} %get-tuple-element.57), channel_id=1, source_target_pairs={{8,0},{18,16},{40,32},{50,48},{72,64},{82,80},{104,96},{114,112},{... | collective-permute-start | bytes 786440 | tf_op jit(solution)/shard_map/ppermute | solution.py:33
  120.4 9.6 %collective-permute-start.20 = (bf16[4,2,32,1024]{3,2,1,0:T(8,128)(2,1)S(1)}, bf16[4,2,32,1024]{3,2,1,0:T(8,128)(2,1)S(1)}, u32[]{:S(2)}, u32[]{:S(2)}) collective-permute-start(bf16[4,2,32,1024]{3,2,1,0:T(8,128)(2,1)S(1)} %pad_maximum_fusion.1), channel_id=1, source_target_pairs={{9,0},{22,16},{41,32},{54,48},{73,64},{86,80},{105,96},{118,112},{... | collective-permute-start | bytes 1572872 | tf_op jit(solution)/shard_map/ppermute | solution.py:33
  120.6 9.4 %collective-permute-start.22 = (bf16[4,2,32,1024]{3,2,1,0:T(8,128)(2,1)S(1)}, bf16[4,2,32,1024]{3,2,1,0:T(8,128)(2,1)S(1)}, u32[]{:S(2)}, u32[]{:S(2)}) collective-permute-start(bf16[4,2,32,1024]{3,2,1,0:T(8,128)(2,1)S(1)} %pad_maximum_fusion.2), channel_id=1, source_target_pairs={{8,0},{18,16},{40,32},{50,48},{72,64},{82,80},{104,96},{114,112},{... | collective-permute-start | bytes 1572872 | tf_op jit(solution)/shard_map/ppermute | solution.py:33
  130.4 7.7 %collective-permute-start.27 = (bf16[2,32,1024]{2,1,0:T(8,128)(2,1)S(1)}, bf16[2,32,1024]{2,1,0:T(8,128)(2,1)S(1)}, u32[]{:S(2)}, u32[]{:S(2)}) collective-permute-start(bf16[2,32,1024]{2,1,0:T(8,128)(2,1)S(1)} %get-tuple-element.78), channel_id=1, source_target_pairs={{6,0},{25,16},{38,32},{57,48},{70,64},{89,80},{102,96},{121,112},{... | collective-permute-start | bytes 393224 | tf_op jit(solution)/shard_map/ppermute | solution.py:33
  (22 other events, 133.1 us)

commit v3 on v2

--- a/solution.py
+++ b/solution.py
@@ -97,14 +97,15 @@
         copy.wait()
     copies = copies[total:]
     results = [pltpu.make_async_copy(rows.at[k], out, sems.at[k]) for k, out in enumerate((rows_mine, rows_other))]
-    for copy in results:
-        copy.start()
     for m in range(3):
         src = 0 if m < 2 else 1
         dims = (((1,), (0,)), ((), ())) if m < 2 else LANES
         copies[2 * m].wait()
+        v = lax.dot_general(rows[0, src], held[2 * m][...], dims, preferred_element_type=F32)
         copies[2 * m + 1].wait()
-        v = lax.dot_general(rows[0, src], held[2 * m][...], dims, preferred_element_type=F32)
+        if m == 2:
+            for copy in results:
+                copy.start()
         v = v + lax.dot_general(rows[1, src], held[2 * m + 1][...], dims, preferred_element_type=F32)
         v = v.astype(BF)
         for block in range(4):
@@ -196,73 +197,102 @@
     )(*parts)
 
 
-def assemble_kernel(n, *refs):
-    out = refs[n]
-    if n == 1:
-        t = refs[0].shape[2]
-        for k in range(4):
-            for m in range(3):
-                out[m, k * t:(k + 1) * t] = refs[0][k, m]
-        return
-    t = refs[0].shape[1]
-    for k in range(3):
-        out[:, k * t:(k + 1) * t] = refs[k][...]
-    out[:, 3 * t:3 * t + t // 2] = refs[3][...]
-    out[:, 3 * t + t // 2:] = refs[4][...]
-
-
-def assemble(*parts):
-    *_, t, f = parts[0].shape
-    return pl.pallas_call(
-        functools.partial(assemble_kernel, len(parts)),
-        out_shape=shape(3, 4 * t, f),
-        in_specs=vmem(len(parts)),
-        out_specs=vmem(1)[0],
-        compiler_params=params(12),
-        name="assemble",
-    )(*parts)
-
-
-def backward_kernel(counts, ring, where, trio, *refs):
-    mine, other = refs[:2], refs[2:4]
-    outs, (res, held, sems) = refs[4:-3], refs[-3:]
-    copies = [pltpu.make_async_copy(w, held.at[k], sems.at[k]) for k, w in enumerate((*mine, *other))]
-    for copy in copies:
-        copy.start()
-    per = sum(counts) // 4
+def gradient_terms(trio, rows, held, copies, res):
     for b in range(2):
         copies[2 * b].wait()
         v = lax.dot_general(trio[1], held[2 * b], LANES, preferred_element_type=F32)
         copies[2 * b + 1].wait()
         v = v + lax.dot_general(trio[2], held[2 * b + 1], LANES, preferred_element_type=F32)
-        res[b] = v.astype(BF)
+        res[b, rows] = v.astype(BF)
+
+
+def start_all(sources, targets, sems):
+    copies = [pltpu.make_async_copy(a, targets.at[k], sems.at[k]) for k, a in enumerate(sources)]
+    for copy in copies:
+        copy.start()
+    return copies
+
+
+def hand_out(counts, place, res, outs):
     i = 0
     for ref, count in zip(outs, counts):
         for j in range(count):
-            row = place_of(i, per, where[0] if ring else None)
+            row = place(i)
             for b in range(2):
                 ref[j, b] = res[b, pl.ds(row, PIECE), :]
             i += 1
 
 
-def backward(where, trio, mine, other, counts, ring):
-    _, tokens, f = trio.shape
-    d = mine[0].shape[0]
-    return pl.pallas_call(
-        functools.partial(backward_kernel, counts, ring),
-        out_shape=tuple(shape(n, 2, PIECE, d) for n in counts),
-        in_specs=[SMEM] + vmem(1) + [pl.BlockSpec(memory_space=pltpu.HBM)] * 4,
-        out_specs=tuple(vmem(len(counts))),
-        scratch_shapes=[pltpu.VMEM((2, tokens, d), BF), pltpu.VMEM((4, d, f), BF), pltpu.SemaphoreType.DMA((4,))],
-        compiler_params=params(12 + 14 * tokens // 512),
-        cost_estimate=pl.CostEstimate(flops=8 * tokens * d * f, bytes_accessed=8 * d * f + tokens * (6 * f + 4 * d), transcendentals=0),
-        name="backward",
-    )(where, trio, *mine[:2], *other[:2])
-
-
-def weights_kernel(n, *refs):
-    rows, trios = refs[:n], refs[n:2 * n]
-    o_gate, o_up, x, both = refs[2 * n:]
+def backward_kernel(counts, parts, *refs):
+    copies = start_all(refs[:4], refs[-2], refs[-1])
+    trio, outs, res = refs[4], refs[5:-3], refs[-3]
+    t = parts.shape[2]
+    for k in range(4):
+        for m in range(3):
+            trio[m, k * t:(k + 1) * t] = parts[k, m]
+    gradient_terms(trio, slice(0, 4 * t), refs[-2], copies, res)
+    hand_out(counts, lambda i: i * PIECE, res, outs)
+
+
+def early_kernel(own, up, down, *refs):
+    copies = start_all(refs[:4], refs[-2], refs[-1])
+    trio, res = refs[4:6]
+    t = own.shape[1]
+    for k, ref in enumerate((own, up, down)):
+        trio[:, k * t:(k + 1) * t] = ref[...]
+    gradient_terms(trio, slice(0, 3 * t), refs[-2], copies, res)
+
+
+def late_kernel(counts, where, f0, f1, early, *refs):
+    copies = start_all(refs[:4], refs[-2], refs[-1])
+    trio, outs, res = refs[4], refs[5:-3], refs[-3]
+    t = 2 * f0.shape[1]
+    trio[:, : t // 2] = f0[...]
+    trio[:, t // 2:] = f1[...]
+    res[:, : 3 * t] = early[...]
+    gradient_terms(trio, slice(3 * t, 4 * t), refs[-2], copies, res)
+    hand_out(counts, lambda i: place_of(i, sum(counts) // 4, where[0]), res, outs)
+
+
+def backward_call(kernel, name, smem, inputs, mine, other, rows, outs, scratch=()):
+    d, f = mine[0].shape
+    return pl.pallas_call(
+        kernel,
+        out_shape=outs,
+        in_specs=[SMEM] * len(smem) + vmem(len(inputs)) + [pl.BlockSpec(memory_space=pltpu.HBM)] * 4,
+        out_specs=tuple(vmem(len(outs))),
+        scratch_shapes=[*scratch, pltpu.VMEM((4, d, f), BF), pltpu.SemaphoreType.DMA((4,))],
+        compiler_params=params(28),
+        cost_estimate=pl.CostEstimate(flops=8 * rows * d * f, bytes_accessed=8 * d * f + rows * (6 * f + 4 * d), transcendentals=0),
+        name=name,
+    )(*smem, *inputs, *mine[:2], *other[:2])
+
+
+def backward(parts, mine, other, counts):
+    d, f = mine[0].shape
+    rows = sum(counts) * PIECE
+    outs = shape(3, rows, f), *(shape(n, 2, PIECE, d) for n in counts)
+    kernel = functools.partial(backward_kernel, counts)
+    return backward_call(kernel, "backward", (), (parts,), mine, other, rows, outs, (pltpu.VMEM((2, rows, d), BF),))
+
+
+def backward_early(own, up, down, mine, other):
+    d, f = mine[0].shape
+    rows = 3 * own.shape[1]
+    return backward_call(early_kernel, "backward_early", (), (own, up, down), mine, other, rows, (shape(3, rows, f), shape(2, rows, d)))
+
+
+def backward_late(where, f0, f1, early, mine, other, counts):
+    d, f = mine[0].shape
+    t = 2 * f0.shape[1]
+    outs = shape(3, t, f), *(shape(n, 2, PIECE, d) for n in counts)
+    kernel = functools.partial(late_kernel, counts)
+    return backward_call(kernel, "backward_late", (where,), (f0, f1, early), mine, other, t, outs, (pltpu.VMEM((2, 4 * t, d), BF),))
+
+
+def weights_kernel(n, m, *refs):
+    rows, trios = refs[:n], refs[n:n + m]
+    o_gate, o_up, x, both = refs[n + m:]
     f = o_gate.shape[1]
 
     @pl.when(pl.program_id(0) == 0)
@@ -290,7 +320,7 @@
     tokens = sum(t.shape[1] for t in trios)
     w = 512
     return pl.pallas_call(
-        functools.partial(weights_kernel, n),
+        functools.partial(weights_kernel, n, len(trios)),
         grid=(d // w,),
         out_shape=(shape(d, f), shape(d, f)),
         in_specs=[pl.BlockSpec((1, r.shape[1], w), lambda i: (0, 0, i)) for r in rows]
@@ -303,9 +333,9 @@
     )(*rows, *trios)
 
 
-def down_kernel(n, *refs):
-    rows, trios = refs[:n], refs[n:2 * n]
-    o_down, y, turned = refs[2 * n:]
+def down_kernel(n, m, *refs):
+    rows, trios = refs[:n], refs[n:n + m]
+    o_down, y, turned = refs[n + m:]
 
     @pl.when(pl.program_id(0) == 0)
     def _():
@@ -329,7 +359,7 @@
     tokens = sum(t.shape[1] for t in trios)
     w = 512
     return pl.pallas_call(
-        functools.partial(down_kernel, n),
+        functools.partial(down_kernel, n, len(trios)),
         grid=(d // w,),
         out_shape=shape(f, d),
         in_specs=[pl.BlockSpec((1, r.shape[1], w), lambda i: (1, 0, i)) for r in rows]
@@ -386,22 +416,22 @@
     trio = activate(b0, q1, q2)
     t = trio.shape[1]
     up, down = from_z(trio, 1), from_z(trio, -1)
-    trio_far = assemble(to_all_z(trio_far))
-    trio_far_got = from_core(trio_far)
-    up, down = after((up, down), trio_far)
-    far0, far1 = backward(where, trio_far, mine, other, (2, 2), False)
+    trio_far, far0, far1 = backward(to_all_z(trio_far), mine, other, (2, 2))
     up, down = after((up, down), (far0, far1))
     far0, far1 = from_side(far0, -1), from_side(far1, 1)
-    trio = assemble(trio, up, down, from_z(down[:, : t // 2], -1), from_z(up[:, t // 2:], 1))
-    trio_got = from_core(trio)
-    line, ahead, behind = backward(where, trio, mine, other, (4, 4, 4), True)
+    f0, f1 = from_z(down[:, : t // 2], -1), from_z(up[:, t // 2:], 1)
+    trio_early, early = backward_early(trio, up, down, mine, other)
+    f0, f1 = after((f0, f1), (far0, far1, early))
+    trio_far_got, trio_early_got = (from_core(v) for v in after((trio_far, trio_early), f0))
+    trio_late, line, ahead, behind = backward_late(where, f0, f1, early, mine, other, (4, 4, 4))
+    trio_late_got = from_core(trio_late)
 
     ahead = jnp.concatenate([plus(ahead[:2], far0).astype(BF), ahead[2:]])
     behind = jnp.concatenate([behind[:2], plus(behind[2:], far1).astype(BF)])
     ahead, behind = from_side(ahead, -1), from_side(behind, 1)
 
     rows = near_mine, far_mine, near_got, far_got
-    trios = trio, trio_far, trio_got, trio_far_got
+    trios = trio_early, trio_late, trio_far, trio_early_got, trio_late_got, trio_far_got
     gate_up = weights(rows, trios)
     ahead, behind = after((ahead, behind), gate_up)
 

time: 144 us -> 139 us (0.965)
  waiting for transfers between devices: 43.5 us -> 36.3 us
  Pallas kernels: 38.6 us -> 41.4 us
    ppermute x31 -> x32, waiting for transfers between devices: 35.2 us -> 28 us  [from_where(): return lax.ppermute(value, ALL, pairs)]
    pallas_call x6 -> x5, Pallas kernels: 19 us -> 22.2 us  [the longest x3 12.2 us: backward_call(): pl.pallas_call(kernel, out_shape=outs, in_specs=[SMEM] * len(smem) + vmem...]
    ppermute x31 -> x32, starting transfers between devices: 44.6 us -> 43.7 us  [from_where(): return lax.ppermute(value, ALL, pairs)]
  transfers between devices with their start and end apart: 33 -> 34, of which waited for: 15 -> 12; matrix products, arithmetic and copies ran while one was open for 1% -> 2% of each run, Pallas kernels for 26% -> 30%
where the time goes in v3:
time: 139 us
  starting transfers between devices  50.8 us (37%)
  Pallas kernels  41.4 us (30%)
  waiting for transfers between devices  36.3 us (26%)
  local copies, waits for them, and re-layouts  6.59 us (5%)
  other arithmetic  2.52 us (2%)
    ppermute x32, starting transfers between devices, from_where(): return lax.ppermute(value, ALL, pairs)  43.7 us
    ppermute x32, waiting for transfers between devices, from_where(): return lax.ppermute(value, ALL, pairs)  28 us
    pallas_call x2, Pallas kernels, forward(): pl.pallas_call(functools.partial(forward_kernel, counts, ring), out_shape...  15.8 us
    pallas_call x3, Pallas kernels, backward_call(): pl.pallas_call(kernel, out_shape=outs, in_specs=[SMEM] * len(smem) + vmem...  12.2 us
    all_to_all x2, waiting for transfers between devices, to_all_z(): lax.all_to_all(value, 'inp', 0, 0, axis_index_groups=[[0, 2, 4, 6], [1, 3...  8.29 us
    all_to_all x2, starting transfers between devices, to_all_z(): lax.all_to_all(value, 'inp', 0, 0, axis_index_groups=[[0, 2, 4, 6], [1, 3...  7.12 us
    pallas_call x1, Pallas kernels, weights(): pl.pallas_call(functools.partial(weights_kernel, n, len(trios)), grid=(d...  5.66 us
    pallas_call x1, Pallas kernels, down_weights(): pl.pallas_call(functools.partial(down_kernel, n, len(trios)), grid=(d //...  4.31 us
  transfers between devices with their start and end apart: 34, of which 12 were waited for; matrix products, arithmetic and copies ran while one was open for 2% of the time, Pallas kernels for 30%

profile of v3, /device:TPU:1, one launch (start us, length us, event | category | flops | bytes accessed | tf_op | source)
XLA Modules:
  0.0 138.6 jit_solution(469089245246744676)
XLA Ops:
  4.3 3.1 %collective-permute-start.3 = (bf16[2,2,32,1024]{3,2,1,0:T(8,128)(2,1)S(1)}, bf16[2,2,32,1024]{3,2,1,0:T(8,128)(2,1)S(1)}, u32[]{:S(2)}, u32[]{:S(2)}) collective-permute-start(bf16[2,2,32,1024]{3,2,1,0:T(8,128)(2,1)S(1)} %get-tuple-element.92), channel_id=1, source_target_pairs={{4,0},{17,16},{36,32},{49,48},{68,64},{81,80},{100,96},{113,112},{... | collective-permute-start | bytes 786440 | tf_op jit(solution)/shard_map/ppermute | solution.py:33
  7.8 2.3 %collective-permute-start.1 = (bf16[2,2,32,1024]{3,2,1,0:T(8,128)(2,1)S(1)}, bf16[2,2,32,1024]{3,2,1,0:T(8,128)(2,1)S(1)}, u32[]{:S(2)}, u32[]{:S(2)}) collective-permute-start(bf16[2,2,32,1024]{3,2,1,0:T(8,128)(2,1)S(1)} %get-tuple-element.92), channel_id=1, source_target_pairs={{2,0},{24,16},{34,32},{56,48},{66,64},{88,80},{98,96},{120,112},{1... | collective-permute-start | bytes 786440 | tf_op jit(solution)/shard_map/ppermute | solution.py:33
  11.4 2.8 %collective-permute-done.2 = bf16[2,2,32,1024]{3,2,1,0:T(8,128)(2,1)S(1)} collective-permute-done((bf16[2,2,32,1024]{3,2,1,0:T(8,128)(2,1)S(1)}, bf16[2,2,32,1024]{3,2,1,0:T(8,128)(2,1)S(1)}, u32[]{:S(2)}, u32[]{:S(2)}) %collective-permute-start.2) | collective-permute-done | bytes 262176 | tf_op jit(solution)/shard_map/ppermute | solution.py:33
  16.3 2.8 %collective-permute-start.4 = (bf16[4,2,2,32,1024]{4,3,2,1,0:T(8,128)(2,1)S(1)}, bf16[4,2,2,32,1024]{4,3,2,1,0:T(8,128)(2,1)S(1)}, u32[]{:S(2)}, u32[]{:S(2)}) collective-permute-start(bf16[4,2,2,32,1024]{4,3,2,1,0:T(8,128)(2,1)S(1)} %pad_maximum_fusion.refs_0_), channel_id=1, source_target_pairs={{8,0},{18,16},{40,32},{50,48},{72,64},{82,80},{104,96},{114,112},{... | collective-permute-start | bytes 3145736 | tf_op jit(solution)/shard_map/ppermute | solution.py:33
  19.1 11.7 %collective-permute-done.4.refs_1_ = bf16[4,2,2,32,1024]{4,3,2,1,0:T(8,128)(2,1)S(1)} collective-permute-done((bf16[4,2,2,32,1024]{4,3,2,1,0:T(8,128)(2,1)S(1)}, bf16[4,2,2,32,1024]{4,3,2,1,0:T(8,128)(2,1)S(1)}, u32[]{:S(2)}, u32[]{:S(2)}) %collective-permute-start.4) | collective-permute-done | bytes 1048608 | tf_op jit(solution)/shard_map/ppermute | solution.py:33
  31.8 3.4 %collective-permute-start.11 = (bf16[2,2,2,32,1024]{4,3,2,1,0:T(8,128)(2,1)}, bf16[2,2,2,32,1024]{4,3,2,1,0:T(8,128)(2,1)}, u32[]{:S(2)}, u32[]{:S(2)}) collective-permute-start(bf16[2,2,2,32,1024]{4,3,2,1,0:T(8,128)(2,1)} %slice.60), channel_id=1, source_target_pairs={{8,0},{18,16},{40,32},{50,48},{72,64},{82,80},{104,96},{114,112},{... | collective-permute-start | bytes 1572872 | tf_op jit(solution)/shard_map/ppermute | solution.py:33
  36.4 9.1 %forward.2 = (bf16[2,384,1024]{2,1,0:T(8,128)(2,1)}, bf16[2,384,1024]{2,1,0:T(8,128)(2,1)}, bf16[3,96,896]{2,1,0:T(8,128)(2,1)S(1)}, bf16[3,96,896]{2,1,0:T(8,12...) custom-call(s32[1]{0:T(128)} %bitcast.where, ...), custom_call_target="tpu_custom_call" | custom-call | flops 4227858432 | bytes 17301504 | tf_op jit(solution)/shard_map/forward/pallas_call | solution.py:132
  47.2 2.2 %collective-permute-start.10 = (bf16[3,48,896]{2,1,0:T(8,128)(2,1)S(1)}, bf16[3,48,896]{2,1,0:T(8,128)(2,1)S(1)}, u32[]{:S(2)}, u32[]{:S(2)}) collective-permute-start(bf16[3,48,896]{2,1,0:T(8,128)(2,1)S(1)} %get-tuple-element.52), channel_id=1, source_target_pairs={{32,0},{48,16},{64,32},{80,48},{96,64},{112,80},{0,96},{16,112},{4... | collective-permute-start | bytes 774152 | tf_op jit(solution)/shard_map/ppermute | solution.py:33
  49.5 6.7 %forward.3 = (bf16[2,128,1024]{2,1,0:T(8,128)(2,1)}, bf16[2,128,1024]{2,1,0:T(8,128)(2,1)}, bf16[4,3,32,896]{3,2,1,0:T(8,128)(2,1)}) custom-call(s32[1]{0:T(128)} %bitcast.where, bf16[2,2,2,32,1024]{4,3,2,1,0:T(8,128)(2,1)} %collective-permute-done.11.refs_0_, bf16[2,2,2,32,1024]{4,3,2,1,0:T(8,128)(2,1)} %collective-permute-done.12.refs_1_, ...), custom_call_target="tpu_custom_call" | custom-call | flops 1409286144 | bytes 13107200 | tf_op jit(solution)/shard_map/forward/pallas_call | solution.py:132
  56.2 3.5 %all-to-all-start = ((bf16[4,3,32,896]{3,2,1,0:T(8,128)(2,1)}), bf16[4,3,32,896]{3,2,1,0:T(8,128)(2,1)S(1)}, u32[]{:S(2)}, u32[]{:S(2)}) async-start(bf16[4,3,32,896]{3,2,1,0:T(8,128)(2,1)} %get-tuple-element.53), calls=%async_computation | async-start | bytes 1376256 | tf_op jit(solution)/shard_map/all_to_all | solution.py:387
  63.4 5.7 %all-to-all-done.refs_0_ = bf16[4,3,32,896]{3,2,1,0:T(8,128)(2,1)S(1)} async-done(((bf16[4,3,32,896]{3,2,1,0:T(8,128)(2,1)}), bf16[4,3,32,896]{3,2,1,0:T(8,128)(2,1)S(1)}, u32[]{:S(2)}, u32[]{:S(2)}) %all-to-all-start) | async-done | bytes 688160 | tf_op jit(solution)/shard_map/all_to_all | solution.py:387
  70.2 3.6 %all-to-all-start.1 = ((bf16[4,3,32,896]{3,2,1,0:T(8,128)(2,1)}), bf16[4,3,32,896]{3,2,1,0:T(8,128)(2,1)S(1)}, u32[]{:S(2)}, u32[]{:S(2)}) async-start(bf16[4,3,32,896]{3,2,1,0:T(8,128)(2,1)} %activate.2), calls=%async_computation.1 | async-start | bytes 1376256 | tf_op jit(solution)/shard_map/all_to_all | solution.py:387
  73.8 6.4 %collective-permute-done.13.refs_1_ = bf16[3,96,896]{2,1,0:T(8,128)(2,1)S(1)} collective-permute-done((bf16[3,96,896]{2,1,0:T(8,128)(2,1)}, bf16[3,96,896]{2,1,0:T(8,128)(2,1)S(1)}, u32[]{:S(2)}, u32[]{:S(2)}) %collective-permute-start.13) | collective-permute-done | bytes 516128 | tf_op jit(solution)/shard_map/ppermute | solution.py:33
  85.0 2.6 %all-to-all-done.1.parts = bf16[4,3,32,896]{3,2,1,0:T(8,128)(2,1)S(1)} async-done(((bf16[4,3,32,896]{3,2,1,0:T(8,128)(2,1)}), bf16[4,3,32,896]{3,2,1,0:T(8,128)(2,1)S(1)}, u32[]{:S(2)}, u32[]{:S(2)}) %all-to-all-start.1) | async-done | bytes 688160 | tf_op jit(solution)/shard_map/all_to_all | solution.py:387
  89.1 3.8 %backward.1 = (bf16[3,128,896]{2,1,0:T(8,128)(2,1)S(1)}, bf16[2,2,32,1024]{3,2,1,0:T(8,128)(2,1)S(1)}, bf16[2,2,32,1024]{3,2,1,0:T(8,128)(2,1)S(1)}) custom-call(bf16[4,3,32,896]{3,2,1,0:T(8,128)(2,1)S(1)} %all-to-all-done.1.parts, bf16[1024,896]{1,0:T(8,128)(2,1)S(1)} %copy-done.1, bf16[1024,896]{1,0:T(8,128)(2,1)S(1)} %copy-done.2, ...), custom_call_target="tpu_custom_call" | custom-call | flops 939524096 | bytes 8552448 | tf_op jit(solution)/shard_map/backward/pallas_call | solution.py:259
  93.0 2.7 %collective-permute-start.20 = (bf16[2,2,32,1024]{3,2,1,0:T(8,128)(2,1)S(1)}, bf16[2,2,32,1024]{3,2,1,0:T(8,128)(2,1)S(1)}, u32[]{:S(2)}, u32[]{:S(2)}) collective-permute-start(bf16[2,2,32,1024]{3,2,1,0:T(8,128)(2,1)S(1)} %get-tuple-element.61), channel_id=1, source_target_pairs={{8,0},{18,16},{40,32},{50,48},{72,64},{82,80},{104,96},{114,112},{... | collective-permute-start | bytes 786440 | tf_op jit(solution)/shard_map/ppermute | solution.py:33
  101.8 4.2 %collective-permute-start.23 = (bf16[2,384,1024]{2,1,0:T(8,128)(2,1)S(1)}, bf16[2,384,1024]{2,1,0:T(8,128)(2,1)S(1)}, u32[]{:S(2)}, u32[]{:S(2)}) collective-permute-start(bf16[2,384,1024]{2,1,0:T(8,128)(2,1)S(1)} %copy-done.11), channel_id=1, source_target_pairs={{16,0},{0,16},{48,32},{32,48},{80,64},{64,80},{112,96},{96,112},{2... | collective-permute-start | bytes 4718600 | tf_op jit(solution)/shard_map/ppermute | solution.py:33
  105.9 4.8 %backward_early.1 = (bf16[3,288,896]{2,1,0:T(8,128)(2,1)S(1)}, bf16[2,288,1024]{2,1,0:T(8,128)(2,1)S(1)}) custom-call(bf16[3,96,896]{2,1,0:T(8,128)(2,1)S(1)} %activate.3.own, bf16[3,96,896]{2,1,0:T(8,128)(2,1)S(1)} %collective-permute-done.15.up, bf16[3,96,896]{2,1,0:T(8,128)(2,1)} %collective-permute-done.16.down, bf16[1024,896]{1,0:T(8,128)(2,1)S(1)} %copy-done.1, ...), custom_call_target="tpu_custom_call" | custom-call | flops 2113929216 | bytes 10067968 | tf_op jit(solution)/shard_map/backward_early/pallas_call | solution.py:259
  111.4 3.6 %backward_late.1 = (bf16[3,96,896]{2,1,0:T(8,128)(2,1)S(1)}, bf16[4,2,32,1024]{3,2,1,0:T(8,128)(2,1)S(1)}, bf16[4,2,32,1024]{3,2,1,0:T(8,128)(2,1)S(1)}, bf16[4,2,32,1024]{3,2,1,0:T(8,128)(2,1)S(1)}) custom-call(s32[1]{0:T(128)} %bitcast.where, bf16[3,48,896]{2,1,0:T(8,128)(2,1)S(1)} %collective-permute-done.17.f0, ...), custom_call_target="tpu_custom_call" | custom-call | flops 704643072 | bytes 8249344 | tf_op jit(solution)/shard_map/backward_late/pallas_call | solution.py:259
  116.0 2.8 %collective-permute-start.22 = (bf16[4,2,32,1024]{3,2,1,0:T(8,128)(2,1)S(1)}, bf16[4,2,32,1024]{3,2,1,0:T(8,128)(2,1)S(1)}, u32[]{:S(2)}, u32[]{:S(2)}) collective-permute-start(bf16[4,2,32,1024]{3,2,1,0:T(8,128)(2,1)S(1)} %pad_maximum_fusion.2), channel_id=1, source_target_pairs={{8,0},{18,16},{40,32},{50,48},{72,64},{82,80},{104,96},{114,112},{... | collective-permute-start | bytes 1572872 | tf_op jit(solution)/shard_map/ppermute | solution.py:33
  118.9 5.7 %weights.1 = (bf16[1024,896]{1,0:T(8,128)(2,1)}, bf16[1024,896]{1,0:T(8,128)(2,1)}) custom-call(bf16[2,384,1024]{2,1,0:T(8,128)(2,1)S(1)} %copy-done.4, bf16[2,128,1024]{2,1,0:T(8,128)(2,1)S(1)} %copy-done.5, bf16[2,384,1024]{2,1,0:T(8,128)(2,1)S(1)} %collective-permute-done.23.refs_2_, bf16[2,128,1024]{2,1,0:T(8,128)(2,1)S(1)} %collective-permute-done.24.refs_3_, ...), custom_call_target="tpu_custom_call" | custom-call | flops 3758096384 | bytes 9437184 | tf_op jit(solution)/shard_map/weights/pallas_call | solution.py:322
  126.7 2.0 %collective-permute-start.29 = (bf16[2,32,1024]{2,1,0:T(8,128)(2,1)S(1)}, bf16[2,32,1024]{2,1,0:T(8,128)(2,1)S(1)}, u32[]{:S(2)}, u32[]{:S(2)}) collective-permute-start(bf16[2,32,1024]{2,1,0:T(8,128)(2,1)S(1)} %get-tuple-element.89), channel_id=1, source_target_pairs={{2,0},{24,16},{34,32},{56,48},{66,64},{88,80},{98,96},{120,112},{1... | collective-permute-start | bytes 393224 | tf_op jit(solution)/shard_map/ppermute | solution.py:33
  129.9 4.3 %down_weights.1 = bf16[896,1024]{1,0:T(8,128)(2,1)} custom-call(bf16[2,384,1024]{2,1,0:T(8,128)(2,1)S(1)} %copy-done.4, bf16[2,128,1024]{2,1,0:T(8,128)(2,1)S(1)} %copy-done.5, bf16[2,384,1024]{2,1,0:T(8,128)(2,1)S(1)} %collective-permute-done.23.refs_2_, bf16[2,128,1024]{2,1,0:T(8,128)(2,1)S(1)} %collective-permute-done.24.refs_3_, ...), custom_call_target="tpu_custom_call" | custom-call | flops 1879048192 | bytes 5767168 | tf_op jit(solution)/shard_map/down_weights/pallas_call | solution.py:361
  134.3 2.7 %collective-permute-start.31 = (bf16[32,1024]{1,0:T(8,128)(2,1)S(1)}, bf16[32,1024]{1,0:T(8,128)(2,1)S(1)}, u32[]{:S(2)}, u32[]{:S(2)}) collective-permute-start(bf16[32,1024]{1,0:T(8,128)(2,1)S(1)} %slice_bitcast_fusion.4), channel_id=1, source_target_pairs={{16,0},{0,16},{48,32},{32,48},{80,64},{64,80},{112,96},{96,112},{2... | collective-permute-start | bytes 196616 | tf_op jit(solution)/shard_map/ppermute | solution.py:33
  (99 shorter events, 35.1 us)
Async XLA Ops:
  14.8 21.6 %collective-permute-start.6 = (bf16[1024,896]{1,0:T(8,128)(2,1)S(1)}, bf16[1024,896]{1,0:T(8,128)(2,1)}, u32[]{:S(2)}, u32[]{:S(2)}) collective-permute-start(bf16[1024,896]{1,0:T(8,128)(2,1)S(1)} %copy-done), channel_id=1, source_target_pairs={{16,0},{0,16},{48,32},{32,48},{80,64},{64,80},{112,96},{96,112},{2... | collective-permute-start | bytes 5505032 | tf_op jit(solution)/shard_map/ppermute | solution.py:33
  15.8 20.6 %collective-permute-start.7 = (bf16[1024,896]{1,0:T(8,128)(2,1)}, bf16[1024,896]{1,0:T(8,128)(2,1)}, u32[]{:S(2)}, u32[]{:S(2)}) collective-permute-start(bf16[1024,896]{1,0:T(8,128)(2,1)} %refs_1_.5), channel_id=1, source_target_pairs={{16,0},{0,16},{48,32},{32,48},{80,64},{64,80},{112,96},{96,112},{2... | collective-permute-start | bytes 5505032 | tf_op jit(solution)/shard_map/ppermute | solution.py:33
  15.9 20.5 %collective-permute-start.8 = (bf16[896,1024]{1,0:T(8,128)(2,1)}, bf16[896,1024]{1,0:T(8,128)(2,1)}, u32[]{:S(2)}, u32[]{:S(2)}) collective-permute-start(bf16[896,1024]{1,0:T(8,128)(2,1)} %refs_4_.3), channel_id=1, source_target_pairs={{16,0},{0,16},{48,32},{32,48},{80,64},{64,80},{112,96},{96,112},{2... | collective-permute-start | bytes 5505032 | tf_op jit(solution)/shard_map/ppermute | solution.py:33
  16.3 14.5 %collective-permute-start.4 = (bf16[4,2,2,32,1024]{4,3,2,1,0:T(8,128)(2,1)S(1)}, bf16[4,2,2,32,1024]{4,3,2,1,0:T(8,128)(2,1)S(1)}, u32[]{:S(2)}, u32[]{:S(2)}) collective-permute-start(bf16[4,2,2,32,1024]{4,3,2,1,0:T(8,128)(2,1)S(1)} %pad_maximum_fusion.refs_0_), channel_id=1, source_target_pairs={{8,0},{18,16},{40,32},{50,48},{72,64},{82,80},{104,96},{114,112},{... | collective-permute-start | bytes 3145736 | tf_op jit(solution)/shard_map/ppermute | solution.py:33
  19.1 16.1 %collective-permute-start.5 = (bf16[4,2,2,32,1024]{4,3,2,1,0:T(8,128)(2,1)S(1)}, bf16[4,2,2,32,1024]{4,3,2,1,0:T(8,128)(2,1)S(1)}, u32[]{:S(2)}, u32[]{:S(2)}) collective-permute-start(bf16[4,2,2,32,1024]{4,3,2,1,0:T(8,128)(2,1)S(1)} %pad_maximum_fusion.refs_0_), channel_id=1, source_target_pairs={{9,0},{22,16},{41,32},{54,48},{73,64},{86,80},{105,96},{118,112},{... | collective-permute-start | bytes 3145736 | tf_op jit(solution)/shard_map/ppermute | solution.py:33
  31.8 17.6 %collective-permute-start.11 = (bf16[2,2,2,32,1024]{4,3,2,1,0:T(8,128)(2,1)}, bf16[2,2,2,32,1024]{4,3,2,1,0:T(8,128)(2,1)}, u32[]{:S(2)}, u32[]{:S(2)}) collective-permute-start(bf16[2,2,2,32,1024]{4,3,2,1,0:T(8,128)(2,1)} %slice.60), channel_id=1, source_target_pairs={{8,0},{18,16},{40,32},{50,48},{72,64},{82,80},{104,96},{114,112},{... | collective-permute-start | bytes 1572872 | tf_op jit(solution)/shard_map/ppermute | solution.py:33
  36.4 13.0 %collective-permute-start.12 = (bf16[2,2,2,32,1024]{4,3,2,1,0:T(8,128)(2,1)}, bf16[2,2,2,32,1024]{4,3,2,1,0:T(8,128)(2,1)}, u32[]{:S(2)}, u32[]{:S(2)}) collective-permute-start(bf16[2,2,2,32,1024]{4,3,2,1,0:T(8,128)(2,1)} %slice.61), channel_id=1, source_target_pairs={{9,0},{22,16},{41,32},{54,48},{73,64},{86,80},{105,96},{118,112},{... | collective-permute-start | bytes 1572872 | tf_op jit(solution)/shard_map/ppermute | solution.py:33
  45.5 14.1 %collective-permute-start.9 = (bf16[3,48,896]{2,1,0:T(8,128)(2,1)S(1)}, bf16[3,48,896]{2,1,0:T(8,128)(2,1)S(1)}, u32[]{:S(2)}, u32[]{:S(2)}) collective-permute-start(bf16[3,48,896]{2,1,0:T(8,128)(2,1)S(1)} %get-tuple-element.51), channel_id=1, source_target_pairs={{96,0},{112,16},{0,32},{16,48},{32,64},{48,80},{64,96},{80,112},{1... | collective-permute-start | bytes 774152 | tf_op jit(solution)/shard_map/ppermute | solution.py:33
  47.2 12.4 %collective-permute-start.10 = (bf16[3,48,896]{2,1,0:T(8,128)(2,1)S(1)}, bf16[3,48,896]{2,1,0:T(8,128)(2,1)S(1)}, u32[]{:S(2)}, u32[]{:S(2)}) collective-permute-start(bf16[3,48,896]{2,1,0:T(8,128)(2,1)S(1)} %get-tuple-element.52), channel_id=1, source_target_pairs={{32,0},{48,16},{64,32},{80,48},{96,64},{112,80},{0,96},{16,112},{4... | collective-permute-start | bytes 774152 | tf_op jit(solution)/shard_map/ppermute | solution.py:33
  56.2 13.0 %all-to-all-start = ((bf16[4,3,32,896]{3,2,1,0:T(8,128)(2,1)}), bf16[4,3,32,896]{3,2,1,0:T(8,128)(2,1)S(1)}, u32[]{:S(2)}, u32[]{:S(2)}) async-start(bf16[4,3,32,896]{3,2,1,0:T(8,128)(2,1)} %get-tuple-element.53), calls=%async_computation | async-start | bytes 1376256 | tf_op jit(solution)/shard_map/all_to_all | solution.py:387
  60.8 19.5 %collective-permute-start.13 = (bf16[3,96,896]{2,1,0:T(8,128)(2,1)}, bf16[3,96,896]{2,1,0:T(8,128)(2,1)S(1)}, u32[]{:S(2)}, u32[]{:S(2)}) collective-permute-start(bf16[3,96,896]{2,1,0:T(8,128)(2,1)} %get-tuple-element.56), channel_id=1, source_target_pairs={{96,0},{112,16},{0,32},{16,48},{32,64},{48,80},{64,96},{80,112},{1... | collective-permute-start | bytes 1548296 | tf_op jit(solution)/shard_map/ppermute | solution.py:33
  62.2 18.9 %collective-permute-start.14 = (bf16[3,96,896]{2,1,0:T(8,128)(2,1)}, bf16[3,96,896]{2,1,0:T(8,128)(2,1)}, u32[]{:S(2)}, u32[]{:S(2)}) collective-permute-start(bf16[3,96,896]{2,1,0:T(8,128)(2,1)} %get-tuple-element.57), channel_id=1, source_target_pairs={{32,0},{48,16},{64,32},{80,48},{96,64},{112,80},{0,96},{16,112},{4... | collective-permute-start | bytes 1548296 | tf_op jit(solution)/shard_map/ppermute | solution.py:33
  70.2 17.4 %all-to-all-start.1 = ((bf16[4,3,32,896]{3,2,1,0:T(8,128)(2,1)}), bf16[4,3,32,896]{3,2,1,0:T(8,128)(2,1)S(1)}, u32[]{:S(2)}, u32[]{:S(2)}) async-start(bf16[4,3,32,896]{3,2,1,0:T(8,128)(2,1)} %activate.2), calls=%async_computation.1 | async-start | bytes 1376256 | tf_op jit(solution)/shard_map/all_to_all | solution.py:387
  83.5 13.4 %collective-permute-start.15 = (bf16[3,96,896]{2,1,0:T(8,128)(2,1)S(1)}, bf16[3,96,896]{2,1,0:T(8,128)(2,1)S(1)}, u32[]{:S(2)}, u32[]{:S(2)}) collective-permute-start(bf16[3,96,896]{2,1,0:T(8,128)(2,1)S(1)} %activate.3.own), channel_id=1, source_target_pairs={{32,0},{48,16},{64,32},{80,48},{96,64},{112,80},{0,96},{16,112},{4... | collective-permute-start | bytes 1548296 | tf_op jit(solution)/shard_map/ppermute | solution.py:33
  84.2 13.7 %collective-permute-start.16 = (bf16[3,96,896]{2,1,0:T(8,128)(2,1)S(1)}, bf16[3,96,896]{2,1,0:T(8,128)(2,1)}, u32[]{:S(2)}, u32[]{:S(2)}) collective-permute-start(bf16[3,96,896]{2,1,0:T(8,128)(2,1)S(1)} %activate.3.own), channel_id=1, source_target_pairs={{96,0},{112,16},{0,32},{16,48},{32,64},{48,80},{64,96},{80,112},{1... | collective-permute-start | bytes 1548296 | tf_op jit(solution)/shard_map/ppermute | solution.py:33
  92.9 17.8 %collective-permute-start.19 = (bf16[2,2,32,1024]{3,2,1,0:T(8,128)(2,1)S(1)}, bf16[2,2,32,1024]{3,2,1,0:T(8,128)(2,1)S(1)}, u32[]{:S(2)}, u32[]{:S(2)}) collective-permute-start(bf16[2,2,32,1024]{3,2,1,0:T(8,128)(2,1)S(1)} %get-tuple-element.60), channel_id=1, source_target_pairs={{9,0},{22,16},{41,32},{54,48},{73,64},{86,80},{105,96},{118,112},{... | collective-permute-start | bytes 786440 | tf_op jit(solution)/shard_map/ppermute | solution.py:33
  93.0 17.8 %collective-permute-start.20 = (bf16[2,2,32,1024]{3,2,1,0:T(8,128)(2,1)S(1)}, bf16[2,2,32,1024]{3,2,1,0:T(8,128)(2,1)S(1)}, u32[]{:S(2)}, u32[]{:S(2)}) collective-permute-start(bf16[2,2,32,1024]{3,2,1,0:T(8,128)(2,1)S(1)} %get-tuple-element.61), channel_id=1, source_target_pairs={{8,0},{18,16},{40,32},{50,48},{72,64},{82,80},{104,96},{114,112},{... | collective-permute-start | bytes 786440 | tf_op jit(solution)/shard_map/ppermute | solution.py:33
  98.9 11.8 %collective-permute-start.17 = (bf16[3,48,896]{2,1,0:T(8,128)(2,1)S(1)}, bf16[3,48,896]{2,1,0:T(8,128)(2,1)S(1)}, u32[]{:S(2)}, u32[]{:S(2)}) collective-permute-start(bf16[3,48,896]{2,1,0:T(8,128)(2,1)S(1)} %slice.48), channel_id=1, source_target_pairs={{96,0},{112,16},{0,32},{16,48},{32,64},{48,80},{64,96},{80,112},{1... | collective-permute-start | bytes 774152 | tf_op jit(solution)/shard_map/ppermute | solution.py:33
  100.5 10.3 %collective-permute-start.18 = (bf16[3,48,896]{2,1,0:T(8,128)(2,1)S(1)}, bf16[3,48,896]{2,1,0:T(8,128)(2,1)S(1)}, u32[]{:S(2)}, u32[]{:S(2)}) collective-permute-start(bf16[3,48,896]{2,1,0:T(8,128)(2,1)S(1)} %slice.49), channel_id=1, source_target_pairs={{32,0},{48,16},{64,32},{80,48},{96,64},{112,80},{0,96},{16,112},{4... | collective-permute-start | bytes 774152 | tf_op jit(solution)/shard_map/ppermute | solution.py:33
  101.8 14.3 %collective-permute-start.23 = (bf16[2,384,1024]{2,1,0:T(8,128)(2,1)S(1)}, bf16[2,384,1024]{2,1,0:T(8,128)(2,1)S(1)}, u32[]{:S(2)}, u32[]{:S(2)}) collective-permute-start(bf16[2,384,1024]{2,1,0:T(8,128)(2,1)S(1)} %copy-done.11), channel_id=1, source_target_pairs={{16,0},{0,16},{48,32},{32,48},{80,64},{64,80},{112,96},{96,112},{2... | collective-permute-start | bytes 4718600 | tf_op jit(solution)/shard_map/ppermute | solution.py:33
  110.8 8.1 %collective-permute-start.25 = (bf16[3,288,896]{2,1,0:T(8,128)(2,1)S(1)}, bf16[3,288,896]{2,1,0:T(8,128)(2,1)S(1)}, u32[]{:S(2)}, u32[]{:S(2)}) collective-permute-start(bf16[3,288,896]{2,1,0:T(8,128)(2,1)S(1)} %get-tuple-element.77.refs_4_), channel_id=1, source_target_pairs={{16,0},{0,16},{48,32},{32,48},{80,64},{64,80},{112,96},{96,112},{2... | collective-permute-start | bytes 4644872 | tf_op jit(solution)/shard_map/ppermute | solution.py:33
  115.9 9.6 %collective-permute-start.21 = (bf16[4,2,32,1024]{3,2,1,0:T(8,128)(2,1)S(1)}, bf16[4,2,32,1024]{3,2,1,0:T(8,128)(2,1)S(1)}, u32[]{:S(2)}, u32[]{:S(2)}) collective-permute-start(bf16[4,2,32,1024]{3,2,1,0:T(8,128)(2,1)S(1)} %pad_maximum_fusion.1), channel_id=1, source_target_pairs={{9,0},{22,16},{41,32},{54,48},{73,64},{86,80},{105,96},{118,112},{... | collective-permute-start | bytes 1572872 | tf_op jit(solution)/shard_map/ppermute | solution.py:33
  116.0 9.5 %collective-permute-start.22 = (bf16[4,2,32,1024]{3,2,1,0:T(8,128)(2,1)S(1)}, bf16[4,2,32,1024]{3,2,1,0:T(8,128)(2,1)S(1)}, u32[]{:S(2)}, u32[]{:S(2)}) collective-permute-start(bf16[4,2,32,1024]{3,2,1,0:T(8,128)(2,1)S(1)} %pad_maximum_fusion.2), channel_id=1, source_target_pairs={{8,0},{18,16},{40,32},{50,48},{72,64},{82,80},{104,96},{114,112},{... | collective-permute-start | bytes 1572872 | tf_op jit(solution)/shard_map/ppermute | solution.py:33
  125.9 8.3 %collective-permute-start.28 = (bf16[2,32,1024]{2,1,0:T(8,128)(2,1)S(1)}, bf16[2,32,1024]{2,1,0:T(8,128)(2,1)S(1)}, u32[]{:S(2)}, u32[]{:S(2)}) collective-permute-start(bf16[2,32,1024]{2,1,0:T(8,128)(2,1)S(1)} %get-tuple-element.90), channel_id=1, source_target_pairs={{6,0},{25,16},{38,32},{57,48},{70,64},{89,80},{102,96},{121,112},{... | collective-permute-start | bytes 393224 | tf_op jit(solution)/shard_map/ppermute | solution.py:33
  (23 other events, 136.1 us)

commit v4 on v3

--- a/solution.py
+++ b/solution.py
@@ -243,7 +243,7 @@
     gradient_terms(trio, slice(0, 3 * t), refs[-2], copies, res)
 
 
-def late_kernel(counts, where, f0, f1, early, *refs):
+def late_kernel(counts, where, f0, f1, early, far0, far1, *refs):
     copies = start_all(refs[:4], refs[-2], refs[-1])
     trio, outs, res = refs[4], refs[5:-3], refs[-3]
     t = 2 * f0.shape[1]
@@ -252,6 +252,9 @@
     res[:, : 3 * t] = early[...]
     gradient_terms(trio, slice(3 * t, 4 * t), refs[-2], copies, res)
     hand_out(counts, lambda i: place_of(i, sum(counts) // 4, where[0]), res, outs)
+    for ref, first, got in ((outs[1], 0, far0), (outs[2], 2, far1)):
+        for j in range(2):
+            ref[first + j] = (ref[first + j].astype(F32) + got[j].astype(F32)).astype(BF)
 
 
 def backward_call(kernel, name, smem, inputs, mine, other, rows, outs, scratch=()):
@@ -282,12 +285,12 @@
     return backward_call(early_kernel, "backward_early", (), (own, up, down), mine, other, rows, (shape(3, rows, f), shape(2, rows, d)))
 
 
-def backward_late(where, f0, f1, early, mine, other, counts):
+def backward_late(where, f0, f1, early, far0, far1, mine, other, counts):
     d, f = mine[0].shape
     t = 2 * f0.shape[1]
     outs = shape(3, t, f), *(shape(n, 2, PIECE, d) for n in counts)
     kernel = functools.partial(late_kernel, counts)
-    return backward_call(kernel, "backward_late", (where,), (f0, f1, early), mine, other, t, outs, (pltpu.VMEM((2, 4 * t, d), BF),))
+    return backward_call(kernel, "backward_late", (where,), (f0, f1, early, far0, far1), mine, other, t, outs, (pltpu.VMEM((2, 4 * t, d), BF),))
 
 
 def weights_kernel(n, m, *refs):
@@ -423,11 +426,9 @@
     trio_early, early = backward_early(trio, up, down, mine, other)
     f0, f1 = after((f0, f1), (far0, far1, early))
     trio_far_got, trio_early_got = (from_core(v) for v in after((trio_far, trio_early), f0))
-    trio_late, line, ahead, behind = backward_late(where, f0, f1, early, mine, other, (4, 4, 4))
+    trio_late, line, ahead, behind = backward_late(where, f0, f1, early, far0, far1, mine, other, (4, 4, 4))
     trio_late_got = from_core(trio_late)
 
-    ahead = jnp.concatenate([plus(ahead[:2], far0).astype(BF), ahead[2:]])
-    behind = jnp.concatenate([behind[:2], plus(behind[2:], far1).astype(BF)])
     ahead, behind = from_side(ahead, -1), from_side(behind, 1)
 
     rows = near_mine, far_mine, near_got, far_got

time: 139 us -> 139 us (level)
  no operation moved by 1% of the time
where the time goes in v4:
time: 139 us; the launch traced here: 138 us
  starting transfers between devices  50.7 us (36%)
  Pallas kernels  41.5 us (30%)
  waiting for transfers between devices  36.3 us (26%)
  local copies, waits for them, and re-layouts  6.55 us (5%)
  other arithmetic  2.3 us (2%)
    ppermute x32, starting transfers between devices, from_where(): return lax.ppermute(value, ALL, pairs)  43.6 us
    ppermute x32, waiting for transfers between devices, from_where(): return lax.ppermute(value, ALL, pairs)  28 us
    pallas_call x2, Pallas kernels, forward(): pl.pallas_call(functools.partial(forward_kernel, counts, ring), out_shape...  15.8 us
    pallas_call x3, Pallas kernels, backward_call(): pl.pallas_call(kernel, out_shape=outs, in_specs=[SMEM] * len(smem) + vmem...  12.2 us
    all_to_all x2, waiting for transfers between devices, to_all_z(): lax.all_to_all(value, 'inp', 0, 0, axis_index_groups=[[0, 2, 4, 6], [1, 3...  8.29 us
    all_to_all x2, starting transfers between devices, to_all_z(): lax.all_to_all(value, 'inp', 0, 0, axis_index_groups=[[0, 2, 4, 6], [1, 3...  7.12 us
    pallas_call x1, Pallas kernels, weights(): pl.pallas_call(functools.partial(weights_kernel, n, len(trios)), grid=(d...  5.66 us
    pallas_call x1, Pallas kernels, down_weights(): pl.pallas_call(functools.partial(down_kernel, n, len(trios)), grid=(d //...  4.3 us
  transfers between devices with their start and end apart: 34, of which 12 were waited for; matrix products, arithmetic and copies ran while one was open for 2% of the time, Pallas kernels for 30%

profile of v4, /device:TPU:1, one launch (start us, length us, event | category | flops | bytes accessed | tf_op | source)
XLA Modules:
  0.0 138.3 jit_solution(11567593905385447699)
XLA Ops:
  4.3 3.1 %collective-permute-start.3 = (bf16[2,2,32,1024]{3,2,1,0:T(8,128)(2,1)S(1)}, bf16[2,2,32,1024]{3,2,1,0:T(8,128)(2,1)S(1)}, u32[]{:S(2)}, u32[]{:S(2)}) collective-permute-start(bf16[2,2,32,1024]{3,2,1,0:T(8,128)(2,1)S(1)} %get-tuple-element.92), channel_id=1, source_target_pairs={{4,0},{17,16},{36,32},{49,48},{68,64},{81,80},{100,96},{113,112},{... | collective-permute-start | bytes 786440 | tf_op jit(solution)/shard_map/ppermute | solution.py:33
  7.8 2.3 %collective-permute-start.1 = (bf16[2,2,32,1024]{3,2,1,0:T(8,128)(2,1)S(1)}, bf16[2,2,32,1024]{3,2,1,0:T(8,128)(2,1)S(1)}, u32[]{:S(2)}, u32[]{:S(2)}) collective-permute-start(bf16[2,2,32,1024]{3,2,1,0:T(8,128)(2,1)S(1)} %get-tuple-element.92), channel_id=1, source_target_pairs={{2,0},{24,16},{34,32},{56,48},{66,64},{88,80},{98,96},{120,112},{1... | collective-permute-start | bytes 786440 | tf_op jit(solution)/shard_map/ppermute | solution.py:33
  11.4 2.8 %collective-permute-done.2 = bf16[2,2,32,1024]{3,2,1,0:T(8,128)(2,1)S(1)} collective-permute-done((bf16[2,2,32,1024]{3,2,1,0:T(8,128)(2,1)S(1)}, bf16[2,2,32,1024]{3,2,1,0:T(8,128)(2,1)S(1)}, u32[]{:S(2)}, u32[]{:S(2)}) %collective-permute-start.2) | collective-permute-done | bytes 262176 | tf_op jit(solution)/shard_map/ppermute | solution.py:33
  16.3 2.8 %collective-permute-start.4 = (bf16[4,2,2,32,1024]{4,3,2,1,0:T(8,128)(2,1)S(1)}, bf16[4,2,2,32,1024]{4,3,2,1,0:T(8,128)(2,1)S(1)}, u32[]{:S(2)}, u32[]{:S(2)}) collective-permute-start(bf16[4,2,2,32,1024]{4,3,2,1,0:T(8,128)(2,1)S(1)} %pad_maximum_fusion.refs_0_), channel_id=1, source_target_pairs={{8,0},{18,16},{40,32},{50,48},{72,64},{82,80},{104,96},{114,112},{... | collective-permute-start | bytes 3145736 | tf_op jit(solution)/shard_map/ppermute | solution.py:33
  19.1 11.7 %collective-permute-done.4.refs_1_ = bf16[4,2,2,32,1024]{4,3,2,1,0:T(8,128)(2,1)S(1)} collective-permute-done((bf16[4,2,2,32,1024]{4,3,2,1,0:T(8,128)(2,1)S(1)}, bf16[4,2,2,32,1024]{4,3,2,1,0:T(8,128)(2,1)S(1)}, u32[]{:S(2)}, u32[]{:S(2)}) %collective-permute-start.4) | collective-permute-done | bytes 1048608 | tf_op jit(solution)/shard_map/ppermute | solution.py:33
  31.8 3.4 %collective-permute-start.11 = (bf16[2,2,2,32,1024]{4,3,2,1,0:T(8,128)(2,1)}, bf16[2,2,2,32,1024]{4,3,2,1,0:T(8,128)(2,1)}, u32[]{:S(2)}, u32[]{:S(2)}) collective-permute-start(bf16[2,2,2,32,1024]{4,3,2,1,0:T(8,128)(2,1)} %slice.44), channel_id=1, source_target_pairs={{8,0},{18,16},{40,32},{50,48},{72,64},{82,80},{104,96},{114,112},{... | collective-permute-start | bytes 1572872 | tf_op jit(solution)/shard_map/ppermute | solution.py:33
  36.4 9.1 %forward.2 = (bf16[2,384,1024]{2,1,0:T(8,128)(2,1)}, bf16[2,384,1024]{2,1,0:T(8,128)(2,1)}, bf16[3,96,896]{2,1,0:T(8,128)(2,1)S(1)}, bf16[3,96,896]{2,1,0:T(8,12...) custom-call(s32[1]{0:T(128)} %bitcast.where, ...), custom_call_target="tpu_custom_call" | custom-call | flops 4227858432 | bytes 17301504 | tf_op jit(solution)/shard_map/forward/pallas_call | solution.py:132
  47.2 2.2 %collective-permute-start.10 = (bf16[3,48,896]{2,1,0:T(8,128)(2,1)S(1)}, bf16[3,48,896]{2,1,0:T(8,128)(2,1)S(1)}, u32[]{:S(2)}, u32[]{:S(2)}) collective-permute-start(bf16[3,48,896]{2,1,0:T(8,128)(2,1)S(1)} %get-tuple-element.52), channel_id=1, source_target_pairs={{32,0},{48,16},{64,32},{80,48},{96,64},{112,80},{0,96},{16,112},{4... | collective-permute-start | bytes 774152 | tf_op jit(solution)/shard_map/ppermute | solution.py:33
  49.5 6.7 %forward.3 = (bf16[2,128,1024]{2,1,0:T(8,128)(2,1)}, bf16[2,128,1024]{2,1,0:T(8,128)(2,1)}, bf16[4,3,32,896]{3,2,1,0:T(8,128)(2,1)}) custom-call(s32[1]{0:T(128)} %bitcast.where, bf16[2,2,2,32,1024]{4,3,2,1,0:T(8,128)(2,1)} %collective-permute-done.11.refs_0_, bf16[2,2,2,32,1024]{4,3,2,1,0:T(8,128)(2,1)} %collective-permute-done.12.refs_1_, ...), custom_call_target="tpu_custom_call" | custom-call | flops 1409286144 | bytes 13107200 | tf_op jit(solution)/shard_map/forward/pallas_call | solution.py:132
  56.2 3.5 %all-to-all-start = ((bf16[4,3,32,896]{3,2,1,0:T(8,128)(2,1)}), bf16[4,3,32,896]{3,2,1,0:T(8,128)(2,1)S(1)}, u32[]{:S(2)}, u32[]{:S(2)}) async-start(bf16[4,3,32,896]{3,2,1,0:T(8,128)(2,1)} %get-tuple-element.53), calls=%async_computation | async-start | bytes 1376256 | tf_op jit(solution)/shard_map/all_to_all | solution.py:390
  63.4 5.7 %all-to-all-done.refs_0_ = bf16[4,3,32,896]{3,2,1,0:T(8,128)(2,1)S(1)} async-done(((bf16[4,3,32,896]{3,2,1,0:T(8,128)(2,1)}), bf16[4,3,32,896]{3,2,1,0:T(8,128)(2,1)S(1)}, u32[]{:S(2)}, u32[]{:S(2)}) %all-to-all-start) | async-done | bytes 688160 | tf_op jit(solution)/shard_map/all_to_all | solution.py:390
  70.2 3.6 %all-to-all-start.1 = ((bf16[4,3,32,896]{3,2,1,0:T(8,128)(2,1)}), bf16[4,3,32,896]{3,2,1,0:T(8,128)(2,1)S(1)}, u32[]{:S(2)}, u32[]{:S(2)}) async-start(bf16[4,3,32,896]{3,2,1,0:T(8,128)(2,1)} %activate.2), calls=%async_computation.1 | async-start | bytes 1376256 | tf_op jit(solution)/shard_map/all_to_all | solution.py:390
  73.8 6.4 %collective-permute-done.13.refs_1_ = bf16[3,96,896]{2,1,0:T(8,128)(2,1)S(1)} collective-permute-done((bf16[3,96,896]{2,1,0:T(8,128)(2,1)}, bf16[3,96,896]{2,1,0:T(8,128)(2,1)S(1)}, u32[]{:S(2)}, u32[]{:S(2)}) %collective-permute-start.13) | collective-permute-done | bytes 516128 | tf_op jit(solution)/shard_map/ppermute | solution.py:33
  85.0 2.6 %all-to-all-done.1.parts = bf16[4,3,32,896]{3,2,1,0:T(8,128)(2,1)S(1)} async-done(((bf16[4,3,32,896]{3,2,1,0:T(8,128)(2,1)}), bf16[4,3,32,896]{3,2,1,0:T(8,128)(2,1)S(1)}, u32[]{:S(2)}, u32[]{:S(2)}) %all-to-all-start.1) | async-done | bytes 688160 | tf_op jit(solution)/shard_map/all_to_all | solution.py:390
  89.1 3.8 %backward.1 = (bf16[3,128,896]{2,1,0:T(8,128)(2,1)S(1)}, bf16[2,2,32,1024]{3,2,1,0:T(8,128)(2,1)S(1)}, bf16[2,2,32,1024]{3,2,1,0:T(8,128)(2,1)S(1)}) custom-call(bf16[4,3,32,896]{3,2,1,0:T(8,128)(2,1)S(1)} %all-to-all-done.1.parts, bf16[1024,896]{1,0:T(8,128)(2,1)S(1)} %copy-done.1, bf16[1024,896]{1,0:T(8,128)(2,1)S(1)} %copy-done.2, ...), custom_call_target="tpu_custom_call" | custom-call | flops 939524096 | bytes 8552448 | tf_op jit(solution)/shard_map/backward/pallas_call | solution.py:262
  92.9 2.7 %collective-permute-start.20 = (bf16[2,2,32,1024]{3,2,1,0:T(8,128)(2,1)S(1)}, bf16[2,2,32,1024]{3,2,1,0:T(8,128)(2,1)S(1)}, u32[]{:S(2)}, u32[]{:S(2)}) collective-permute-start(bf16[2,2,32,1024]{3,2,1,0:T(8,128)(2,1)S(1)} %get-tuple-element.61), channel_id=1, source_target_pairs={{8,0},{18,16},{40,32},{50,48},{72,64},{82,80},{104,96},{114,112},{... | collective-permute-start | bytes 786440 | tf_op jit(solution)/shard_map/ppermute | solution.py:33
  101.8 4.2 %collective-permute-start.23 = (bf16[2,384,1024]{2,1,0:T(8,128)(2,1)S(1)}, bf16[2,384,1024]{2,1,0:T(8,128)(2,1)S(1)}, u32[]{:S(2)}, u32[]{:S(2)}) collective-permute-start(bf16[2,384,1024]{2,1,0:T(8,128)(2,1)S(1)} %copy-done.11), channel_id=1, source_target_pairs={{16,0},{0,16},{48,32},{32,48},{80,64},{64,80},{112,96},{96,112},{2... | collective-permute-start | bytes 4718600 | tf_op jit(solution)/shard_map/ppermute | solution.py:33
  105.9 4.8 %backward_early.1 = (bf16[3,288,896]{2,1,0:T(8,128)(2,1)S(1)}, bf16[2,288,1024]{2,1,0:T(8,128)(2,1)S(1)}) custom-call(bf16[3,96,896]{2,1,0:T(8,128)(2,1)S(1)} %activate.3.own, bf16[3,96,896]{2,1,0:T(8,128)(2,1)S(1)} %collective-permute-done.15.up, bf16[3,96,896]{2,1,0:T(8,128)(2,1)} %collective-permute-done.16.down, bf16[1024,896]{1,0:T(8,128)(2,1)S(1)} %copy-done.1, ...), custom_call_target="tpu_custom_call" | custom-call | flops 2113929216 | bytes 10067968 | tf_op jit(solution)/shard_map/backward_early/pallas_call | solution.py:262
  111.5 3.7 %backward_late.1 = (bf16[3,96,896]{2,1,0:T(8,128)(2,1)S(1)}, bf16[4,2,32,1024]{3,2,1,0:T(8,128)(2,1)S(1)}, bf16[4,2,32,1024]{3,2,1,0:T(8,128)(2,1)S(1)}, bf16[4,2,32,1024]{3,2,1,0:T(8,128)(2,1)S(1)}) custom-call(s32[1]{0:T(128)} %bitcast.where, bf16[3,48,896]{2,1,0:T(8,128)(2,1)S(1)} %collective-permute-done.17.f0, ...), custom_call_target="tpu_custom_call" | custom-call | flops 704643072 | bytes 8249344 | tf_op jit(solution)/shard_map/backward_late/pallas_call | solution.py:262
  115.7 2.8 %collective-permute-start.22 = (bf16[4,2,32,1024]{3,2,1,0:T(8,128)(2,1)S(1)}, bf16[4,2,32,1024]{3,2,1,0:T(8,128)(2,1)S(1)}, u32[]{:S(2)}, u32[]{:S(2)}) collective-permute-start(bf16[4,2,32,1024]{3,2,1,0:T(8,128)(2,1)S(1)} %get-tuple-element.69), channel_id=1, source_target_pairs={{8,0},{18,16},{40,32},{50,48},{72,64},{82,80},{104,96},{114,112},{... | collective-permute-start | bytes 1572872 | tf_op jit(solution)/shard_map/ppermute | solution.py:33
  118.6 5.7 %weights.1 = (bf16[1024,896]{1,0:T(8,128)(2,1)}, bf16[1024,896]{1,0:T(8,128)(2,1)}) custom-call(bf16[2,384,1024]{2,1,0:T(8,128)(2,1)S(1)} %copy-done.4, bf16[2,128,1024]{2,1,0:T(8,128)(2,1)S(1)} %copy-done.5, bf16[2,384,1024]{2,1,0:T(8,128)(2,1)S(1)} %collective-permute-done.23.refs_2_, bf16[2,128,1024]{2,1,0:T(8,128)(2,1)S(1)} %collective-permute-done.24.refs_3_, ...), custom_call_target="tpu_custom_call" | custom-call | flops 3758096384 | bytes 9437184 | tf_op jit(solution)/shard_map/weights/pallas_call | solution.py:325
  126.4 2.0 %collective-permute-start.29 = (bf16[2,32,1024]{2,1,0:T(8,128)(2,1)S(1)}, bf16[2,32,1024]{2,1,0:T(8,128)(2,1)S(1)}, u32[]{:S(2)}, u32[]{:S(2)}) collective-permute-start(bf16[2,32,1024]{2,1,0:T(8,128)(2,1)S(1)} %get-tuple-element.89), channel_id=1, source_target_pairs={{2,0},{24,16},{34,32},{56,48},{66,64},{88,80},{98,96},{120,112},{1... | collective-permute-start | bytes 393224 | tf_op jit(solution)/shard_map/ppermute | solution.py:33
  129.6 4.3 %down_weights.1 = bf16[896,1024]{1,0:T(8,128)(2,1)} custom-call(bf16[2,384,1024]{2,1,0:T(8,128)(2,1)S(1)} %copy-done.4, bf16[2,128,1024]{2,1,0:T(8,128)(2,1)S(1)} %copy-done.5, bf16[2,384,1024]{2,1,0:T(8,128)(2,1)S(1)} %collective-permute-done.23.refs_2_, bf16[2,128,1024]{2,1,0:T(8,128)(2,1)S(1)} %collective-permute-done.24.refs_3_, ...), custom_call_target="tpu_custom_call" | custom-call | flops 1879048192 | bytes 5767168 | tf_op jit(solution)/shard_map/down_weights/pallas_call | solution.py:364
  134.0 2.7 %collective-permute-start.31 = (bf16[32,1024]{1,0:T(8,128)(2,1)S(1)}, bf16[32,1024]{1,0:T(8,128)(2,1)S(1)}, u32[]{:S(2)}, u32[]{:S(2)}) collective-permute-start(bf16[32,1024]{1,0:T(8,128)(2,1)S(1)} %slice_bitcast_fusion.4), channel_id=1, source_target_pairs={{16,0},{0,16},{48,32},{32,48},{80,64},{64,80},{112,96},{96,112},{2... | collective-permute-start | bytes 196616 | tf_op jit(solution)/shard_map/ppermute | solution.py:33
  (93 shorter events, 34.8 us)
Async XLA Ops:
  14.8 21.6 %collective-permute-start.6 = (bf16[1024,896]{1,0:T(8,128)(2,1)S(1)}, bf16[1024,896]{1,0:T(8,128)(2,1)}, u32[]{:S(2)}, u32[]{:S(2)}) collective-permute-start(bf16[1024,896]{1,0:T(8,128)(2,1)S(1)} %copy-done), channel_id=1, source_target_pairs={{16,0},{0,16},{48,32},{32,48},{80,64},{64,80},{112,96},{96,112},{2... | collective-permute-start | bytes 5505032 | tf_op jit(solution)/shard_map/ppermute | solution.py:33
  15.8 20.6 %collective-permute-start.7 = (bf16[1024,896]{1,0:T(8,128)(2,1)}, bf16[1024,896]{1,0:T(8,128)(2,1)}, u32[]{:S(2)}, u32[]{:S(2)}) collective-permute-start(bf16[1024,896]{1,0:T(8,128)(2,1)} %refs_1_.5), channel_id=1, source_target_pairs={{16,0},{0,16},{48,32},{32,48},{80,64},{64,80},{112,96},{96,112},{2... | collective-permute-start | bytes 5505032 | tf_op jit(solution)/shard_map/ppermute | solution.py:33
  15.9 20.5 %collective-permute-start.8 = (bf16[896,1024]{1,0:T(8,128)(2,1)}, bf16[896,1024]{1,0:T(8,128)(2,1)}, u32[]{:S(2)}, u32[]{:S(2)}) collective-permute-start(bf16[896,1024]{1,0:T(8,128)(2,1)} %refs_4_.3), channel_id=1, source_target_pairs={{16,0},{0,16},{48,32},{32,48},{80,64},{64,80},{112,96},{96,112},{2... | collective-permute-start | bytes 5505032 | tf_op jit(solution)/shard_map/ppermute | solution.py:33
  16.3 14.5 %collective-permute-start.4 = (bf16[4,2,2,32,1024]{4,3,2,1,0:T(8,128)(2,1)S(1)}, bf16[4,2,2,32,1024]{4,3,2,1,0:T(8,128)(2,1)S(1)}, u32[]{:S(2)}, u32[]{:S(2)}) collective-permute-start(bf16[4,2,2,32,1024]{4,3,2,1,0:T(8,128)(2,1)S(1)} %pad_maximum_fusion.refs_0_), channel_id=1, source_target_pairs={{8,0},{18,16},{40,32},{50,48},{72,64},{82,80},{104,96},{114,112},{... | collective-permute-start | bytes 3145736 | tf_op jit(solution)/shard_map/ppermute | solution.py:33
  19.1 16.1 %collective-permute-start.5 = (bf16[4,2,2,32,1024]{4,3,2,1,0:T(8,128)(2,1)S(1)}, bf16[4,2,2,32,1024]{4,3,2,1,0:T(8,128)(2,1)S(1)}, u32[]{:S(2)}, u32[]{:S(2)}) collective-permute-start(bf16[4,2,2,32,1024]{4,3,2,1,0:T(8,128)(2,1)S(1)} %pad_maximum_fusion.refs_0_), channel_id=1, source_target_pairs={{9,0},{22,16},{41,32},{54,48},{73,64},{86,80},{105,96},{118,112},{... | collective-permute-start | bytes 3145736 | tf_op jit(solution)/shard_map/ppermute | solution.py:33
  31.8 17.6 %collective-permute-start.11 = (bf16[2,2,2,32,1024]{4,3,2,1,0:T(8,128)(2,1)}, bf16[2,2,2,32,1024]{4,3,2,1,0:T(8,128)(2,1)}, u32[]{:S(2)}, u32[]{:S(2)}) collective-permute-start(bf16[2,2,2,32,1024]{4,3,2,1,0:T(8,128)(2,1)} %slice.44), channel_id=1, source_target_pairs={{8,0},{18,16},{40,32},{50,48},{72,64},{82,80},{104,96},{114,112},{... | collective-permute-start | bytes 1572872 | tf_op jit(solution)/shard_map/ppermute | solution.py:33
  36.4 13.0 %collective-permute-start.12 = (bf16[2,2,2,32,1024]{4,3,2,1,0:T(8,128)(2,1)}, bf16[2,2,2,32,1024]{4,3,2,1,0:T(8,128)(2,1)}, u32[]{:S(2)}, u32[]{:S(2)}) collective-permute-start(bf16[2,2,2,32,1024]{4,3,2,1,0:T(8,128)(2,1)} %slice.45), channel_id=1, source_target_pairs={{9,0},{22,16},{41,32},{54,48},{73,64},{86,80},{105,96},{118,112},{... | collective-permute-start | bytes 1572872 | tf_op jit(solution)/shard_map/ppermute | solution.py:33
  45.5 14.1 %collective-permute-start.9 = (bf16[3,48,896]{2,1,0:T(8,128)(2,1)S(1)}, bf16[3,48,896]{2,1,0:T(8,128)(2,1)S(1)}, u32[]{:S(2)}, u32[]{:S(2)}) collective-permute-start(bf16[3,48,896]{2,1,0:T(8,128)(2,1)S(1)} %get-tuple-element.51), channel_id=1, source_target_pairs={{96,0},{112,16},{0,32},{16,48},{32,64},{48,80},{64,96},{80,112},{1... | collective-permute-start | bytes 774152 | tf_op jit(solution)/shard_map/ppermute | solution.py:33
  47.2 12.4 %collective-permute-start.10 = (bf16[3,48,896]{2,1,0:T(8,128)(2,1)S(1)}, bf16[3,48,896]{2,1,0:T(8,128)(2,1)S(1)}, u32[]{:S(2)}, u32[]{:S(2)}) collective-permute-start(bf16[3,48,896]{2,1,0:T(8,128)(2,1)S(1)} %get-tuple-element.52), channel_id=1, source_target_pairs={{32,0},{48,16},{64,32},{80,48},{96,64},{112,80},{0,96},{16,112},{4... | collective-permute-start | bytes 774152 | tf_op jit(solution)/shard_map/ppermute | solution.py:33
  56.2 13.0 %all-to-all-start = ((bf16[4,3,32,896]{3,2,1,0:T(8,128)(2,1)}), bf16[4,3,32,896]{3,2,1,0:T(8,128)(2,1)S(1)}, u32[]{:S(2)}, u32[]{:S(2)}) async-start(bf16[4,3,32,896]{3,2,1,0:T(8,128)(2,1)} %get-tuple-element.53), calls=%async_computation | async-start | bytes 1376256 | tf_op jit(solution)/shard_map/all_to_all | solution.py:390
  60.8 19.5 %collective-permute-start.13 = (bf16[3,96,896]{2,1,0:T(8,128)(2,1)}, bf16[3,96,896]{2,1,0:T(8,128)(2,1)S(1)}, u32[]{:S(2)}, u32[]{:S(2)}) collective-permute-start(bf16[3,96,896]{2,1,0:T(8,128)(2,1)} %get-tuple-element.56), channel_id=1, source_target_pairs={{96,0},{112,16},{0,32},{16,48},{32,64},{48,80},{64,96},{80,112},{1... | collective-permute-start | bytes 1548296 | tf_op jit(solution)/shard_map/ppermute | solution.py:33
  62.2 18.9 %collective-permute-start.14 = (bf16[3,96,896]{2,1,0:T(8,128)(2,1)}, bf16[3,96,896]{2,1,0:T(8,128)(2,1)}, u32[]{:S(2)}, u32[]{:S(2)}) collective-permute-start(bf16[3,96,896]{2,1,0:T(8,128)(2,1)} %get-tuple-element.57), channel_id=1, source_target_pairs={{32,0},{48,16},{64,32},{80,48},{96,64},{112,80},{0,96},{16,112},{4... | collective-permute-start | bytes 1548296 | tf_op jit(solution)/shard_map/ppermute | solution.py:33
  70.2 17.4 %all-to-all-start.1 = ((bf16[4,3,32,896]{3,2,1,0:T(8,128)(2,1)}), bf16[4,3,32,896]{3,2,1,0:T(8,128)(2,1)S(1)}, u32[]{:S(2)}, u32[]{:S(2)}) async-start(bf16[4,3,32,896]{3,2,1,0:T(8,128)(2,1)} %activate.2), calls=%async_computation.1 | async-start | bytes 1376256 | tf_op jit(solution)/shard_map/all_to_all | solution.py:390
  83.5 13.4 %collective-permute-start.15 = (bf16[3,96,896]{2,1,0:T(8,128)(2,1)S(1)}, bf16[3,96,896]{2,1,0:T(8,128)(2,1)S(1)}, u32[]{:S(2)}, u32[]{:S(2)}) collective-permute-start(bf16[3,96,896]{2,1,0:T(8,128)(2,1)S(1)} %activate.3.own), channel_id=1, source_target_pairs={{32,0},{48,16},{64,32},{80,48},{96,64},{112,80},{0,96},{16,112},{4... | collective-permute-start | bytes 1548296 | tf_op jit(solution)/shard_map/ppermute | solution.py:33
  84.2 13.7 %collective-permute-start.16 = (bf16[3,96,896]{2,1,0:T(8,128)(2,1)S(1)}, bf16[3,96,896]{2,1,0:T(8,128)(2,1)}, u32[]{:S(2)}, u32[]{:S(2)}) collective-permute-start(bf16[3,96,896]{2,1,0:T(8,128)(2,1)S(1)} %activate.3.own), channel_id=1, source_target_pairs={{96,0},{112,16},{0,32},{16,48},{32,64},{48,80},{64,96},{80,112},{1... | collective-permute-start | bytes 1548296 | tf_op jit(solution)/shard_map/ppermute | solution.py:33
  92.9 17.9 %collective-permute-start.19 = (bf16[2,2,32,1024]{3,2,1,0:T(8,128)(2,1)S(1)}, bf16[2,2,32,1024]{3,2,1,0:T(8,128)(2,1)S(1)}, u32[]{:S(2)}, u32[]{:S(2)}) collective-permute-start(bf16[2,2,32,1024]{3,2,1,0:T(8,128)(2,1)S(1)} %get-tuple-element.60), channel_id=1, source_target_pairs={{9,0},{22,16},{41,32},{54,48},{73,64},{86,80},{105,96},{118,112},{... | collective-permute-start | bytes 786440 | tf_op jit(solution)/shard_map/ppermute | solution.py:33
  92.9 17.8 %collective-permute-start.20 = (bf16[2,2,32,1024]{3,2,1,0:T(8,128)(2,1)S(1)}, bf16[2,2,32,1024]{3,2,1,0:T(8,128)(2,1)S(1)}, u32[]{:S(2)}, u32[]{:S(2)}) collective-permute-start(bf16[2,2,32,1024]{3,2,1,0:T(8,128)(2,1)S(1)} %get-tuple-element.61), channel_id=1, source_target_pairs={{8,0},{18,16},{40,32},{50,48},{72,64},{82,80},{104,96},{114,112},{... | collective-permute-start | bytes 786440 | tf_op jit(solution)/shard_map/ppermute | solution.py:33
  98.9 11.8 %collective-permute-start.17 = (bf16[3,48,896]{2,1,0:T(8,128)(2,1)S(1)}, bf16[3,48,896]{2,1,0:T(8,128)(2,1)S(1)}, u32[]{:S(2)}, u32[]{:S(2)}) collective-permute-start(bf16[3,48,896]{2,1,0:T(8,128)(2,1)S(1)} %slice.36), channel_id=1, source_target_pairs={{96,0},{112,16},{0,32},{16,48},{32,64},{48,80},{64,96},{80,112},{1... | collective-permute-start | bytes 774152 | tf_op jit(solution)/shard_map/ppermute | solution.py:33
  100.5 10.3 %collective-permute-start.18 = (bf16[3,48,896]{2,1,0:T(8,128)(2,1)S(1)}, bf16[3,48,896]{2,1,0:T(8,128)(2,1)S(1)}, u32[]{:S(2)}, u32[]{:S(2)}) collective-permute-start(bf16[3,48,896]{2,1,0:T(8,128)(2,1)S(1)} %slice.37), channel_id=1, source_target_pairs={{32,0},{48,16},{64,32},{80,48},{96,64},{112,80},{0,96},{16,112},{4... | collective-permute-start | bytes 774152 | tf_op jit(solution)/shard_map/ppermute | solution.py:33
  101.8 13.9 %collective-permute-start.23 = (bf16[2,384,1024]{2,1,0:T(8,128)(2,1)S(1)}, bf16[2,384,1024]{2,1,0:T(8,128)(2,1)S(1)}, u32[]{:S(2)}, u32[]{:S(2)}) collective-permute-start(bf16[2,384,1024]{2,1,0:T(8,128)(2,1)S(1)} %copy-done.11), channel_id=1, source_target_pairs={{16,0},{0,16},{48,32},{32,48},{80,64},{64,80},{112,96},{96,112},{2... | collective-permute-start | bytes 4718600 | tf_op jit(solution)/shard_map/ppermute | solution.py:33
  110.8 7.8 %collective-permute-start.25 = (bf16[3,288,896]{2,1,0:T(8,128)(2,1)S(1)}, bf16[3,288,896]{2,1,0:T(8,128)(2,1)S(1)}, u32[]{:S(2)}, u32[]{:S(2)}) collective-permute-start(bf16[3,288,896]{2,1,0:T(8,128)(2,1)S(1)} %get-tuple-element.77.refs_4_), channel_id=1, source_target_pairs={{16,0},{0,16},{48,32},{32,48},{80,64},{64,80},{112,96},{96,112},{2... | collective-permute-start | bytes 4644872 | tf_op jit(solution)/shard_map/ppermute | solution.py:33
  115.7 9.5 %collective-permute-start.21 = (bf16[4,2,32,1024]{3,2,1,0:T(8,128)(2,1)S(1)}, bf16[4,2,32,1024]{3,2,1,0:T(8,128)(2,1)S(1)}, u32[]{:S(2)}, u32[]{:S(2)}) collective-permute-start(bf16[4,2,32,1024]{3,2,1,0:T(8,128)(2,1)S(1)} %get-tuple-element.68), channel_id=1, source_target_pairs={{9,0},{22,16},{41,32},{54,48},{73,64},{86,80},{105,96},{118,112},{... | collective-permute-start | bytes 1572872 | tf_op jit(solution)/shard_map/ppermute | solution.py:33
  115.7 9.5 %collective-permute-start.22 = (bf16[4,2,32,1024]{3,2,1,0:T(8,128)(2,1)S(1)}, bf16[4,2,32,1024]{3,2,1,0:T(8,128)(2,1)S(1)}, u32[]{:S(2)}, u32[]{:S(2)}) collective-permute-start(bf16[4,2,32,1024]{3,2,1,0:T(8,128)(2,1)S(1)} %get-tuple-element.69), channel_id=1, source_target_pairs={{8,0},{18,16},{40,32},{50,48},{72,64},{82,80},{104,96},{114,112},{... | collective-permute-start | bytes 1572872 | tf_op jit(solution)/shard_map/ppermute | solution.py:33
  125.6 8.3 %collective-permute-start.28 = (bf16[2,32,1024]{2,1,0:T(8,128)(2,1)S(1)}, bf16[2,32,1024]{2,1,0:T(8,128)(2,1)S(1)}, u32[]{:S(2)}, u32[]{:S(2)}) collective-permute-start(bf16[2,32,1024]{2,1,0:T(8,128)(2,1)S(1)} %get-tuple-element.90), channel_id=1, source_target_pairs={{6,0},{25,16},{38,32},{57,48},{70,64},{89,80},{102,96},{121,112},{... | collective-permute-start | bytes 393224 | tf_op jit(solution)/shard_map/ppermute | solution.py:33
  (23 other events, 146.5 us)

commit v5 on v4

--- a/solution.py
+++ b/solution.py
@@ -437,7 +437,7 @@
     ahead, behind = after((ahead, behind), gate_up)
 
     line = plus(line, ahead, behind)
-    sent = [from_line(line[j].astype(BF), -OFFSETS[j]) for j in range(1, 4)]
+    sent = [from_line(line[j].astype(BF), -OFFSETS[j]) for j in (3, 2, 1)]
     grad_w_down = down_weights(rows, trios)
     sent = after(sent, grad_w_down)
     sums = plus(line[0], *sent).astype(BF)

time: 139 us -> 138 us (level)
  transfers between devices with their start and end apart: 34 -> 34, of which waited for: 12 -> 13; matrix products, arithmetic and copies ran while one was open for 2% -> 2% of each run, Pallas kernels for 30% -> 30%
where the time goes in v5:
time: 138 us
  starting transfers between devices  50.1 us (36%)
  Pallas kernels  41.5 us (30%)
  waiting for transfers between devices  36.4 us (26%)
  local copies, waits for them, and re-layouts  6.55 us (5%)
  other arithmetic  2.3 us (2%)
    ppermute x32, starting transfers between devices, from_where(): return lax.ppermute(value, ALL, pairs)  43 us
    ppermute x32, waiting for transfers between devices, from_where(): return lax.ppermute(value, ALL, pairs)  28.1 us
    pallas_call x2, Pallas kernels, forward(): pl.pallas_call(functools.partial(forward_kernel, counts, ring), out_shape...  15.8 us
    pallas_call x3, Pallas kernels, backward_call(): pl.pallas_call(kernel, out_shape=outs, in_specs=[SMEM] * len(smem) + vmem...  12.2 us
    all_to_all x2, waiting for transfers between devices, to_all_z(): lax.all_to_all(value, 'inp', 0, 0, axis_index_groups=[[0, 2, 4, 6], [1, 3...  8.29 us
    all_to_all x2, starting transfers between devices, to_all_z(): lax.all_to_all(value, 'inp', 0, 0, axis_index_groups=[[0, 2, 4, 6], [1, 3...  7.12 us
    pallas_call x1, Pallas kernels, weights(): pl.pallas_call(functools.partial(weights_kernel, n, len(trios)), grid=(d...  5.66 us
    pallas_call x1, Pallas kernels, down_weights(): pl.pallas_call(functools.partial(down_kernel, n, len(trios)), grid=(d //...  4.3 us
  transfers between devices with their start and end apart: 34, of which 13 were waited for; matrix products, arithmetic and copies ran while one was open for 2% of the time, Pallas kernels for 30%

profile of v5, /device:TPU:1, one launch (start us, length us, event | category | flops | bytes accessed | tf_op | source)
XLA Modules:
  0.0 137.7 jit_solution(1546242936502833742)
XLA Ops:
  4.3 3.1 %collective-permute-start.3 = (bf16[2,2,32,1024]{3,2,1,0:T(8,128)(2,1)S(1)}, bf16[2,2,32,1024]{3,2,1,0:T(8,128)(2,1)S(1)}, u32[]{:S(2)}, u32[]{:S(2)}) collective-permute-start(bf16[2,2,32,1024]{3,2,1,0:T(8,128)(2,1)S(1)} %get-tuple-element.92), channel_id=1, source_target_pairs={{4,0},{17,16},{36,32},{49,48},{68,64},{81,80},{100,96},{113,112},{... | collective-permute-start | bytes 786440 | tf_op jit(solution)/shard_map/ppermute | solution.py:33
  7.8 2.3 %collective-permute-start.1 = (bf16[2,2,32,1024]{3,2,1,0:T(8,128)(2,1)S(1)}, bf16[2,2,32,1024]{3,2,1,0:T(8,128)(2,1)S(1)}, u32[]{:S(2)}, u32[]{:S(2)}) collective-permute-start(bf16[2,2,32,1024]{3,2,1,0:T(8,128)(2,1)S(1)} %get-tuple-element.92), channel_id=1, source_target_pairs={{2,0},{24,16},{34,32},{56,48},{66,64},{88,80},{98,96},{120,112},{1... | collective-permute-start | bytes 786440 | tf_op jit(solution)/shard_map/ppermute | solution.py:33
  11.4 2.8 %collective-permute-done.2 = bf16[2,2,32,1024]{3,2,1,0:T(8,128)(2,1)S(1)} collective-permute-done((bf16[2,2,32,1024]{3,2,1,0:T(8,128)(2,1)S(1)}, bf16[2,2,32,1024]{3,2,1,0:T(8,128)(2,1)S(1)}, u32[]{:S(2)}, u32[]{:S(2)}) %collective-permute-start.2) | collective-permute-done | bytes 262176 | tf_op jit(solution)/shard_map/ppermute | solution.py:33
  16.3 2.8 %collective-permute-start.4 = (bf16[4,2,2,32,1024]{4,3,2,1,0:T(8,128)(2,1)S(1)}, bf16[4,2,2,32,1024]{4,3,2,1,0:T(8,128)(2,1)S(1)}, u32[]{:S(2)}, u32[]{:S(2)}) collective-permute-start(bf16[4,2,2,32,1024]{4,3,2,1,0:T(8,128)(2,1)S(1)} %pad_maximum_fusion.refs_0_), channel_id=1, source_target_pairs={{8,0},{18,16},{40,32},{50,48},{72,64},{82,80},{104,96},{114,112},{... | collective-permute-start | bytes 3145736 | tf_op jit(solution)/shard_map/ppermute | solution.py:33
  19.1 11.7 %collective-permute-done.4.refs_1_ = bf16[4,2,2,32,1024]{4,3,2,1,0:T(8,128)(2,1)S(1)} collective-permute-done((bf16[4,2,2,32,1024]{4,3,2,1,0:T(8,128)(2,1)S(1)}, bf16[4,2,2,32,1024]{4,3,2,1,0:T(8,128)(2,1)S(1)}, u32[]{:S(2)}, u32[]{:S(2)}) %collective-permute-start.4) | collective-permute-done | bytes 1048608 | tf_op jit(solution)/shard_map/ppermute | solution.py:33
  31.8 3.4 %collective-permute-start.11 = (bf16[2,2,2,32,1024]{4,3,2,1,0:T(8,128)(2,1)}, bf16[2,2,2,32,1024]{4,3,2,1,0:T(8,128)(2,1)}, u32[]{:S(2)}, u32[]{:S(2)}) collective-permute-start(bf16[2,2,2,32,1024]{4,3,2,1,0:T(8,128)(2,1)} %slice.44), channel_id=1, source_target_pairs={{8,0},{18,16},{40,32},{50,48},{72,64},{82,80},{104,96},{114,112},{... | collective-permute-start | bytes 1572872 | tf_op jit(solution)/shard_map/ppermute | solution.py:33
  36.4 9.1 %forward.2 = (bf16[2,384,1024]{2,1,0:T(8,128)(2,1)}, bf16[2,384,1024]{2,1,0:T(8,128)(2,1)}, bf16[3,96,896]{2,1,0:T(8,128)(2,1)S(1)}, bf16[3,96,896]{2,1,0:T(8,12...) custom-call(s32[1]{0:T(128)} %bitcast.where, ...), custom_call_target="tpu_custom_call" | custom-call | flops 4227858432 | bytes 17301504 | tf_op jit(solution)/shard_map/forward/pallas_call | solution.py:132
  47.2 2.2 %collective-permute-start.10 = (bf16[3,48,896]{2,1,0:T(8,128)(2,1)S(1)}, bf16[3,48,896]{2,1,0:T(8,128)(2,1)S(1)}, u32[]{:S(2)}, u32[]{:S(2)}) collective-permute-start(bf16[3,48,896]{2,1,0:T(8,128)(2,1)S(1)} %get-tuple-element.52), channel_id=1, source_target_pairs={{32,0},{48,16},{64,32},{80,48},{96,64},{112,80},{0,96},{16,112},{4... | collective-permute-start | bytes 774152 | tf_op jit(solution)/shard_map/ppermute | solution.py:33
  49.5 6.7 %forward.3 = (bf16[2,128,1024]{2,1,0:T(8,128)(2,1)}, bf16[2,128,1024]{2,1,0:T(8,128)(2,1)}, bf16[4,3,32,896]{3,2,1,0:T(8,128)(2,1)}) custom-call(s32[1]{0:T(128)} %bitcast.where, bf16[2,2,2,32,1024]{4,3,2,1,0:T(8,128)(2,1)} %collective-permute-done.11.refs_0_, bf16[2,2,2,32,1024]{4,3,2,1,0:T(8,128)(2,1)} %collective-permute-done.12.refs_1_, ...), custom_call_target="tpu_custom_call" | custom-call | flops 1409286144 | bytes 13107200 | tf_op jit(solution)/shard_map/forward/pallas_call | solution.py:132
  56.2 3.5 %all-to-all-start = ((bf16[4,3,32,896]{3,2,1,0:T(8,128)(2,1)}), bf16[4,3,32,896]{3,2,1,0:T(8,128)(2,1)S(1)}, u32[]{:S(2)}, u32[]{:S(2)}) async-start(bf16[4,3,32,896]{3,2,1,0:T(8,128)(2,1)} %get-tuple-element.53), calls=%async_computation | async-start | bytes 1376256 | tf_op jit(solution)/shard_map/all_to_all | solution.py:390
  63.4 5.7 %all-to-all-done.refs_0_ = bf16[4,3,32,896]{3,2,1,0:T(8,128)(2,1)S(1)} async-done(((bf16[4,3,32,896]{3,2,1,0:T(8,128)(2,1)}), bf16[4,3,32,896]{3,2,1,0:T(8,128)(2,1)S(1)}, u32[]{:S(2)}, u32[]{:S(2)}) %all-to-all-start) | async-done | bytes 688160 | tf_op jit(solution)/shard_map/all_to_all | solution.py:390
  70.2 3.6 %all-to-all-start.1 = ((bf16[4,3,32,896]{3,2,1,0:T(8,128)(2,1)}), bf16[4,3,32,896]{3,2,1,0:T(8,128)(2,1)S(1)}, u32[]{:S(2)}, u32[]{:S(2)}) async-start(bf16[4,3,32,896]{3,2,1,0:T(8,128)(2,1)} %activate.2), calls=%async_computation.1 | async-start | bytes 1376256 | tf_op jit(solution)/shard_map/all_to_all | solution.py:390
  73.8 6.4 %collective-permute-done.13.refs_1_ = bf16[3,96,896]{2,1,0:T(8,128)(2,1)S(1)} collective-permute-done((bf16[3,96,896]{2,1,0:T(8,128)(2,1)}, bf16[3,96,896]{2,1,0:T(8,128)(2,1)S(1)}, u32[]{:S(2)}, u32[]{:S(2)}) %collective-permute-start.13) | collective-permute-done | bytes 516128 | tf_op jit(solution)/shard_map/ppermute | solution.py:33
  85.0 2.6 %all-to-all-done.1.parts = bf16[4,3,32,896]{3,2,1,0:T(8,128)(2,1)S(1)} async-done(((bf16[4,3,32,896]{3,2,1,0:T(8,128)(2,1)}), bf16[4,3,32,896]{3,2,1,0:T(8,128)(2,1)S(1)}, u32[]{:S(2)}, u32[]{:S(2)}) %all-to-all-start.1) | async-done | bytes 688160 | tf_op jit(solution)/shard_map/all_to_all | solution.py:390
  89.1 3.8 %backward.1 = (bf16[3,128,896]{2,1,0:T(8,128)(2,1)S(1)}, bf16[2,2,32,1024]{3,2,1,0:T(8,128)(2,1)S(1)}, bf16[2,2,32,1024]{3,2,1,0:T(8,128)(2,1)S(1)}) custom-call(bf16[4,3,32,896]{3,2,1,0:T(8,128)(2,1)S(1)} %all-to-all-done.1.parts, bf16[1024,896]{1,0:T(8,128)(2,1)S(1)} %copy-done.1, bf16[1024,896]{1,0:T(8,128)(2,1)S(1)} %copy-done.2, ...), custom_call_target="tpu_custom_call" | custom-call | flops 939524096 | bytes 8552448 | tf_op jit(solution)/shard_map/backward/pallas_call | solution.py:262
  92.9 2.7 %collective-permute-start.20 = (bf16[2,2,32,1024]{3,2,1,0:T(8,128)(2,1)S(1)}, bf16[2,2,32,1024]{3,2,1,0:T(8,128)(2,1)S(1)}, u32[]{:S(2)}, u32[]{:S(2)}) collective-permute-start(bf16[2,2,32,1024]{3,2,1,0:T(8,128)(2,1)S(1)} %get-tuple-element.61), channel_id=1, source_target_pairs={{8,0},{18,16},{40,32},{50,48},{72,64},{82,80},{104,96},{114,112},{... | collective-permute-start | bytes 786440 | tf_op jit(solution)/shard_map/ppermute | solution.py:33
  101.8 4.2 %collective-permute-start.23 = (bf16[2,384,1024]{2,1,0:T(8,128)(2,1)S(1)}, bf16[2,384,1024]{2,1,0:T(8,128)(2,1)S(1)}, u32[]{:S(2)}, u32[]{:S(2)}) collective-permute-start(bf16[2,384,1024]{2,1,0:T(8,128)(2,1)S(1)} %copy-done.11), channel_id=1, source_target_pairs={{16,0},{0,16},{48,32},{32,48},{80,64},{64,80},{112,96},{96,112},{2... | collective-permute-start | bytes 4718600 | tf_op jit(solution)/shard_map/ppermute | solution.py:33
  105.9 4.8 %backward_early.1 = (bf16[3,288,896]{2,1,0:T(8,128)(2,1)S(1)}, bf16[2,288,1024]{2,1,0:T(8,128)(2,1)S(1)}) custom-call(bf16[3,96,896]{2,1,0:T(8,128)(2,1)S(1)} %activate.3.own, bf16[3,96,896]{2,1,0:T(8,128)(2,1)S(1)} %collective-permute-done.15.up, bf16[3,96,896]{2,1,0:T(8,128)(2,1)} %collective-permute-done.16.down, bf16[1024,896]{1,0:T(8,128)(2,1)S(1)} %copy-done.1, ...), custom_call_target="tpu_custom_call" | custom-call | flops 2113929216 | bytes 10067968 | tf_op jit(solution)/shard_map/backward_early/pallas_call | solution.py:262
  111.5 3.7 %backward_late.1 = (bf16[3,96,896]{2,1,0:T(8,128)(2,1)S(1)}, bf16[4,2,32,1024]{3,2,1,0:T(8,128)(2,1)S(1)}, bf16[4,2,32,1024]{3,2,1,0:T(8,128)(2,1)S(1)}, bf16[4,2,32,1024]{3,2,1,0:T(8,128)(2,1)S(1)}) custom-call(s32[1]{0:T(128)} %bitcast.where, bf16[3,48,896]{2,1,0:T(8,128)(2,1)S(1)} %collective-permute-done.17.f0, ...), custom_call_target="tpu_custom_call" | custom-call | flops 704643072 | bytes 8249344 | tf_op jit(solution)/shard_map/backward_late/pallas_call | solution.py:262
  115.7 2.8 %collective-permute-start.22 = (bf16[4,2,32,1024]{3,2,1,0:T(8,128)(2,1)S(1)}, bf16[4,2,32,1024]{3,2,1,0:T(8,128)(2,1)S(1)}, u32[]{:S(2)}, u32[]{:S(2)}) collective-permute-start(bf16[4,2,32,1024]{3,2,1,0:T(8,128)(2,1)S(1)} %get-tuple-element.69), channel_id=1, source_target_pairs={{8,0},{18,16},{40,32},{50,48},{72,64},{82,80},{104,96},{114,112},{... | collective-permute-start | bytes 1572872 | tf_op jit(solution)/shard_map/ppermute | solution.py:33
  118.6 5.7 %weights.1 = (bf16[1024,896]{1,0:T(8,128)(2,1)}, bf16[1024,896]{1,0:T(8,128)(2,1)}) custom-call(bf16[2,384,1024]{2,1,0:T(8,128)(2,1)S(1)} %copy-done.4, bf16[2,128,1024]{2,1,0:T(8,128)(2,1)S(1)} %copy-done.5, bf16[2,384,1024]{2,1,0:T(8,128)(2,1)S(1)} %collective-permute-done.23.refs_2_, bf16[2,128,1024]{2,1,0:T(8,128)(2,1)S(1)} %collective-permute-done.24.refs_3_, ...), custom_call_target="tpu_custom_call" | custom-call | flops 3758096384 | bytes 9437184 | tf_op jit(solution)/shard_map/weights/pallas_call | solution.py:325
  125.6 2.5 %collective-permute-start.28 = (bf16[2,32,1024]{2,1,0:T(8,128)(2,1)S(1)}, bf16[2,32,1024]{2,1,0:T(8,128)(2,1)S(1)}, u32[]{:S(2)}, u32[]{:S(2)}) collective-permute-start(bf16[2,32,1024]{2,1,0:T(8,128)(2,1)S(1)} %get-tuple-element.90), channel_id=1, source_target_pairs={{4,0},{17,16},{36,32},{49,48},{68,64},{81,80},{100,96},{113,112},{... | collective-permute-start | bytes 393224 | tf_op jit(solution)/shard_map/ppermute | solution.py:33
  129.5 4.3 %down_weights.1 = bf16[896,1024]{1,0:T(8,128)(2,1)} custom-call(bf16[2,384,1024]{2,1,0:T(8,128)(2,1)S(1)} %copy-done.4, bf16[2,128,1024]{2,1,0:T(8,128)(2,1)S(1)} %copy-done.5, bf16[2,384,1024]{2,1,0:T(8,128)(2,1)S(1)} %collective-permute-done.23.refs_2_, bf16[2,128,1024]{2,1,0:T(8,128)(2,1)S(1)} %collective-permute-done.24.refs_3_, ...), custom_call_target="tpu_custom_call" | custom-call | flops 1879048192 | bytes 5767168 | tf_op jit(solution)/shard_map/down_weights/pallas_call | solution.py:364
  133.9 2.2 %collective-permute-start.31 = (bf16[32,1024]{1,0:T(8,128)(2,1)S(1)}, bf16[32,1024]{1,0:T(8,128)(2,1)S(1)}, u32[]{:S(2)}, u32[]{:S(2)}) collective-permute-start(bf16[32,1024]{1,0:T(8,128)(2,1)S(1)} %slice_bitcast_fusion.4), channel_id=1, source_target_pairs={{16,0},{0,16},{48,32},{32,48},{80,64},{64,80},{112,96},{96,112},{2... | collective-permute-start | bytes 196616 | tf_op jit(solution)/shard_map/ppermute | solution.py:33
  (93 shorter events, 34.3 us)
Async XLA Ops:
  14.8 21.6 %collective-permute-start.6 = (bf16[1024,896]{1,0:T(8,128)(2,1)S(1)}, bf16[1024,896]{1,0:T(8,128)(2,1)}, u32[]{:S(2)}, u32[]{:S(2)}) collective-permute-start(bf16[1024,896]{1,0:T(8,128)(2,1)S(1)} %copy-done), channel_id=1, source_target_pairs={{16,0},{0,16},{48,32},{32,48},{80,64},{64,80},{112,96},{96,112},{2... | collective-permute-start | bytes 5505032 | tf_op jit(solution)/shard_map/ppermute | solution.py:33
  15.8 20.6 %collective-permute-start.7 = (bf16[1024,896]{1,0:T(8,128)(2,1)}, bf16[1024,896]{1,0:T(8,128)(2,1)}, u32[]{:S(2)}, u32[]{:S(2)}) collective-permute-start(bf16[1024,896]{1,0:T(8,128)(2,1)} %refs_1_.5), channel_id=1, source_target_pairs={{16,0},{0,16},{48,32},{32,48},{80,64},{64,80},{112,96},{96,112},{2... | collective-permute-start | bytes 5505032 | tf_op jit(solution)/shard_map/ppermute | solution.py:33
  15.9 20.5 %collective-permute-start.8 = (bf16[896,1024]{1,0:T(8,128)(2,1)}, bf16[896,1024]{1,0:T(8,128)(2,1)}, u32[]{:S(2)}, u32[]{:S(2)}) collective-permute-start(bf16[896,1024]{1,0:T(8,128)(2,1)} %refs_4_.3), channel_id=1, source_target_pairs={{16,0},{0,16},{48,32},{32,48},{80,64},{64,80},{112,96},{96,112},{2... | collective-permute-start | bytes 5505032 | tf_op jit(solution)/shard_map/ppermute | solution.py:33
  16.3 14.5 %collective-permute-start.4 = (bf16[4,2,2,32,1024]{4,3,2,1,0:T(8,128)(2,1)S(1)}, bf16[4,2,2,32,1024]{4,3,2,1,0:T(8,128)(2,1)S(1)}, u32[]{:S(2)}, u32[]{:S(2)}) collective-permute-start(bf16[4,2,2,32,1024]{4,3,2,1,0:T(8,128)(2,1)S(1)} %pad_maximum_fusion.refs_0_), channel_id=1, source_target_pairs={{8,0},{18,16},{40,32},{50,48},{72,64},{82,80},{104,96},{114,112},{... | collective-permute-start | bytes 3145736 | tf_op jit(solution)/shard_map/ppermute | solution.py:33
  19.1 16.1 %collective-permute-start.5 = (bf16[4,2,2,32,1024]{4,3,2,1,0:T(8,128)(2,1)S(1)}, bf16[4,2,2,32,1024]{4,3,2,1,0:T(8,128)(2,1)S(1)}, u32[]{:S(2)}, u32[]{:S(2)}) collective-permute-start(bf16[4,2,2,32,1024]{4,3,2,1,0:T(8,128)(2,1)S(1)} %pad_maximum_fusion.refs_0_), channel_id=1, source_target_pairs={{9,0},{22,16},{41,32},{54,48},{73,64},{86,80},{105,96},{118,112},{... | collective-permute-start | bytes 3145736 | tf_op jit(solution)/shard_map/ppermute | solution.py:33
  31.8 17.6 %collective-permute-start.11 = (bf16[2,2,2,32,1024]{4,3,2,1,0:T(8,128)(2,1)}, bf16[2,2,2,32,1024]{4,3,2,1,0:T(8,128)(2,1)}, u32[]{:S(2)}, u32[]{:S(2)}) collective-permute-start(bf16[2,2,2,32,1024]{4,3,2,1,0:T(8,128)(2,1)} %slice.44), channel_id=1, source_target_pairs={{8,0},{18,16},{40,32},{50,48},{72,64},{82,80},{104,96},{114,112},{... | collective-permute-start | bytes 1572872 | tf_op jit(solution)/shard_map/ppermute | solution.py:33
  36.4 13.0 %collective-permute-start.12 = (bf16[2,2,2,32,1024]{4,3,2,1,0:T(8,128)(2,1)}, bf16[2,2,2,32,1024]{4,3,2,1,0:T(8,128)(2,1)}, u32[]{:S(2)}, u32[]{:S(2)}) collective-permute-start(bf16[2,2,2,32,1024]{4,3,2,1,0:T(8,128)(2,1)} %slice.45), channel_id=1, source_target_pairs={{9,0},{22,16},{41,32},{54,48},{73,64},{86,80},{105,96},{118,112},{... | collective-permute-start | bytes 1572872 | tf_op jit(solution)/shard_map/ppermute | solution.py:33
  45.5 14.1 %collective-permute-start.9 = (bf16[3,48,896]{2,1,0:T(8,128)(2,1)S(1)}, bf16[3,48,896]{2,1,0:T(8,128)(2,1)S(1)}, u32[]{:S(2)}, u32[]{:S(2)}) collective-permute-start(bf16[3,48,896]{2,1,0:T(8,128)(2,1)S(1)} %get-tuple-element.51), channel_id=1, source_target_pairs={{96,0},{112,16},{0,32},{16,48},{32,64},{48,80},{64,96},{80,112},{1... | collective-permute-start | bytes 774152 | tf_op jit(solution)/shard_map/ppermute | solution.py:33
  47.2 12.4 %collective-permute-start.10 = (bf16[3,48,896]{2,1,0:T(8,128)(2,1)S(1)}, bf16[3,48,896]{2,1,0:T(8,128)(2,1)S(1)}, u32[]{:S(2)}, u32[]{:S(2)}) collective-permute-start(bf16[3,48,896]{2,1,0:T(8,128)(2,1)S(1)} %get-tuple-element.52), channel_id=1, source_target_pairs={{32,0},{48,16},{64,32},{80,48},{96,64},{112,80},{0,96},{16,112},{4... | collective-permute-start | bytes 774152 | tf_op jit(solution)/shard_map/ppermute | solution.py:33
  56.2 13.0 %all-to-all-start = ((bf16[4,3,32,896]{3,2,1,0:T(8,128)(2,1)}), bf16[4,3,32,896]{3,2,1,0:T(8,128)(2,1)S(1)}, u32[]{:S(2)}, u32[]{:S(2)}) async-start(bf16[4,3,32,896]{3,2,1,0:T(8,128)(2,1)} %get-tuple-element.53), calls=%async_computation | async-start | bytes 1376256 | tf_op jit(solution)/shard_map/all_to_all | solution.py:390
  60.8 19.5 %collective-permute-start.13 = (bf16[3,96,896]{2,1,0:T(8,128)(2,1)}, bf16[3,96,896]{2,1,0:T(8,128)(2,1)S(1)}, u32[]{:S(2)}, u32[]{:S(2)}) collective-permute-start(bf16[3,96,896]{2,1,0:T(8,128)(2,1)} %get-tuple-element.56), channel_id=1, source_target_pairs={{96,0},{112,16},{0,32},{16,48},{32,64},{48,80},{64,96},{80,112},{1... | collective-permute-start | bytes 1548296 | tf_op jit(solution)/shard_map/ppermute | solution.py:33
  62.2 18.9 %collective-permute-start.14 = (bf16[3,96,896]{2,1,0:T(8,128)(2,1)}, bf16[3,96,896]{2,1,0:T(8,128)(2,1)}, u32[]{:S(2)}, u32[]{:S(2)}) collective-permute-start(bf16[3,96,896]{2,1,0:T(8,128)(2,1)} %get-tuple-element.57), channel_id=1, source_target_pairs={{32,0},{48,16},{64,32},{80,48},{96,64},{112,80},{0,96},{16,112},{4... | collective-permute-start | bytes 1548296 | tf_op jit(solution)/shard_map/ppermute | solution.py:33
  70.2 17.4 %all-to-all-start.1 = ((bf16[4,3,32,896]{3,2,1,0:T(8,128)(2,1)}), bf16[4,3,32,896]{3,2,1,0:T(8,128)(2,1)S(1)}, u32[]{:S(2)}, u32[]{:S(2)}) async-start(bf16[4,3,32,896]{3,2,1,0:T(8,128)(2,1)} %activate.2), calls=%async_computation.1 | async-start | bytes 1376256 | tf_op jit(solution)/shard_map/all_to_all | solution.py:390
  83.5 13.4 %collective-permute-start.15 = (bf16[3,96,896]{2,1,0:T(8,128)(2,1)S(1)}, bf16[3,96,896]{2,1,0:T(8,128)(2,1)S(1)}, u32[]{:S(2)}, u32[]{:S(2)}) collective-permute-start(bf16[3,96,896]{2,1,0:T(8,128)(2,1)S(1)} %activate.3.own), channel_id=1, source_target_pairs={{32,0},{48,16},{64,32},{80,48},{96,64},{112,80},{0,96},{16,112},{4... | collective-permute-start | bytes 1548296 | tf_op jit(solution)/shard_map/ppermute | solution.py:33
  84.2 13.7 %collective-permute-start.16 = (bf16[3,96,896]{2,1,0:T(8,128)(2,1)S(1)}, bf16[3,96,896]{2,1,0:T(8,128)(2,1)}, u32[]{:S(2)}, u32[]{:S(2)}) collective-permute-start(bf16[3,96,896]{2,1,0:T(8,128)(2,1)S(1)} %activate.3.own), channel_id=1, source_target_pairs={{96,0},{112,16},{0,32},{16,48},{32,64},{48,80},{64,96},{80,112},{1... | collective-permute-start | bytes 1548296 | tf_op jit(solution)/shard_map/ppermute | solution.py:33
  92.9 17.9 %collective-permute-start.19 = (bf16[2,2,32,1024]{3,2,1,0:T(8,128)(2,1)S(1)}, bf16[2,2,32,1024]{3,2,1,0:T(8,128)(2,1)S(1)}, u32[]{:S(2)}, u32[]{:S(2)}) collective-permute-start(bf16[2,2,32,1024]{3,2,1,0:T(8,128)(2,1)S(1)} %get-tuple-element.60), channel_id=1, source_target_pairs={{9,0},{22,16},{41,32},{54,48},{73,64},{86,80},{105,96},{118,112},{... | collective-permute-start | bytes 786440 | tf_op jit(solution)/shard_map/ppermute | solution.py:33
  92.9 17.8 %collective-permute-start.20 = (bf16[2,2,32,1024]{3,2,1,0:T(8,128)(2,1)S(1)}, bf16[2,2,32,1024]{3,2,1,0:T(8,128)(2,1)S(1)}, u32[]{:S(2)}, u32[]{:S(2)}) collective-permute-start(bf16[2,2,32,1024]{3,2,1,0:T(8,128)(2,1)S(1)} %get-tuple-element.61), channel_id=1, source_target_pairs={{8,0},{18,16},{40,32},{50,48},{72,64},{82,80},{104,96},{114,112},{... | collective-permute-start | bytes 786440 | tf_op jit(solution)/shard_map/ppermute | solution.py:33
  98.9 11.8 %collective-permute-start.17 = (bf16[3,48,896]{2,1,0:T(8,128)(2,1)S(1)}, bf16[3,48,896]{2,1,0:T(8,128)(2,1)S(1)}, u32[]{:S(2)}, u32[]{:S(2)}) collective-permute-start(bf16[3,48,896]{2,1,0:T(8,128)(2,1)S(1)} %slice.36), channel_id=1, source_target_pairs={{96,0},{112,16},{0,32},{16,48},{32,64},{48,80},{64,96},{80,112},{1... | collective-permute-start | bytes 774152 | tf_op jit(solution)/shard_map/ppermute | solution.py:33
  100.5 10.3 %collective-permute-start.18 = (bf16[3,48,896]{2,1,0:T(8,128)(2,1)S(1)}, bf16[3,48,896]{2,1,0:T(8,128)(2,1)S(1)}, u32[]{:S(2)}, u32[]{:S(2)}) collective-permute-start(bf16[3,48,896]{2,1,0:T(8,128)(2,1)S(1)} %slice.37), channel_id=1, source_target_pairs={{32,0},{48,16},{64,32},{80,48},{96,64},{112,80},{0,96},{16,112},{4... | collective-permute-start | bytes 774152 | tf_op jit(solution)/shard_map/ppermute | solution.py:33
  101.8 13.9 %collective-permute-start.23 = (bf16[2,384,1024]{2,1,0:T(8,128)(2,1)S(1)}, bf16[2,384,1024]{2,1,0:T(8,128)(2,1)S(1)}, u32[]{:S(2)}, u32[]{:S(2)}) collective-permute-start(bf16[2,384,1024]{2,1,0:T(8,128)(2,1)S(1)} %copy-done.11), channel_id=1, source_target_pairs={{16,0},{0,16},{48,32},{32,48},{80,64},{64,80},{112,96},{96,112},{2... | collective-permute-start | bytes 4718600 | tf_op jit(solution)/shard_map/ppermute | solution.py:33
  110.8 7.8 %collective-permute-start.25 = (bf16[3,288,896]{2,1,0:T(8,128)(2,1)S(1)}, bf16[3,288,896]{2,1,0:T(8,128)(2,1)S(1)}, u32[]{:S(2)}, u32[]{:S(2)}) collective-permute-start(bf16[3,288,896]{2,1,0:T(8,128)(2,1)S(1)} %get-tuple-element.77.refs_4_), channel_id=1, source_target_pairs={{16,0},{0,16},{48,32},{32,48},{80,64},{64,80},{112,96},{96,112},{2... | collective-permute-start | bytes 4644872 | tf_op jit(solution)/shard_map/ppermute | solution.py:33
  115.7 9.5 %collective-permute-start.21 = (bf16[4,2,32,1024]{3,2,1,0:T(8,128)(2,1)S(1)}, bf16[4,2,32,1024]{3,2,1,0:T(8,128)(2,1)S(1)}, u32[]{:S(2)}, u32[]{:S(2)}) collective-permute-start(bf16[4,2,32,1024]{3,2,1,0:T(8,128)(2,1)S(1)} %get-tuple-element.68), channel_id=1, source_target_pairs={{9,0},{22,16},{41,32},{54,48},{73,64},{86,80},{105,96},{118,112},{... | collective-permute-start | bytes 1572872 | tf_op jit(solution)/shard_map/ppermute | solution.py:33
  115.7 9.5 %collective-permute-start.22 = (bf16[4,2,32,1024]{3,2,1,0:T(8,128)(2,1)S(1)}, bf16[4,2,32,1024]{3,2,1,0:T(8,128)(2,1)S(1)}, u32[]{:S(2)}, u32[]{:S(2)}) collective-permute-start(bf16[4,2,32,1024]{3,2,1,0:T(8,128)(2,1)S(1)} %get-tuple-element.69), channel_id=1, source_target_pairs={{8,0},{18,16},{40,32},{50,48},{72,64},{82,80},{104,96},{114,112},{... | collective-permute-start | bytes 1572872 | tf_op jit(solution)/shard_map/ppermute | solution.py:33
  125.6 8.2 %collective-permute-start.28 = (bf16[2,32,1024]{2,1,0:T(8,128)(2,1)S(1)}, bf16[2,32,1024]{2,1,0:T(8,128)(2,1)S(1)}, u32[]{:S(2)}, u32[]{:S(2)}) collective-permute-start(bf16[2,32,1024]{2,1,0:T(8,128)(2,1)S(1)} %get-tuple-element.90), channel_id=1, source_target_pairs={{4,0},{17,16},{36,32},{49,48},{68,64},{81,80},{100,96},{113,112},{... | collective-permute-start | bytes 393224 | tf_op jit(solution)/shard_map/ppermute | solution.py:33
  (23 other events, 143.9 us)
